TPU v7x, 32 devices: a whole 2x2x4 slice. The times are simulated.
32 devices in a mesh: fsdp: 16 (over z, y, x), tp: 2 (over core).
Axes of the slice: x: 2, y: 2, z: 4, core: 2. Of those that a mesh axis runs over, the one named last changes fastest.
Arguments:
- hidden: bfloat16 [16384, 1408], P(('fsdp', 'tp')), may hold values from -6 to 6
- skip_rows: bfloat16 [16384, 1408], P(('fsdp', 'tp')), may hold values from -6 to 6
- timestep: bfloat16 [16, 1408], P('fsdp'), may hold values from -6 to 6
- text: bfloat16 [5328, 1024], P('fsdp'), may hold values from -6 to 6
- grid_pos: int32 [16384, 2], P('fsdp'), may hold values from 0 to 62, as said below
- cotangent: bfloat16 [16384, 1408], P(('fsdp', 'tp')), may hold values from -6 to 6
- skip_weight: float32 [2816, 1408], P(('fsdp', 'tp')), may hold values from -0.109375 to 0.109375
- shift_weight: float32 [1408, 1408], P(('fsdp', 'tp')), may hold values from -0.15625 to 0.15625
- qkv_weight: float32 [1408, 3, 1408], P('fsdp', None, 'tp'), may hold values from -0.15625 to 0.15625
- cross_query: float32 [1408, 1408], P('fsdp', 'tp'), may hold values from -0.15625 to 0.15625
- cross_kv: float32 [1024, 2, 1408], P('fsdp', None, 'tp'), may hold values from -0.1875 to 0.1875
- out_weight: float32 [2, 1408, 1408], P(None, 'tp', 'fsdp'), may hold values from -2 to 2
- up_weight: float32 [1408, 6144], P('fsdp', 'tp'), may hold values from -0.15625 to 0.15625
- down_weight: float32 [6144, 1408], P('tp', 'fsdp'), may hold values from -0.078125 to 0.078125
- column_bias: float32 [6, 2, 704], P(None, 'tp', 'fsdp'), may hold values from -2 to 2
- up_bias: float32 [2, 3072], P('tp', 'fsdp'), may hold values from -2 to 2
- skip_gain: float32 [2816], P(('fsdp', 'tp')), may hold values from 0.5 to 1.5
- skip_bias: float32 [2816], P(('fsdp', 'tp')), may hold values from -2 to 2
- norm_gains: float32 [3, 1408], P(None, ('fsdp', 'tp')), may hold values from 0.5 to 1.5
- row_biases: float32 [8, 1408], P(None, ('fsdp', 'tp')), may hold values from -2 to 2
- head_gains: float32 [4, 88], replicated, may hold values from 0.5 to 1.5
- head_biases: float32 [4, 88], replicated, may hold values from -2 to 2
Outputs:
- output: bfloat16 [16384, 1408], P(('fsdp', 'tp'))
- input_grad: float32 [16384, 1408], P(('fsdp', 'tp'))
- skip_grad: float32 [16384, 1408], P(('fsdp', 'tp'))
- text_grad: float32 [5328, 1024], P('fsdp', 'tp')
- skip_weight_grad: float32 [2816, 1408], P(('fsdp', 'tp'))
- shift_weight_grad: float32 [1408, 1408], P(('fsdp', 'tp'))
- qkv_weight_grad: float32 [1408, 3, 1408], P('fsdp', None, 'tp')
- cross_query_grad: float32 [1408, 1408], P('fsdp', 'tp')
- cross_kv_grad: float32 [1024, 2, 1408], P('fsdp', None, 'tp')
- out_weight_grad: float32 [2, 1408, 1408], P(None, 'tp', 'fsdp')
- up_weight_grad: float32 [1408, 6144], P('fsdp', 'tp')
- down_weight_grad: float32 [6144, 1408], P('tp', 'fsdp')
- column_bias_grad: float32 [6, 2, 704], P(None, 'tp', 'fsdp')
- up_bias_grad: float32 [2, 3072], P('tp', 'fsdp')
- skip_gain_grad: float32 [2816], P(('fsdp', 'tp'))
- skip_bias_grad: float32 [2816], P(('fsdp', 'tp'))
- norm_gains_grad: float32 [3, 1408], P(None, ('fsdp', 'tp'))
- row_biases_grad: float32 [8, 1408], P(None, ('fsdp', 'tp'))
- head_gains_grad: float32 [4, 88], replicated
- head_biases_grad: float32 [4, 88], replicated
Inputs may be any that keep to these rules, and one draw needn't show every extreme that they name: `grid_pos`: within each image the tokens lie in raster order on a rectangle of whole rows, 32 tokens wide, in either orientation; both coordinates are shifted by one offset of 0 to 31 for that image, and some image has offset 0 and some offset 31.
All inputs are finite; a program needn't handle non-finite values.
Results may differ from a plain program's by a relative error of at most 0.02.
Values may be sent and summed in bfloat16 or wider, within the bound.
No kernel may reach another device: no remote copies, remote signals or barrier semaphores. Data moves between devices by JAX's collectives and lax.ppermute only.
A program may use at most 384 MiB of HBM per device.

v0:
```python
import jax
import jax.numpy as jnp
from jax import lax
from jax.sharding import PartitionSpec as P

HEAD_DIM = 88
SEQ = 1024


EPS_NORM = 1e-06
PRECISE = lax.Precision.HIGHEST


def layer_norm(values, scales, offsets):
    center = values - jnp.mean(values, axis=-1, keepdims=True)
    spread = jnp.mean(center * center, axis=-1, keepdims=True)
    return center * lax.rsqrt(spread + EPS_NORM) * scales + offsets


def head_norm(values, scales, offsets):
    row_count = values.shape[0]
    shaped = values.reshape(row_count, -1, HEAD_DIM)
    return layer_norm(shaped, scales, offsets).reshape(row_count, -1)


def rotary_tables(positions):
    quarter = HEAD_DIM // 4
    freqs = 10000.0 ** (-jnp.arange(quarter).astype(jnp.float32) / quarter)
    coords = positions.astype(jnp.float32)
    angles = jnp.concatenate([coords[:, 0:1] * freqs, coords[:, 1:2] * freqs], axis=1)
    angles = jnp.repeat(angles, 2, axis=1)
    return (jnp.cos(angles), jnp.sin(angles))


def rotate(values, cosine, sine):
    row_count = values.shape[0]
    head_count = values.shape[1] // HEAD_DIM
    paired = values.reshape(row_count, -1, 2)
    turned = jnp.stack([-paired[:, :, 1], paired[:, :, 0]], axis=2).reshape(row_count, -1)
    return values * jnp.tile(cosine, (1, head_count)) + turned * jnp.tile(sine, (1, head_count))


def gelu_tanh(values):
    return jax.nn.gelu(values, approximate=True)


def first_norm(values, scales, offsets, shifts):
    return layer_norm(values, scales, offsets) + shifts


def plain_dot(first_operand, second_operand):
    return jnp.dot(first_operand, second_operand, preferred_element_type=jnp.float32)


def dot_first(first_operand, second_operand):
    return lax.dot_general(
        first_operand, second_operand, (((0,), (0,)), ((), ())), preferred_element_type=jnp.float32
    )


def dot_last(first_operand, second_operand):
    return lax.dot_general(
        first_operand, second_operand, (((1,), (1,)), ((), ())), preferred_element_type=jnp.float32
    )


def gather_rows(values):
    return lax.all_gather(values, "tp", axis=0, tiled=True)


def gather_grads(values):
    return lax.all_gather(values, "tp", axis=0, tiled=True)


def scatter_branch(operand, weight, rows_local):

    def term(start, count):
        return plain_dot(operand, weight)

    return lax.psum_scatter(
        term(jnp.int32(0), rows_local * lax.axis_size("tp")).astype(jnp.bfloat16),
        "tp",
        scatter_dimension=0,
        tiled=True,
    ).astype(jnp.float32)


def scatter_input_grad(operand, weight, rows_local):

    def term(start, count):
        return dot_last(operand, weight)

    return lax.psum_scatter(
        term(jnp.int32(0), rows_local * lax.axis_size("tp")).astype(jnp.bfloat16),
        "tp",
        scatter_dimension=0,
        tiled=True,
    ).astype(jnp.float32)


def split_heads(values, image_count):
    return values.reshape(image_count, values.shape[0] // image_count, -1, HEAD_DIM)


def attention_forward(queries, keys, values, image_count):
    query_heads = split_heads(queries, image_count)
    key_heads = split_heads(keys, image_count)
    value_heads = split_heads(values, image_count)
    query_len = query_heads.shape[1]
    block_rows = min(512, query_len)
    scaling = HEAD_DIM ** (-0.5)
    outputs = []
    totals = []
    for offset_row in range(0, query_len, block_rows):
        query_piece = query_heads[:, offset_row : offset_row + block_rows]
        scores = (
            jnp.einsum(
                "iqhd,ikhd->ihqk", query_piece, key_heads, preferred_element_type=jnp.float32
            )
            * scaling
        )
        row_peak = jnp.max(scores, axis=-1, keepdims=True)
        exponent = jnp.exp(scores - row_peak)
        summed = jnp.sum(exponent, axis=-1, keepdims=True)
        chances = exponent / summed
        outputs.append(
            jnp.einsum(
                "ihqk,ikhd->iqhd",
                chances.astype(jnp.bfloat16),
                value_heads,
                preferred_element_type=jnp.float32,
            )
        )
        totals.append(row_peak + jnp.log(summed))
    mixture = jnp.concatenate(outputs, axis=1).reshape(queries.shape[0], -1)
    return (mixture, totals)


def attention_backward(grad_mix, queries, keys, values, totals, image_count):
    query_heads = split_heads(queries, image_count)
    key_heads = split_heads(keys, image_count)
    value_heads = split_heads(values, image_count)
    grad_heads = split_heads(grad_mix, image_count)
    query_len = query_heads.shape[1]
    block_rows = min(512, query_len)
    scaling = HEAD_DIM ** (-0.5)
    grad_keys = jnp.zeros(key_heads.shape, jnp.float32)
    grad_values = jnp.zeros(value_heads.shape, jnp.float32)
    grad_queries = []
    for index_blk, offset_row in enumerate(range(0, query_len, block_rows)):
        query_piece = query_heads[:, offset_row : offset_row + block_rows]
        grad_piece = grad_heads[:, offset_row : offset_row + block_rows]
        scores = (
            jnp.einsum(
                "iqhd,ikhd->ihqk", query_piece, key_heads, preferred_element_type=jnp.float32
            )
            * scaling
        )
        chances = jnp.exp(scores - totals[index_blk])
        grad_values = grad_values + jnp.einsum(
            "ihqk,iqhd->ikhd",
            chances.astype(jnp.bfloat16),
            grad_piece,
            preferred_element_type=jnp.float32,
        )
        grad_chance = jnp.einsum(
            "iqhd,ikhd->ihqk", grad_piece, value_heads, preferred_element_type=jnp.float32
        )
        grad_score = chances * (
            grad_chance - jnp.sum(grad_chance * chances, axis=-1, keepdims=True)
        )
        grad_low = grad_score.astype(jnp.bfloat16)
        grad_queries.append(
            jnp.einsum("ihqk,ikhd->iqhd", grad_low, key_heads, preferred_element_type=jnp.float32)
            * scaling
        )
        grad_keys = (
            grad_keys
            + jnp.einsum(
                "ihqk,iqhd->ikhd", grad_low, query_piece, preferred_element_type=jnp.float32
            )
            * scaling
        )
    query_grad = jnp.concatenate(grad_queries, axis=1).reshape(queries.shape[0], -1)
    return (
        query_grad,
        grad_keys.reshape(keys.shape[0], -1),
        grad_values.reshape(values.shape[0], -1),
    )


def body(
    hidden,
    skip_rows,
    timestep,
    text,
    grid_pos,
    cotangent,
    skip_weight,
    shift_weight,
    qkv_weight,
    cross_query,
    cross_kv,
    out_weight,
    up_weight,
    down_weight,
    column_bias,
    up_bias,
    skip_gain,
    skip_bias,
    norm_gains,
    row_biases,
    head_gains,
    head_biases,
):
    bfloat = jnp.bfloat16
    qkv_w, query_w, pair_w, proj_w, col_b, up_w, down_w, up_b = (
        lax.all_gather(qkv_weight.astype(bfloat), "fsdp", axis=0, tiled=True),
        lax.all_gather(cross_query.astype(bfloat), "fsdp", axis=0, tiled=True),
        lax.all_gather(cross_kv.astype(bfloat), "fsdp", axis=0, tiled=True),
        lax.all_gather(out_weight.astype(bfloat), "fsdp", axis=2, tiled=True),
        lax.all_gather(column_bias.astype(bfloat), "fsdp", axis=2, tiled=True),
        lax.all_gather(up_weight.astype(bfloat), "fsdp", axis=0, tiled=True),
        lax.all_gather(down_weight.astype(bfloat), "fsdp", axis=1, tiled=True),
        lax.all_gather(up_bias.astype(bfloat), "fsdp", axis=1, tiled=True),
    )
    skip_w, shift_w, sgain, sbias, ngain, rbias = (
        lax.all_gather(skip_weight.astype(bfloat), ("fsdp", "tp"), axis=0, tiled=True),
        lax.all_gather(shift_weight.astype(bfloat), ("fsdp", "tp"), axis=0, tiled=True),
        lax.all_gather(skip_gain.astype(bfloat), ("fsdp", "tp"), axis=0, tiled=True),
        lax.all_gather(skip_bias.astype(bfloat), ("fsdp", "tp"), axis=0, tiled=True),
        lax.all_gather(norm_gains.astype(bfloat), ("fsdp", "tp"), axis=1, tiled=True),
        lax.all_gather(row_biases.astype(bfloat), ("fsdp", "tp"), axis=1, tiled=True),
    )
    sgain_f = sgain.astype(jnp.float32)
    sbias_f = sbias.astype(jnp.float32)
    ngain_f = ngain.astype(jnp.float32)
    rbias_f = rbias.astype(jnp.float32)
    col_bf = col_b.astype(jnp.float32)
    rows_local = hidden.shape[0]
    image_count = timestep.shape[0]
    model_width = hidden.shape[1]
    local_width = qkv_w.shape[2]
    joined = jnp.concatenate([hidden, skip_rows], axis=1).astype(jnp.float32)
    normed_f, skip_pull = jax.vjp(layer_norm, joined, sgain_f, sbias_f)
    normed_skip = normed_f.astype(bfloat)
    stream_zero = plain_dot(normed_skip, skip_w) + rbias_f[6]
    activated = jax.nn.silu(timestep.astype(jnp.float32)).astype(bfloat)
    shift_image = plain_dot(activated, shift_w) + rbias_f[7]
    image_ids = (lax.axis_index("tp") * rows_local + jnp.arange(rows_local, dtype=jnp.int32)) // SEQ
    selector = (image_ids[:, None] == jnp.arange(image_count, dtype=jnp.int32)[None, :]).astype(
        jnp.float32
    )
    shift_tokens = jnp.dot(selector, shift_image, precision=PRECISE)
    first_f, first_pull = jax.vjp(first_norm, stream_zero, ngain_f[0], rbias_f[0], shift_tokens)
    first_in = gather_rows(first_f.astype(bfloat))
    projected = plain_dot(first_in, qkv_w.reshape(model_width, -1)) + col_bf[0:3].reshape(-1)
    cosine, sine = rotary_tables(grid_pos)

    def rotary_prep(values, scales, offsets):
        return rotate(head_norm(values, scales, offsets), cosine, sine)

    queries_f, query_pull = jax.vjp(
        rotary_prep, projected[:, :local_width], head_gains[0], head_biases[0]
    )
    keys_f, key_pull = jax.vjp(
        rotary_prep, projected[:, local_width : 2 * local_width], head_gains[1], head_biases[1]
    )
    queries = queries_f.astype(bfloat)
    keys = keys_f.astype(bfloat)
    values = projected[:, 2 * local_width :].astype(bfloat)
    mixture_f, self_totals = attention_forward(queries, keys, values, image_count)
    mixture = mixture_f.astype(bfloat)
    stream_one = stream_zero + scatter_branch(mixture, proj_w[0], rows_local) + rbias_f[3]
    second_f, second_pull = jax.vjp(layer_norm, stream_one, ngain_f[1], rbias_f[1])
    second_in = gather_rows(second_f.astype(bfloat))
    cross_pre = plain_dot(second_in, query_w) + col_bf[3].reshape(-1)
    pair_pre = plain_dot(text, pair_w.reshape(pair_w.shape[0], -1)) + col_bf[4:6].reshape(-1)
    cross_q_f, cross_q_pull = jax.vjp(rotary_prep, cross_pre, head_gains[2], head_biases[2])
    cross_k_f, cross_k_pull = jax.vjp(
        head_norm, pair_pre[:, :local_width], head_gains[3], head_biases[3]
    )
    cross_queries = cross_q_f.astype(bfloat)
    cross_keys = cross_k_f.astype(bfloat)
    cross_values = pair_pre[:, local_width:].astype(bfloat)
    cross_mix_f, cross_totals = attention_forward(
        cross_queries, cross_keys, cross_values, image_count
    )
    cross_mixture = cross_mix_f.astype(bfloat)
    stream_two = stream_one + scatter_branch(cross_mixture, proj_w[1], rows_local) + rbias_f[4]
    third_f, third_pull = jax.vjp(layer_norm, stream_two, ngain_f[2], rbias_f[2])
    third_in = gather_rows(third_f.astype(bfloat))
    hidden_pre = plain_dot(third_in, up_w) + up_b.astype(jnp.float32).reshape(-1)
    gelu_f, gelu_pull = jax.vjp(gelu_tanh, hidden_pre)
    hidden_act = gelu_f.astype(bfloat)
    stream_three = stream_two + scatter_branch(hidden_act, down_w, rows_local) + rbias_f[5]
    output = stream_three.astype(bfloat)
    grad_three = cotangent.astype(jnp.float32)
    grad_ffn = gather_grads(cotangent)
    grad_act = dot_last(grad_ffn, down_w)
    grad_down = dot_first(hidden_act, grad_ffn)
    grad_pre = gelu_pull(grad_act)[0].astype(bfloat)
    grad_up = dot_first(third_in, grad_pre)
    grad_upb = jnp.sum(grad_pre, axis=0, dtype=jnp.float32).reshape(up_b.shape)
    grad_third = scatter_input_grad(grad_pre, up_w, rows_local)
    stream_grad, third_gain, third_bias = third_pull(grad_third)
    grad_two = grad_three + stream_grad
    grad_cross = gather_grads(grad_two.astype(bfloat))
    grad_cmix = dot_last(grad_cross, proj_w[1]).astype(bfloat)
    grad_cproj = dot_first(cross_mixture, grad_cross)
    cq_grad, ck_grad, cv_grad = attention_backward(
        grad_cmix, cross_queries, cross_keys, cross_values, cross_totals, image_count
    )
    cross_pre_grad, head_gain_two, head_bias_two = cross_q_pull(cq_grad)
    cross_key_grad, head_gain_three, head_bias_three = cross_k_pull(ck_grad)
    grad_cq = cross_pre_grad.astype(bfloat)
    grad_pair = jnp.concatenate([cross_key_grad, cv_grad], axis=1).astype(bfloat)
    grad_query_w = dot_first(second_in, grad_cq)
    grad_pair_w = dot_first(text, grad_pair).reshape(pair_w.shape)
    text_part = dot_last(grad_pair, pair_w.reshape(pair_w.shape[0], -1))
    text_grad = lax.psum_scatter(
        text_part.astype(jnp.bfloat16), "tp", scatter_dimension=1, tiled=True
    ).astype(jnp.float32)
    grad_second = scatter_input_grad(grad_cq, query_w, rows_local)
    stream_grad, second_gain, second_bias = second_pull(grad_second)
    grad_one = grad_two + stream_grad
    grad_self = gather_grads(grad_one.astype(bfloat))
    grad_mix = dot_last(grad_self, proj_w[0]).astype(bfloat)
    grad_sproj = dot_first(mixture, grad_self)
    query_grad, key_grad, value_grad = attention_backward(
        grad_mix, queries, keys, values, self_totals, image_count
    )
    query_pre_grad, head_gain_zero, head_bias_zero = query_pull(query_grad)
    key_pre_grad, head_gain_one, head_bias_one = key_pull(key_grad)
    grad_qkv = jnp.concatenate([query_pre_grad, key_pre_grad, value_grad], axis=1).astype(bfloat)
    grad_qkv_w = dot_first(first_in, grad_qkv).reshape(qkv_w.shape)
    grad_first = scatter_input_grad(grad_qkv, qkv_w.reshape(model_width, -1), rows_local)
    stream_grad, first_gain, first_bias, shift_grad = first_pull(grad_first)
    grad_zero = grad_one + stream_grad
    shift_image_grad = jnp.dot(selector.T, shift_grad, precision=PRECISE)
    grad_shift_w = jnp.dot(activated.astype(jnp.float32).T, shift_image_grad, precision=PRECISE)
    grad_low_zero = grad_zero.astype(bfloat)
    grad_normed = dot_last(grad_low_zero, skip_w)
    grad_skip_w = dot_first(normed_skip, grad_low_zero)
    joined_grad, skip_gain_part, skip_bias_part = skip_pull(grad_normed)
    input_grad = joined_grad[:, :model_width]
    skip_grad = joined_grad[:, model_width:]
    grad_colb = jnp.concatenate(
        [
            jnp.sum(grad_qkv, axis=0, dtype=jnp.float32).reshape(3, local_width),
            jnp.sum(grad_cq, axis=0, dtype=jnp.float32).reshape(1, local_width),
            jnp.sum(grad_pair, axis=0, dtype=jnp.float32).reshape(2, local_width),
        ],
        axis=0,
    ).reshape(col_b.shape)
    grad_proj = jnp.stack([grad_sproj, grad_cproj], axis=0)
    grad_gains = jnp.stack([first_gain, second_gain, third_gain], axis=0)
    grad_biases = jnp.stack(
        [
            first_bias,
            second_bias,
            third_bias,
            jnp.sum(grad_one, axis=0),
            jnp.sum(grad_two, axis=0),
            jnp.sum(grad_three, axis=0),
            jnp.sum(grad_zero, axis=0),
            jnp.sum(shift_grad, axis=0),
        ],
        axis=0,
    )
    sent_qkv, sent_query, sent_pair, sent_proj, sent_colb, sent_up, sent_down, sent_upb = (
        lax.psum_scatter(grad_qkv_w, "fsdp", scatter_dimension=0, tiled=True),
        lax.psum_scatter(grad_query_w, "fsdp", scatter_dimension=0, tiled=True),
        lax.psum_scatter(grad_pair_w, "fsdp", scatter_dimension=0, tiled=True),
        lax.psum_scatter(grad_proj, "fsdp", scatter_dimension=2, tiled=True),
        lax.psum_scatter(grad_colb, "fsdp", scatter_dimension=2, tiled=True),
        lax.psum_scatter(grad_up, "fsdp", scatter_dimension=0, tiled=True),
        lax.psum_scatter(grad_down, "fsdp", scatter_dimension=1, tiled=True),
        lax.psum_scatter(grad_upb, "fsdp", scatter_dimension=1, tiled=True),
    )
    sent_skip, sent_shift, sent_sgain, sent_sbias, sent_gains, sent_biases = (
        lax.psum_scatter(grad_skip_w, ("fsdp", "tp"), scatter_dimension=0, tiled=True),
        lax.psum_scatter(grad_shift_w, ("fsdp", "tp"), scatter_dimension=0, tiled=True),
        lax.psum_scatter(skip_gain_part, ("fsdp", "tp"), scatter_dimension=0, tiled=True),
        lax.psum_scatter(skip_bias_part, ("fsdp", "tp"), scatter_dimension=0, tiled=True),
        lax.psum_scatter(grad_gains, ("fsdp", "tp"), scatter_dimension=1, tiled=True),
        lax.psum_scatter(grad_biases, ("fsdp", "tp"), scatter_dimension=1, tiled=True),
    )
    head_gain_sum, head_bias_sum = lax.psum(
        (
            jnp.stack([head_gain_zero, head_gain_one, head_gain_two, head_gain_three], axis=0),
            jnp.stack([head_bias_zero, head_bias_one, head_bias_two, head_bias_three], axis=0),
        ),
        ("fsdp", "tp"),
    )
    return (
        output,
        input_grad,
        skip_grad,
        text_grad,
        sent_skip,
        sent_shift,
        sent_qkv,
        sent_query,
        sent_pair,
        sent_proj,
        sent_up,
        sent_down,
        sent_colb,
        sent_upb,
        sent_sgain,
        sent_sbias,
        sent_gains,
        sent_biases,
        head_gain_sum,
        head_bias_sum,
    )


def solution(mesh):
    in_specs = (
        P(("fsdp", "tp"), None),
        P(("fsdp", "tp"), None),
        P("fsdp", None),
        P("fsdp", None),
        P("fsdp", None),
        P(("fsdp", "tp"), None),
        P(("fsdp", "tp"), None),
        P(("fsdp", "tp"), None),
        P("fsdp", None, "tp"),
        P("fsdp", "tp"),
        P("fsdp", None, "tp"),
        P(None, "tp", "fsdp"),
        P("fsdp", "tp"),
        P("tp", "fsdp"),
        P(None, "tp", "fsdp"),
        P("tp", "fsdp"),
        P(("fsdp", "tp")),
        P(("fsdp", "tp")),
        P(None, ("fsdp", "tp")),
        P(None, ("fsdp", "tp")),
        P(),
        P(),
    )
    out_specs = (
        P(("fsdp", "tp"), None),
        P(("fsdp", "tp"), None),
        P(("fsdp", "tp"), None),
        P("fsdp", "tp"),
        P(("fsdp", "tp"), None),
        P(("fsdp", "tp"), None),
        P("fsdp", None, "tp"),
        P("fsdp", "tp"),
        P("fsdp", None, "tp"),
        P(None, "tp", "fsdp"),
        P("fsdp", "tp"),
        P("tp", "fsdp"),
        P(None, "tp", "fsdp"),
        P("tp", "fsdp"),
        P(("fsdp", "tp")),
        P(("fsdp", "tp")),
        P(None, ("fsdp", "tp")),
        P(None, ("fsdp", "tp")),
        P(),
        P(),
    )
    return jax.shard_map(body, mesh=mesh, in_specs=in_specs, out_specs=out_specs, check_vma=False)
```

profile of v0, /device:TPU:0, one launch (start us, length us, event | category | flops | bytes accessed | tf_op | source)
XLA Modules:
  0.0 3163.1 jit_solution(13147687266855801899)
XLA Ops:
  13.5 42.3 %all-reduce.21 = (bf16[2816]{0:T(1024)(128)(2,1)S(1)}, bf16[2816]{0:T(1024)(128)(2,1)S(1)}) all-reduce(bf16[2816]{0:T(1024)(128)(2,1)S(1)} %dynamic-update-slice.1, bf16[2816]{0:T(1024)(128)(2,1)S(1)} %dynamic-update-slice), channel_id=1, replica_groups=mesh['fsdp'=16,'tp'=2] {'fsdp','tp'}, use_global_device_ids=true, to_apply=%add.7 | all-reduce | flops 5632 | bytes 22528
  55.8 40.3 %all-gather.1 = bf16[32,44,3]{1,2,0:T(4,128)(2,1)S(1)} all-gather(bf16[1,44,3]{1,2,0:T(4,128)(2,1)S(1)} %convert_bitcast_fusion.2), channel_id=1, replica_groups=mesh['fsdp'=16,'tp'=2] {'fsdp','tp'}, dimensions={0}, use_global_device_ids=true | all-gather | bytes 8712 | tf_op jit(solution)/shard_map/all_gather | solution.py:232
  96.3 37.2 %all-gather = bf16[32,44,8]{1,2,0:T(8,128)(2,1)S(1)} all-gather(bf16[1,44,8]{1,2,0:T(8,128)(2,1)S(1)} %convert_bitcast_fusion.1), channel_id=1, replica_groups=mesh['fsdp'=16,'tp'=2] {'fsdp','tp'}, dimensions={0}, use_global_device_ids=true | all-gather | bytes 23232 | tf_op jit(solution)/shard_map/all_gather | solution.py:233
  175.2 42.0 %all_gather.68 = bf16[6,1,704]{0,1,2:T(2,128)(2,1)S(1)} all-gather(bf16[6,1,44]{0,1,2:T(2,128)(2,1)S(1)} %copy.190), channel_id=1, replica_groups=mesh['fsdp'=16,'tp'=2] {'fsdp'}, dimensions={2}, use_global_device_ids=true | all-gather | bytes 8976 | tf_op jit(solution)/shard_map/all_gather | solution.py:222
  218.1 39.0 %all-gather.22.cloned.1.call-done = bf16[1408,3,704]{2,0,1:T(8,128)(2,1)} async-done(((bf16[88,3,704]{2,0,1:T(8,128)(2,1)}), bf16[1408,3,704]{2,0,1:T(8,128)(2,1)}) %all-gather.22.cloned.1.call-update) | async-done | bytes 5947408 | tf_op jit(solution)/shard_map/all_gather | solution.py:218
  432.1 60.9 %all-gather.26.cloned.1.call-done = bf16[1024,2,704]{2,1,0:T(2,128)(2,1)} async-done(((bf16[64,2,704]{2,1,0:T(2,128)(2,1)}), bf16[1024,2,704]{2,1,0:T(2,128)(2,1)}) %all-gather.26.cloned.1.call-update) | async-done | bytes 2883600 | tf_op jit(solution)/shard_map/all_gather | solution.py:220
  517.8 38.8 %all-gather.30.cloned.1.call-done = bf16[1408,704]{1,0:T(8,128)(2,1)} async-done(((bf16[88,704]{1,0:T(8,128)(2,1)}), bf16[1408,704]{1,0:T(8,128)(2,1)}) %all-gather.30.cloned.1.call-update) | async-done | bytes 1982480 | tf_op jit(solution)/shard_map/all_gather | solution.py:219
  646.7 43.7 %all-reduce.8 = bf16[3072]{0:T(1024)(128)(2,1)S(1)} all-reduce(bf16[3072]{0:T(1024)(128)(2,1)S(1)} %dynamic-update-slice.2), channel_id=1, replica_groups=mesh['fsdp'=16,'tp'=2] {'fsdp'}, use_global_device_ids=true, to_apply=%add.8 | all-reduce | flops 3072 | bytes 12288
  690.4 67.7 %all-gather.34.cloned.1.call-done = bf16[1408,3072]{1,0:T(8,128)(2,1)} async-done(((bf16[88,3072]{1,0:T(8,128)(2,1)}), bf16[1408,3072]{1,0:T(8,128)(2,1)}) %all-gather.34.cloned.1.call-update) | async-done | bytes 8650768 | tf_op jit(solution)/shard_map/all_gather | solution.py:223
  770.1 16.4 fusion.196
  786.5 117.9 %all-gather.36.cloned.1.call-done = bf16[3072,1408]{0,1:T(8,128)(2,1)} async-done(((bf16[3072,88]{0,1:T(8,128)(2,1)}), bf16[3072,1408]{0,1:T(8,128)(2,1)}) %all-gather.36.cloned.1.call-update) | async-done | bytes 8650768 | tf_op jit(solution)/shard_map/all_gather | solution.py:224
  904.4 22.5 convert_reduce_fusion
  943.5 18.8 convolution_convert_fusion.1
  1266.1 27.3 fusion.173
  1449.0 16.8 fusion.176
  1465.9 15.6 fusion.198
  1529.9 77.1 %all-reduce.13 = f32[6,1,704]{2,1,0:T(1,128)S(1)} all-reduce(f32[6,1,704]{2,1,0:T(1,128)S(1)} %reshape.1062), channel_id=17, replica_groups=mesh['fsdp'=16,'tp'=2] {'fsdp'}, use_global_device_ids=true, to_apply=%region_65.66.clone | all-reduce | flops 4224 | bytes 33792
  1611.6 144.7 %fusion = f32[48,1408]{1,0:T(8,128)S(1)} fusion(f32[1408,1408]{1,0:T(8,128)} %broadcast_multiply_fusion), kind=kCustom, calls=%all-reduce-scatter | all-reduce-scatter fusion | flops 2162689 | bytes 8200192
  1788.2 285.2 %all-reduce.27.cloned.1.call-done = (f32[1024,2,704]{2,1,0:T(2,128)}, f32[2,704,1408]{1,0,2:T(2,128)}) async-done(((f32[1024,2,704]{2,1,0:T(2,128)}, f32[2,704,1408]{1,0,2:T(2,128)}), (f32[1024,2,704]{2,1,0:T(2,128)}, f32[2,704,1408]{1,0,2:T(2,128)})) %all-reduce.27.cloned.1.call-update) | async-done | bytes 13697040
  2077.0 137.7 %reduce-scatter.40.cloned.1.call-done = f32[88,704]{1,0:T(8,128)} async-done(((f32[1408,704]{1,0:T(8,128)}), f32[88,704]{1,0:T(8,128)}) %reduce-scatter.40.cloned.1.call-update) | async-done | bytes 247824 | tf_op jit(solution)/shard_map/reduce_scatter | solution.py:373
  2214.8 273.1 %reduce-scatter.44.cloned.1.call-done = f32[3072,88]{0,1:T(8,128)} async-done(((f32[3072,1408]{0,1:T(8,128)}), f32[3072,88]{0,1:T(8,128)}) %reduce-scatter.44.cloned.1.call-update) | async-done | bytes 1081360 | tf_op jit(solution)/shard_map/reduce_scatter | solution.py:378
  2487.9 273.5 %reduce-scatter.42.cloned.1.call-done = f32[88,3072]{1,0:T(8,128)} async-done(((f32[1408,3072]{1,0:T(8,128)}), f32[88,3072]{1,0:T(8,128)}) %reduce-scatter.42.cloned.1.call-update) | async-done | bytes 1081360 | tf_op jit(solution)/shard_map/reduce_scatter | solution.py:377
  2761.4 216.5 %reduce-scatter.38.cloned.1.call-done = f32[88,3,704]{2,0,1:T(8,128)} async-done(((f32[1408,3,704]{2,0,1:T(8,128)}), f32[88,3,704]{2,0,1:T(8,128)}) %reduce-scatter.38.cloned.1.call-update) | async-done | bytes 743440 | tf_op jit(solution)/shard_map/reduce_scatter | solution.py:372
  2977.9 177.4 %reduce-scatter.48.cloned.1.call-done = f32[88,1408]{1,0:T(8,128)} async-done(((f32[2816,1408]{1,0:T(8,128)}), f32[88,1408]{1,0:T(8,128)}) %reduce-scatter.48.cloned.1.call-update) | async-done | bytes 495632
  (924 shorter events, 910.4 us)
Async XLA Ops:
  7.3 130.5 %all-gather.44.cloned.1.call-start = ((), (), s32[]{:S(2)}) async-start(), calls=%async_computation.37 | async-start | bytes 4460544 | tf_op jit(solution)/shard_map/all_gather | solution.py:229
  9.1 145.7 %all-gather.18.cloned.1.call-start = ((), (), s32[]{:S(2)}) async-start(), calls=%async_computation.13 | async-start | bytes 8177664 | tf_op jit(solution)/shard_map/all_gather | solution.py:228
  10.9 246.2 %all-gather.22.cloned.1.call-start = ((), (), s32[]{:S(2)}) async-start(), calls=%async_computation.15 | async-start | bytes 6893568 | tf_op jit(solution)/shard_map/all_gather | solution.py:218
  12.9 256.2 %all-gather.20.cloned.1.call-start = ((), (), s32[]{:S(2)}) async-start(), calls=%async_computation.14 | async-start | bytes 4325376 | tf_op jit(solution)/shard_map/all_gather | solution.py:68
  166.9 235.2 %all-gather.24.cloned.1.call-start = ((), (), s32[]{:S(2)}) async-start(), calls=%async_computation.16 | async-start | bytes 4595712 | tf_op jit(solution)/shard_map/all_gather | solution.py:221
  167.7 252.2 %reduce-scatter.24.cloned.1.call-start = ((), (), s32[]{:S(2)}) async-start(), calls=%async_computation.17 | async-start | bytes 4325376 | tf_op jit(solution)/shard_map/reduce_scatter | solution.py:80
  409.8 146.8 %all-gather.30.cloned.1.call-start = ((), (), s32[]{:S(2)}) async-start(), calls=%async_computation.20 | async-start | bytes 2297856 | tf_op jit(solution)/shard_map/all_gather | solution.py:219
  410.6 158.3 %all-gather.28.cloned.1.call-start = ((), (), s32[]{:S(2)}) async-start(), calls=%async_computation.19 | async-start | bytes 4325376 | tf_op jit(solution)/shard_map/all_gather | solution.py:68
  425.8 211.6 %reduce-scatter.26.cloned.1.call-start = ((), (), s32[]{:S(2)}) async-start(), calls=%async_computation.21 | async-start | bytes 4325376 | tf_op jit(solution)/shard_map/reduce_scatter | solution.py:80
  625.6 132.5 %all-gather.34.cloned.1.call-start = ((), (), s32[]{:S(2)}) async-start(), calls=%async_computation.23 | async-start | bytes 9191424 | tf_op jit(solution)/shard_map/all_gather | solution.py:223
  627.7 142.4 %all-gather.32.cloned.1.call-start = ((), (), s32[]{:S(2)}) async-start(), calls=%async_computation.22 | async-start | bytes 4325376 | tf_op jit(solution)/shard_map/all_gather | solution.py:68
  643.4 143.1 %all-gather.38.cloned.1.call-start = ((), (), s32[]{:S(2)}) async-start(), calls=%async_computation.26 | async-start | bytes 4325376 | tf_op jit(solution)/shard_map/all_gather | solution.py:72
  644.1 260.3 %all-gather.36.cloned.1.call-start = ((), (), s32[]{:S(2)}) async-start(), calls=%async_computation.24 | async-start | bytes 9191424 | tf_op jit(solution)/shard_map/all_gather | solution.py:224
  645.1 317.4 %reduce-scatter.30.cloned.1.call-start = ((), (), s32[]{:S(2)}) async-start(), calls=%async_computation.27 | async-start | bytes 4325376 | tf_op jit(solution)/shard_map/reduce_scatter | solution.py:93
  1101.5 293.8 %reduce-scatter.34.cloned.1.call-start = ((), (), s32[]{:S(2)}) async-start(), calls=%async_computation.31 | async-start | bytes 4325376 | tf_op jit(solution)/shard_map/reduce_scatter | solution.py:93
  1319.4 203.9 %reduce-scatter.46.cloned.1.call-start = ((), (), s32[]{:S(2)}) async-start(), calls=%async_computation.38 | async-start | bytes 1671168
  1325.0 200.2 %reduce-scatter.36.cloned.1.call-start = ((), (), s32[]{:S(2)}) async-start(), calls=%async_computation.32 | async-start | bytes 1032192 | tf_op jit(solution)/shard_map/reduce_scatter | solution.py:321
  1374.0 407.5 %all-reduce.25.cloned.1.call-start = ((), (), s32[]{:S(2)}) async-start(), calls=%async_computation.40 | async-start | bytes 192512
  1419.8 653.5 %all-reduce.27.cloned.1.call-start = ((), (), s32[]{:S(2)}) async-start(), calls=%async_computation.41 | async-start | bytes 29884416
  1441.3 773.5 %reduce-scatter.40.cloned.1.call-start = ((), (), s32[]{:S(2)}) async-start(), calls=%async_computation.34 | async-start | bytes 4595712 | tf_op jit(solution)/shard_map/reduce_scatter | solution.py:373
  1448.3 1039.6 %reduce-scatter.44.cloned.1.call-start = ((), (), s32[]{:S(2)}) async-start(), calls=%async_computation.36 | async-start | bytes 18382848 | tf_op jit(solution)/shard_map/reduce_scatter | solution.py:378
  1465.8 1295.6 %reduce-scatter.42.cloned.1.call-start = ((), (), s32[]{:S(2)}) async-start(), calls=%async_computation.35 | async-start | bytes 18382848 | tf_op jit(solution)/shard_map/reduce_scatter | solution.py:377
  1481.5 1496.4 %reduce-scatter.38.cloned.1.call-start = ((), (), s32[]{:S(2)}) async-start(), calls=%async_computation.33 | async-start | bytes 13787136 | tf_op jit(solution)/shard_map/reduce_scatter | solution.py:372
  1507.9 1647.3 %reduce-scatter.48.cloned.1.call-start = ((), (), s32[]{:S(2)}) async-start(), calls=%async_computation.39 | async-start | bytes 16355328
  (241 other events, 7084.8 us)
Sparse Core Ops, SparseCore 0:
  11.6 65.2 all-gather.43
  80.3 74.4 all-gather.17
  158.1 98.9 all-gather.21
  272.2 78.2 all-gather.23
  408.2 11.6 reduce-scatter.23
  423.6 69.3 all-gather.25
  496.8 59.7 all-gather.29
  558.8 10.0 all-gather.27
  625.7 11.6 reduce-scatter.25
  640.8 117.3 all-gather.33
  771.7 12.8 all-gather.37
  787.8 116.5 all-gather.35
  978.2 12.9 all-gather.39
  1078.4 11.7 reduce-scatter.31
  1101.7 12.9 all-gather.41
  1319.5 11.6 reduce-scatter.33
  1336.0 125.7 reduce-scatter.45
  1480.0 124.4 all-reduce.24
  1610.8 462.5 all-reduce.26
  2079.0 135.6 reduce-scatter.39
  2222.1 265.7 reduce-scatter.43
  2495.3 266.1 reduce-scatter.41
  2768.7 209.1 reduce-scatter.37
  2980.8 174.4 reduce-scatter.47
  (5 shorter events, 43.2 us)
where the time goes:
time: 3180 us; the launch traced here: 3160 us
  waiting for transfers between devices  1770 us (56%)
  blocking collectives  427 us (13%)
  matrix products  336 us (11%)
  other arithmetic  306 us (10%)
  local copies, waits for them, and re-layouts  282 us (9%)
    unnamed x36, waiting for transfers between devices  464 us
    unnamed x4, blocking collectives  308 us
    reduce_scatter x1, waiting for transfers between devices, body(): lax.psum_scatter(grad_up, 'fsdp', scatter_dimension=0, tiled=True)  274 us
    reduce_scatter x1, waiting for transfers between devices, body(): lax.psum_scatter(grad_down, 'fsdp', scatter_dimension=1, tiled=True)  273 us
    reduce_scatter x1, waiting for transfers between devices, body(): lax.psum_scatter(grad_qkv_w, 'fsdp', scatter_dimension=0, tiled=True)  216 us
    reduce_scatter x1, waiting for transfers between devices, body(): lax.psum_scatter(grad_query_w, 'fsdp', scatter_dimension=0, tiled=True)  138 us
    all_gather x1, waiting for transfers between devices, body(): lax.all_gather(down_weight.astype(bfloat), 'fsdp', axis=1, tiled=True)  118 us
    dot_general x8, matrix products, dot_first(): lax.dot_general(first_operand, second_operand, (((0,), (0,)), ((), ())),...  80.7 us
  transfers between devices with their start and end apart: 32, of which 20 were waited for; matrix products, arithmetic and copies ran while one was open for 20% of the time, Pallas kernels for 0%

commit v1 on v0

v1 whole, which is shorter than its diff:
```python
import jax
import jax.numpy as jnp
import numpy as np
from jax import lax
from jax.experimental import pallas as pl
from jax.experimental.pallas import tpu as pltpu
from jax.sharding import PartitionSpec as P

HEAD_DIM = 88
SEQ = 1024
EPS_NORM = 1e-06
PRECISE = lax.Precision.HIGHEST
BF = jnp.bfloat16
F32 = jnp.float32


def hop(values, mask):
    count = lax.axis_size("fsdp")
    return lax.ppermute(values, "fsdp", [(i, i ^ mask) for i in range(count)])


def swap(values):
    return lax.ppermute(values, "tp", [(0, 1), (1, 0)])


def far_masks(count):
    return [4 * j for j in range(1, count // 4)]


def natural_masks(count):
    return np.array([(p // (count // 4) % 2) + 2 * (p // (count // 2)) + 4 * (p % (count // 4)) for p in range(count)])


def order_from_masks(values, masks):
    place = np.argsort(masks)
    table = jnp.asarray(place, jnp.int32)
    count = len(masks)
    wanted = jnp.arange(count, dtype=jnp.int32) ^ lax.axis_index("fsdp")
    return jnp.take(values, jnp.take(table, wanted), axis=0)


def gather_small(values):
    count = lax.axis_size("fsdp")
    parts = [values] + [hop(values, m) for m in far_masks(count)]
    held = jnp.stack(parts, axis=0)
    held = jnp.concatenate([held, hop(held, 1)], axis=0)
    held = jnp.concatenate([held, hop(held, 2)], axis=0)
    return order_from_masks(held, natural_masks(count))


def reduce_small(blocks):
    count = blocks.shape[0]
    masks = jnp.asarray(natural_masks(count), jnp.int32)
    held = jnp.take(blocks, masks ^ lax.axis_index("fsdp"), axis=0)
    half = count // 2
    held = held[:half] + hop(held[half:], 2)
    quarter = count // 4
    held = held[:quarter] + hop(held[quarter:], 1)
    total = held[0]
    for j, m in enumerate(far_masks(count)):
        total = total + hop(held[j + 1], m)
    return total


def xor_split(blocks, order, me):
    count, rows, columns = blocks.shape
    quarter = count // 4
    first, second = order

    def kernel(me_ref, keep_in, send_in, keep_out, send_out):
        keep_out[...] = keep_in[...]
        send_out[...] = send_in[...]

    def mask_of(p):
        return ((p // quarter) << second) + 4 * (p % quarter)

    block = (1, rows, columns)
    return pl.pallas_call(
        kernel,
        grid_spec=pltpu.PrefetchScalarGridSpec(
            num_scalar_prefetch=1,
            grid=(count // 2,),
            in_specs=[
                pl.BlockSpec(block, lambda p, me: (me[0] ^ mask_of(p), 0, 0)),
                pl.BlockSpec(block, lambda p, me: (me[0] ^ (mask_of(p) + (1 << first)), 0, 0)),
            ],
            out_specs=[pl.BlockSpec(block, lambda p, me: (p, 0, 0))] * 2,
        ),
        out_shape=[jax.ShapeDtypeStruct((count // 2, rows, columns), blocks.dtype)] * 2,
        cost_estimate=pl.CostEstimate(flops=0, bytes_accessed=4 * blocks.size, transcendentals=0),
    )(me, blocks, blocks)


def pair_split(blocks, order, me):
    count = blocks.shape[0] // 2
    rows, columns = blocks.shape[1:]
    quarter = count // 4
    first, second = order

    def kernel(me_ref, own_in, other_in, own_out, other_out):
        own_out[...] = own_in[...]
        other_out[...] = other_in[...]

    def mask_of(p):
        return ((p // (2 * quarter)) << first) + ((p // quarter % 2) << second) + 4 * (p % quarter)

    block = (1, rows, columns)
    return pl.pallas_call(
        kernel,
        grid_spec=pltpu.PrefetchScalarGridSpec(
            num_scalar_prefetch=1,
            grid=(count,),
            in_specs=[
                pl.BlockSpec(block, lambda p, me: (2 * (me[0] ^ mask_of(p)) + me[1], 0, 0)),
                pl.BlockSpec(block, lambda p, me: (2 * (me[0] ^ mask_of(p)) + me[2], 0, 0)),
            ],
            out_specs=[pl.BlockSpec(block, lambda p, me: (p, 0, 0))] * 2,
        ),
        out_shape=[jax.ShapeDtypeStruct((count, rows, columns), blocks.dtype)] * 2,
        cost_estimate=pl.CostEstimate(flops=0, bytes_accessed=4 * blocks.size, transcendentals=0),
    )(me, blocks, blocks)


def plus(first, second):
    return (first.astype(F32) + second.astype(F32)).astype(BF)


def near_stages(keep, send, first, second):
    quarter = keep.shape[0] // 2
    received = hop(send, 1 << first)
    sent = plus(keep[quarter:], received[quarter:])
    kept = plus(keep[:quarter], received[:quarter])
    return kept, hop(sent, 1 << second)


def far_stage(pairs, count):
    totals = [kept[0].astype(F32) + received[0].astype(F32) for kept, received in pairs]
    for j, m in enumerate(far_masks(count)):
        sent = [plus(kept[j + 1], received[j + 1]) for kept, received in pairs]
        same = all(s.shape[0] == sent[0].shape[0] for s in sent)
        if same:
            got = hop(jnp.concatenate(sent, axis=-1), m)
            edges = np.cumsum([s.shape[-1] for s in sent])[:-1].tolist()
            got = jnp.split(got, edges, axis=-1)
        else:
            got = [hop(s, m) for s in sent]
        totals = [total + g.astype(F32) for total, g in zip(totals, got)]
    return totals


def reduce_pair(first_blocks, second_blocks, me):
    count = first_blocks.shape[0]
    pairs = []
    for blocks, order in ((first_blocks, (0, 1)), (second_blocks, (1, 0))):
        keep, send = xor_split(blocks, order, me)
        pairs.append(near_stages(keep, send, *order))
    return far_stage(pairs, count)


def cut_of(width):
    return 128 * ((width // 128 + 1) // 2)


def reduce_product(left, right, me):
    count = lax.axis_size("fsdp")
    cut = cut_of(right.shape[1])
    parts = [dot_first(left, v).astype(BF) for v in (right[:, :cut], right[:, cut:])]
    parts = [v.reshape(count, -1, v.shape[1]) for v in parts]
    return jnp.concatenate(reduce_pair(parts[0], parts[1], me), axis=-1)


def reduce_product_all(left, right, me):
    count = lax.axis_size("fsdp")
    cut = cut_of(right.shape[1])
    half = count // 2
    pairs = []
    for part, order in ((right[:, :cut], (0, 1)), (right[:, cut:], (1, 0))):
        grad = dot_first(left, part).astype(BF)
        own, other = pair_split(grad.reshape(2 * count, -1, grad.shape[1]), order, me)
        got = swap(other)
        pairs.append(near_stages(plus(own[:half], got[:half]), plus(own[half:], got[half:]), *order))
    return jnp.concatenate(far_stage(pairs, count), axis=-1)


def layer_norm(values, scales, offsets):
    center = values - jnp.mean(values, axis=-1, keepdims=True)
    spread = jnp.mean(center * center, axis=-1, keepdims=True)
    return center * lax.rsqrt(spread + EPS_NORM) * scales + offsets


def head_norm(values, scales, offsets):
    row_count = values.shape[0]
    shaped = values.reshape(row_count, -1, HEAD_DIM)
    return layer_norm(shaped, scales, offsets).reshape(row_count, -1)


def rotary_tables(positions):
    quarter = HEAD_DIM // 4
    freqs = 10000.0 ** (-jnp.arange(quarter).astype(F32) / quarter)
    coords = positions.astype(F32)
    angles = jnp.concatenate([coords[:, 0:1] * freqs, coords[:, 1:2] * freqs], axis=1)
    angles = jnp.repeat(angles, 2, axis=1)
    return (jnp.cos(angles), jnp.sin(angles))


def rotate(values, cosine, sine):
    row_count = values.shape[0]
    head_count = values.shape[1] // HEAD_DIM
    paired = values.reshape(row_count, -1, 2)
    turned = jnp.stack([-paired[:, :, 1], paired[:, :, 0]], axis=2).reshape(row_count, -1)
    return values * jnp.tile(cosine, (1, head_count)) + turned * jnp.tile(sine, (1, head_count))


def plain_dot(first_operand, second_operand):
    return jnp.dot(first_operand, second_operand, preferred_element_type=F32)


def dot_first(first_operand, second_operand):
    return lax.dot_general(first_operand, second_operand, (((0,), (0,)), ((), ())), preferred_element_type=F32)


def dot_last(first_operand, second_operand):
    return lax.dot_general(first_operand, second_operand, (((1,), (1,)), ((), ())), preferred_element_type=F32)


def norm_parts(values):
    center = values - jnp.mean(values, axis=-1, keepdims=True)
    spread = jnp.mean(center * center, axis=-1, keepdims=True)
    inverse = lax.rsqrt(spread + EPS_NORM)
    return center * inverse, inverse


def norm_backward(grad, values, scales):
    normed, inverse = norm_parts(values)
    scaled = grad * scales
    result = inverse * (
        scaled
        - jnp.mean(scaled, axis=-1, keepdims=True)
        - normed * jnp.mean(scaled * normed, axis=-1, keepdims=True)
    )
    return result, jnp.sum(grad * normed, axis=0), jnp.sum(grad, axis=0)


def split_heads(values, image_count):
    return values.reshape(image_count, values.shape[0] // image_count, -1, HEAD_DIM)


def attention_forward(queries, keys, values, image_count):
    query_heads = split_heads(queries, image_count)
    key_heads = split_heads(keys, image_count)
    value_heads = split_heads(values, image_count)
    query_len = query_heads.shape[1]
    block_rows = min(512, query_len)
    scaling = HEAD_DIM ** (-0.5)
    outputs = []
    totals = []
    for offset_row in range(0, query_len, block_rows):
        query_piece = query_heads[:, offset_row : offset_row + block_rows]
        scores = jnp.einsum("iqhd,ikhd->ihqk", query_piece, key_heads, preferred_element_type=F32) * scaling
        row_peak = jnp.max(scores, axis=-1, keepdims=True)
        exponent = jnp.exp(scores - row_peak)
        summed = jnp.sum(exponent, axis=-1, keepdims=True)
        chances = exponent / summed
        outputs.append(jnp.einsum("ihqk,ikhd->iqhd", chances.astype(BF), value_heads, preferred_element_type=F32))
        totals.append(row_peak + jnp.log(summed))
    mixture = jnp.concatenate(outputs, axis=1).reshape(queries.shape[0], -1)
    return (mixture, totals)


def attention_backward(grad_mix, queries, keys, values, totals, image_count):
    query_heads = split_heads(queries, image_count)
    key_heads = split_heads(keys, image_count)
    value_heads = split_heads(values, image_count)
    grad_heads = split_heads(grad_mix, image_count)
    query_len = query_heads.shape[1]
    block_rows = min(512, query_len)
    scaling = HEAD_DIM ** (-0.5)
    grad_keys = jnp.zeros(key_heads.shape, F32)
    grad_values = jnp.zeros(value_heads.shape, F32)
    grad_queries = []
    for index_blk, offset_row in enumerate(range(0, query_len, block_rows)):
        query_piece = query_heads[:, offset_row : offset_row + block_rows]
        grad_piece = grad_heads[:, offset_row : offset_row + block_rows]
        scores = jnp.einsum("iqhd,ikhd->ihqk", query_piece, key_heads, preferred_element_type=F32) * scaling
        chances = jnp.exp(scores - totals[index_blk])
        grad_values = grad_values + jnp.einsum(
            "ihqk,iqhd->ikhd", chances.astype(BF), grad_piece, preferred_element_type=F32
        )
        grad_chance = jnp.einsum("iqhd,ikhd->ihqk", grad_piece, value_heads, preferred_element_type=F32)
        grad_score = chances * (grad_chance - jnp.sum(grad_chance * chances, axis=-1, keepdims=True))
        grad_low = grad_score.astype(BF)
        grad_queries.append(jnp.einsum("ihqk,ikhd->iqhd", grad_low, key_heads, preferred_element_type=F32) * scaling)
        grad_keys = (
            grad_keys + jnp.einsum("ihqk,iqhd->ikhd", grad_low, query_piece, preferred_element_type=F32) * scaling
        )
    query_grad = jnp.concatenate(grad_queries, axis=1).reshape(queries.shape[0], -1)
    return (query_grad, grad_keys.reshape(keys.shape[0], -1), grad_values.reshape(values.shape[0], -1))


def with_other(values):
    return jnp.concatenate([values, swap(values)], axis=0)


def branch_sum(operand, product, rows_local):
    sent = swap(product(operand[rows_local:]).astype(BF))
    return product(operand[:rows_local]) + sent.astype(F32)


def body(
    hidden,
    skip_rows,
    timestep,
    text,
    grid_pos,
    cotangent,
    skip_weight,
    shift_weight,
    qkv_weight,
    cross_query,
    cross_kv,
    out_weight,
    up_weight,
    down_weight,
    column_bias,
    up_bias,
    skip_gain,
    skip_bias,
    norm_gains,
    row_biases,
    head_gains,
    head_biases,
):
    count = lax.axis_size("fsdp")
    f_index = lax.axis_index("fsdp")
    t_index = lax.axis_index("tp")
    me = jnp.stack([f_index, t_index, 1 - t_index]).astype(jnp.int32)
    rows_local, model_width = hidden.shape
    image_count = timestep.shape[0]
    shard_rows = cross_query.shape[0]
    local_width = cross_query.shape[1]
    ff_local = up_weight.shape[1]
    text_width = cross_kv.shape[0] * count
    own_images = max(image_count // 2, 1)
    first_image = t_index * (image_count // 2)

    activated_own = jax.nn.silu(timestep.astype(F32)).astype(BF)
    small_parts = [column_bias, up_bias, skip_gain, skip_bias, norm_gains, row_biases]
    small = jnp.concatenate([p.astype(BF).reshape(-1) for p in small_parts] + [activated_own.reshape(-1)])
    small_own = gather_small(small)
    small_other = swap(small_own)
    first_is_own = t_index == 0
    small_both = jnp.stack(
        [jnp.where(first_is_own, small_own, small_other), jnp.where(first_is_own, small_other, small_own)], axis=1
    )
    edges = np.cumsum([0] + [p.size for p in small_parts])
    own_f = small_own.astype(F32)
    both_f = small_both.astype(F32)
    column_slice = column_bias.shape[2]
    col_bf = (
        own_f[:, edges[0] : edges[1]].reshape(count, 6, column_slice).transpose(1, 0, 2).reshape(6, local_width)
    )
    up_bf = own_f[:, edges[1] : edges[2]].reshape(-1)
    sgain_f = both_f[:, :, edges[2] : edges[3]].reshape(-1)
    sbias_f = both_f[:, :, edges[3] : edges[4]].reshape(-1)
    ngain_f = both_f[:, :, edges[4] : edges[5]].reshape(count, 2, 3, -1).transpose(2, 0, 1, 3).reshape(3, model_width)
    rbias_f = both_f[:, :, edges[5] : edges[6]].reshape(count, 2, 8, -1).transpose(2, 0, 1, 3).reshape(8, model_width)
    activated = small_own[:, edges[6] :].reshape(count * image_count, model_width)

    skip_w = lax.all_gather(skip_weight.astype(BF), ("fsdp", "tp"), axis=0, tiled=True)
    qkv_w = lax.all_gather(qkv_weight.astype(BF).reshape(shard_rows, -1), "fsdp", axis=0, tiled=True)
    out_t = out_weight.astype(BF).transpose(2, 0, 1).reshape(shard_rows, -1)
    proj_t = lax.all_gather(out_t, "fsdp", axis=0, tiled=True)
    self_t = proj_t[:, :local_width]
    cross_t = proj_t[:, local_width:]
    pair_w = lax.all_gather(cross_kv.astype(BF).reshape(cross_kv.shape[0], -1), "fsdp", axis=0, tiled=True)
    query_w = lax.all_gather(cross_query.astype(BF), "fsdp", axis=0, tiled=True)
    up_w = lax.all_gather(up_weight.astype(BF), "fsdp", axis=0, tiled=True)
    down_t = lax.all_gather(down_weight.astype(BF).T, "fsdp", axis=0, tiled=True)

    device_index = f_index * 2 + t_index
    shift_rows = shift_weight.shape[0]
    activated_cut = lax.dynamic_slice_in_dim(activated, device_index * shift_rows, shift_rows, 1)
    shift_term = plain_dot(activated_cut, shift_weight.astype(BF))
    shift_term = shift_term + swap(shift_term)
    shift_image = reduce_small(shift_term.reshape(count, -1)).reshape(image_count, model_width) + rbias_f[7]
    shift_own = lax.dynamic_slice_in_dim(shift_image, first_image, own_images, 0)
    shift_tokens = jnp.repeat(shift_own, rows_local // own_images, axis=0)

    text_shift = first_image

    def roll_images(values, shift):
        if image_count == 1:
            return values
        shaped = values.reshape(image_count, -1, values.shape[-1])
        return jnp.roll(shaped, shift, axis=0).reshape(values.shape)

    text_in = roll_images(text, -text_shift)
    pos_own = lax.dynamic_slice_in_dim(grid_pos, t_index * rows_local, rows_local, 0)
    pos_other = lax.dynamic_slice_in_dim(grid_pos, (1 - t_index) * rows_local, rows_local, 0)
    positions = jnp.concatenate([pos_own, pos_other], axis=0)

    joined = jnp.concatenate([hidden, skip_rows], axis=1).astype(F32)
    normed_skip = layer_norm(joined, sgain_f, sbias_f).astype(BF)
    stream_zero = plain_dot(normed_skip, skip_w) + rbias_f[6]
    first_in = with_other((layer_norm(stream_zero, ngain_f[0], rbias_f[0]) + shift_tokens).astype(BF))
    grad_ffn = with_other(cotangent)
    projected = plain_dot(first_in, qkv_w) + col_bf[0:3].reshape(-1)
    cosine, sine = rotary_tables(positions)

    def rotary_prep(values, scales, offsets):
        return rotate(head_norm(values, scales, offsets), cosine, sine)

    queries_f, query_pull = jax.vjp(rotary_prep, projected[:, :local_width], head_gains[0], head_biases[0])
    keys_f, key_pull = jax.vjp(
        rotary_prep, projected[:, local_width : 2 * local_width], head_gains[1], head_biases[1]
    )
    queries = queries_f.astype(BF)
    keys = keys_f.astype(BF)
    values = projected[:, 2 * local_width :].astype(BF)
    mixture_f, self_totals = attention_forward(queries, keys, values, image_count)
    mixture = mixture_f.astype(BF)
    stream_one = stream_zero + branch_sum(mixture, lambda v: dot_last(v, self_t), rows_local) + rbias_f[3]
    second_in = with_other(layer_norm(stream_one, ngain_f[1], rbias_f[1]).astype(BF))
    cross_pre = plain_dot(second_in, query_w) + col_bf[3].reshape(-1)
    pair_pre = plain_dot(text_in, pair_w) + col_bf[4:6].reshape(-1)
    cross_q_f, cross_q_pull = jax.vjp(rotary_prep, cross_pre, head_gains[2], head_biases[2])
    cross_k_f, cross_k_pull = jax.vjp(head_norm, pair_pre[:, :local_width], head_gains[3], head_biases[3])
    cross_queries = cross_q_f.astype(BF)
    cross_keys = cross_k_f.astype(BF)
    cross_values = pair_pre[:, local_width:].astype(BF)
    cross_mix_f, cross_totals = attention_forward(cross_queries, cross_keys, cross_values, image_count)
    cross_mixture = cross_mix_f.astype(BF)
    stream_two = stream_one + branch_sum(cross_mixture, lambda v: dot_last(v, cross_t), rows_local) + rbias_f[4]
    third_in = with_other(layer_norm(stream_two, ngain_f[2], rbias_f[2]).astype(BF))
    hidden_pre = plain_dot(third_in, up_w) + up_bf

    def gelu_tanh(v):
        return jax.nn.gelu(v, approximate=True)

    gelu_f, gelu_pull = jax.vjp(gelu_tanh, hidden_pre)
    hidden_act = gelu_f.astype(BF)
    stream_three = stream_two + branch_sum(hidden_act, lambda v: dot_last(v, down_t), rows_local) + rbias_f[5]
    output = stream_three.astype(BF)

    def blocks_of(grad):
        return grad.reshape(count, -1, grad.shape[-1])

    grad_three = cotangent.astype(F32)
    sent_down = reduce_product(grad_ffn, hidden_act, me).T
    grad_act = plain_dot(grad_ffn, down_t)
    grad_pre = gelu_pull(grad_act)[0].astype(BF)
    grad_upb = jnp.sum(grad_pre, axis=0, dtype=F32)
    grad_third = branch_sum(grad_pre, lambda v: dot_last(v, up_w), rows_local)
    sent_up = reduce_product(third_in, grad_pre, me)
    stream_grad, third_gain, third_bias = norm_backward(grad_third, stream_two, ngain_f[2])
    grad_two = grad_three + stream_grad
    grad_cross = with_other(grad_two.astype(BF))
    grad_cmix = plain_dot(grad_cross, cross_t).astype(BF)
    grad_cproj = dot_first(grad_cross, cross_mixture).astype(BF)
    cq_grad, ck_grad, cv_grad = attention_backward(
        grad_cmix, cross_queries, cross_keys, cross_values, cross_totals, image_count
    )
    cross_pre_grad, head_gain_two, head_bias_two = cross_q_pull(cq_grad)
    cross_key_grad, head_gain_three, head_bias_three = cross_k_pull(ck_grad)
    grad_cq = cross_pre_grad.astype(BF)
    grad_ck = cross_key_grad.astype(BF)
    grad_cv = cv_grad.astype(BF)
    grad_pair = jnp.concatenate([grad_ck, grad_cv], axis=1)
    grad_second = branch_sum(grad_cq, lambda v: dot_last(v, query_w), rows_local)
    grad_query_w = dot_first(second_in, grad_cq).astype(BF)
    sent_cproj, sent_query = reduce_pair(blocks_of(grad_cproj), blocks_of(grad_query_w), me)
    grad_k_w = dot_first(text_in, grad_ck).astype(BF)
    grad_v_w = dot_first(text_in, grad_cv).astype(BF)
    sent_k, sent_v = reduce_pair(blocks_of(grad_k_w), blocks_of(grad_v_w), me)
    text_half = text_width // 2
    pair_own = lax.dynamic_slice_in_dim(pair_w, t_index * text_half, text_half, 0)
    pair_other = lax.dynamic_slice_in_dim(pair_w, (1 - t_index) * text_half, text_half, 0)
    text_grad = dot_last(grad_pair, pair_own) + swap(dot_last(grad_pair, pair_other).astype(BF)).astype(F32)
    text_grad = roll_images(text_grad, text_shift)
    stream_grad, second_gain, second_bias = norm_backward(grad_second, stream_one, ngain_f[1])
    grad_one = grad_two + stream_grad
    grad_self = with_other(grad_one.astype(BF))
    grad_mix = plain_dot(grad_self, self_t).astype(BF)
    grad_sproj = dot_first(grad_self, mixture).astype(BF)
    query_grad, key_grad, value_grad = attention_backward(grad_mix, queries, keys, values, self_totals, image_count)
    query_pre_grad, head_gain_zero, head_bias_zero = query_pull(query_grad)
    key_pre_grad, head_gain_one, head_bias_one = key_pull(key_grad)
    grad_q = query_pre_grad.astype(BF)
    grad_k = key_pre_grad.astype(BF)
    grad_v = value_grad.astype(BF)
    grad_qkv = jnp.concatenate([grad_q, grad_k, grad_v], axis=1)
    grad_first = branch_sum(grad_qkv, lambda v: dot_last(v, qkv_w), rows_local)
    grad_wv = dot_first(first_in, grad_v).astype(BF)
    grad_wq = dot_first(first_in, grad_q).astype(BF)
    grad_wk = dot_first(first_in, grad_k).astype(BF)
    sent_sproj, sent_wv = reduce_pair(blocks_of(grad_sproj), blocks_of(grad_wv), me)
    sent_wq, sent_wk = reduce_pair(blocks_of(grad_wq), blocks_of(grad_wk), me)
    stream_grad, first_gain, first_bias = norm_backward(grad_first, stream_zero, ngain_f[0])
    grad_zero = grad_one + stream_grad
    grad_low_zero = grad_zero.astype(BF)
    sent_skip = reduce_product_all(normed_skip, grad_low_zero, me)
    grad_normed = dot_last(grad_low_zero, skip_w)
    joined_grad, skip_gain_part, skip_bias_part = norm_backward(grad_normed, joined, sgain_f)
    input_grad = joined_grad[:, :model_width]
    skip_grad = joined_grad[:, model_width:]

    shift_sums = jnp.sum(grad_first.reshape(own_images, -1, model_width), axis=1)
    if image_count == 1:
        shift_local = shift_sums
    else:
        shift_local = lax.dynamic_update_slice_in_dim(
            jnp.zeros((image_count, model_width), F32), shift_sums, first_image, 0
        )
    shift_local = shift_local + swap(shift_local)
    shift_all = gather_small(shift_local.reshape(-1)).reshape(count * image_count, model_width)
    sent_shift = lax.dot_general(
        activated_cut.astype(F32), shift_all, (((0,), (0,)), ((), ())), precision=PRECISE
    )

    grad_gains = jnp.stack([first_gain, second_gain, third_gain], axis=0)
    grad_biases = jnp.stack(
        [
            first_bias,
            second_bias,
            third_bias,
            jnp.sum(grad_one, axis=0),
            jnp.sum(grad_two, axis=0),
            jnp.sum(grad_three, axis=0),
            jnp.sum(grad_zero, axis=0),
            first_bias,
        ],
        axis=0,
    )
    grad_colb = jnp.concatenate(
        [
            jnp.sum(grad_qkv, axis=0, dtype=F32).reshape(3, local_width),
            jnp.sum(grad_cq, axis=0, dtype=F32).reshape(1, local_width),
            jnp.sum(grad_pair, axis=0, dtype=F32).reshape(2, local_width),
        ],
        axis=0,
    )
    head_part = jnp.concatenate(
        [
            jnp.stack([head_gain_zero, head_gain_one, head_gain_two, head_gain_three], axis=0).reshape(-1),
            jnp.stack([head_bias_zero, head_bias_one, head_bias_two, head_bias_three], axis=0).reshape(-1),
        ]
    )

    def by_device(values):
        shaped = values.reshape(values.shape[0], count, 2, -1).transpose(2, 1, 0, 3)
        return shaped.reshape(2, count, -1)

    shared = jnp.concatenate(
        [
            by_device(skip_gain_part[None]),
            by_device(skip_bias_part[None]),
            by_device(grad_gains),
            by_device(grad_biases),
            jnp.broadcast_to(head_part, (2, count, head_part.shape[0])),
        ],
        axis=-1,
    )
    shared_own = lax.dynamic_index_in_dim(shared, t_index, 0, keepdims=False)
    shared_other = lax.dynamic_index_in_dim(shared, 1 - t_index, 0, keepdims=False)
    shared_sum = shared_own + swap(shared_other)
    colb_blocks = grad_colb.reshape(6, count, -1).transpose(1, 0, 2).reshape(count, -1)
    upb_blocks = grad_upb.reshape(count, -1)
    small_sum = reduce_small(jnp.concatenate([shared_sum, colb_blocks, upb_blocks], axis=-1))
    lengths = [skip_gain.size, skip_bias.size, norm_gains.size, row_biases.size, head_gains.size, head_biases.size]
    lengths += [column_bias.size, up_bias.size]
    cuts = np.cumsum([0] + lengths)
    pieces = [small_sum[cuts[i] : cuts[i + 1]] for i in range(len(lengths))]

    sent_qkv = jnp.stack([sent_wq, sent_wk, sent_wv], axis=1)
    sent_pair = jnp.stack([sent_k, sent_v], axis=1)
    sent_proj = jnp.stack([sent_sproj.T, sent_cproj.T], axis=0)
    return (
        output,
        input_grad,
        skip_grad,
        text_grad,
        sent_skip,
        sent_shift,
        sent_qkv,
        sent_query,
        sent_pair,
        sent_proj,
        sent_up,
        sent_down,
        pieces[6].reshape(column_bias.shape),
        pieces[7].reshape(up_bias.shape),
        pieces[0],
        pieces[1],
        pieces[2].reshape(norm_gains.shape),
        pieces[3].reshape(row_biases.shape),
        pieces[4].reshape(head_gains.shape),
        pieces[5].reshape(head_biases.shape),
    )


def solution(mesh):
    in_specs = (
        P(("fsdp", "tp"), None),
        P(("fsdp", "tp"), None),
        P("fsdp", None),
        P("fsdp", None),
        P("fsdp", None),
        P(("fsdp", "tp"), None),
        P(("fsdp", "tp"), None),
        P(("fsdp", "tp"), None),
        P("fsdp", None, "tp"),
        P("fsdp", "tp"),
        P("fsdp", None, "tp"),
        P(None, "tp", "fsdp"),
        P("fsdp", "tp"),
        P("tp", "fsdp"),
        P(None, "tp", "fsdp"),
        P("tp", "fsdp"),
        P(("fsdp", "tp")),
        P(("fsdp", "tp")),
        P(None, ("fsdp", "tp")),
        P(None, ("fsdp", "tp")),
        P(),
        P(),
    )
    out_specs = (
        P(("fsdp", "tp"), None),
        P(("fsdp", "tp"), None),
        P(("fsdp", "tp"), None),
        P("fsdp", "tp"),
        P(("fsdp", "tp"), None),
        P(("fsdp", "tp"), None),
        P("fsdp", None, "tp"),
        P("fsdp", "tp"),
        P("fsdp", None, "tp"),
        P(None, "tp", "fsdp"),
        P("fsdp", "tp"),
        P("tp", "fsdp"),
        P(None, "tp", "fsdp"),
        P("tp", "fsdp"),
        P(("fsdp", "tp")),
        P(("fsdp", "tp")),
        P(None, ("fsdp", "tp")),
        P(None, ("fsdp", "tp")),
        P(),
        P(),
    )
    return jax.shard_map(body, mesh=mesh, in_specs=in_specs, out_specs=out_specs, check_vma=False)
```

time: 3180 us -> 1630 us (0.51)
  waiting for transfers between devices: 1770 us -> 457 us
  blocking collectives: 427 us -> 0 us
  Pallas kernels: 0 us -> 104 us
  starting transfers between devices: 20.9 us -> 108 us
  local copies, waits for them, and re-layouts: 282 us -> 248 us
    reduce_scatter x11 -> x0, waiting for transfers between devices: 935 us -> none  [the longest x1 274 us: body(): lax.psum_scatter(grad_up, 'fsdp', scatter_dimension=0, tiled=True)]
    unnamed x36 -> x7, waiting for transfers between devices: 464 us -> 0.11 us
    unnamed x4 -> x0, blocking collectives: 308 us -> none
    ppermute x0 -> x88, waiting for transfers between devices: none -> 173 us  [the longest x69 173 us: hop(): return lax.ppermute(values, 'fsdp', [(i, i ^ mask) for i in range(count)])]
    all_gather x3 -> x0, blocking collectives: 120 us -> none  [the longest x1 42 us: body(): lax.all_gather(column_bias.astype(bfloat), 'fsdp', axis=2, tiled=True)]
    ppermute x0 -> x88, starting transfers between devices: none -> 108 us  [the longest x69 104 us: hop(): return lax.ppermute(values, 'fsdp', [(i, i ^ mask) for i in range(count)])]
    pallas_call x0 -> x14, Pallas kernels: none -> 104 us  [the longest x12 81.3 us: xor_split(): pl.pallas_call(kernel, grid_spec=pltpu.PrefetchScalarGridSpec(num_scalar_...]
    all_gather x14 -> x7, waiting for transfers between devices: 371 us -> 284 us  [the longest x1 102 us: body(): lax.all_gather(down_weight.astype(BF).T, 'fsdp', axis=0, tiled=True)]
  transfers between devices with their start and end apart: 32 -> 95, of which waited for: 20 -> 36; matrix products, arithmetic and copies ran while one was open for 20% -> 40% of each run, Pallas kernels for 0% -> 6%
where the time goes in v1:
time: 1630 us; the launch traced here: 1610 us
  waiting for transfers between devices  457 us (28%)
  matrix products  366 us (22%)
  other arithmetic  310 us (19%)
  local copies, waits for them, and re-layouts  248 us (15%)
  starting transfers between devices  108 us (7%)
  Pallas kernels  104 us (6%)
  between operations  19.3 us (1%)
    ppermute x69, waiting for transfers between devices, hop(): return lax.ppermute(values, 'fsdp', [(i, i ^ mask) for i in range(count)])  173 us
    ppermute x69, starting transfers between devices, hop(): return lax.ppermute(values, 'fsdp', [(i, i ^ mask) for i in range(count)])  104 us
    all_gather x1, waiting for transfers between devices, body(): lax.all_gather(down_weight.astype(BF).T, 'fsdp', axis=0, tiled=True)  102 us
    dot_general x15, matrix products, dot_last(): lax.dot_general(first_operand, second_operand, (((1,), (1,)), ((), ())),...  86.7 us
    pallas_call x12, Pallas kernels, xor_split(): pl.pallas_call(kernel, grid_spec=pltpu.PrefetchScalarGridSpec(num_scalar_...  81.3 us
    dot_general x9, matrix products, plain_dot(): return jnp.dot(first_operand, second_operand, preferred_element_type=F32)  81.2 us
    dot_general x14, matrix products, dot_first(): lax.dot_general(first_operand, second_operand, (((0,), (0,)), ((), ())),...  81.1 us
    all_gather x1, waiting for transfers between devices, body(): lax.all_gather(qkv_weight.astype(BF).reshape(shard_rows, -1), 'fsdp', axi...  73.3 us
  transfers between devices with their start and end apart: 95, of which 36 were waited for; matrix products, arithmetic and copies ran while one was open for 40% of the time, Pallas kernels for 6%

profile of v1, /device:TPU:0, one launch (start us, length us, event | category | flops | bytes accessed | tf_op | source)
XLA Modules:
  0.0 1612.3 jit_solution(14334003067745558251)
XLA Ops:
  57.1 33.4 %all-gather.8.cloned.1.call-done = bf16[2816,1408]{1,0:T(8,128)(2,1)} async-done(((bf16[88,1408]{1,0:T(8,128)(2,1)}), bf16[2816,1408]{1,0:T(8,128)(2,1)}) %all-gather.8.cloned.1.call-update) | async-done | bytes 7929872 | tf_op jit(solution)/shard_map/all_gather | solution.py:369
  112.0 73.3 %all-gather.10.cloned.1.call-done = bf16[1408,2112]{1,0:T(8,128)(2,1)} async-done(((bf16[88,2112]{1,0:T(8,128)(2,1)}), bf16[1408,2112]{1,0:T(8,128)(2,1)}) %all-gather.10.cloned.1.call-update) | async-done | bytes 5947408 | tf_op jit(solution)/shard_map/all_gather | solution.py:370
  185.3 10.9 convolution_add_fusion
  364.5 27.3 %all-gather.16.cloned.1.call-done = bf16[1408,704]{1,0:T(8,128)(2,1)} async-done(((bf16[88,704]{1,0:T(8,128)(2,1)}), bf16[1408,704]{1,0:T(8,128)(2,1)}) %all-gather.16.cloned.1.call-update) | async-done | bytes 1982480 | tf_op jit(solution)/shard_map/all_gather | solution.py:376
  460.7 48.0 %all-gather.18.cloned.1.call-done = bf16[1408,3072]{1,0:T(8,128)(2,1)} async-done(((bf16[88,3072]{1,0:T(8,128)(2,1)}), bf16[1408,3072]{1,0:T(8,128)(2,1)}) %all-gather.18.cloned.1.call-update) | async-done | bytes 8650768 | tf_op jit(solution)/shard_map/all_gather | solution.py:377
  508.7 15.4 fusion.153
  524.1 101.6 %all-gather.20.cloned.1.call-done = bf16[1408,3072]{1,0:T(8,128)(2,1)} async-done(((bf16[88,3072]{1,0:T(8,128)(2,1)}), bf16[1408,3072]{1,0:T(8,128)(2,1)}) %all-gather.20.cloned.1.call-update) | async-done | bytes 8650768 | tf_op jit(solution)/shard_map/all_gather | solution.py:378
  625.7 25.6 %convert_reduce_fusion = (f32[3072]{0:T(1024)S(1)}, bf16[1024,3072]{1,0:T(8,128)(2,1)}, bf16[1024,3072]{1,0:T(8,128)(2,1)}) fusion(f32[1024,3072]{1,0:T(8,128)} %fusion.153, f32[3072]{0:T(1024)S(1)} %copy-done.203, bf16[1024,1408]{1,0:T(8,128)(2,1)} %copy-done.119, bf16[1408,3072]{1,0:T(8,128)(2,1)} %all-gather.20.cloned.1.call-done), kind=kOutput, calls=%fused_computation.28 | convolution fusion | flops 8937010176 | bytes 36724736 | tf_op jit(solution)/shard_map/dot_general | solution.py:215
  735.8 12.9 multiply_reduce_fusion.12
  748.8 13.3 fusion.298
  874.7 14.5 fusion.290
  996.1 14.9 collective-permute-done.80
  1022.3 35.0 %collective-permute-done.73 = bf16[88,3072]{1,0:T(8,128)(2,1)S(1)} collective-permute-done((bf16[88,3072]{1,0:T(8,128)(2,1)S(1)}, bf16[88,3072]{1,0:T(8,128)(2,1)S(1)}, u32[]{:S(2)}, u32[]{:S(2)}) %collective-permute-start.73) | collective-permute-done | bytes 540704 | tf_op jit(solution)/shard_map/ppermute | solution.py:19
  1069.2 16.0 collective-permute-start.65
  1104.8 12.8 collective-permute-done.59
  1126.0 15.3 multiply_reduce_fusion.1
  1158.3 15.3 multiply_reduce_fusion
  1269.3 27.3 %fusion.291 = (f32[352,2]{1,0:T(8,128)S(1)}, f32[1024,352]{0,1:T(8,128)}, f32[1024,352]{0,1:T(8,128)}, f32[352,2]{1,0:T(8,128)S(1)}) fusion(f32[1024,352,2]{0,2,1:T(2,128)} %reshape.1356, f32[1024,352,2]{0,2,1:T(2,128)} %tile.17, f32[1024,352,1]{0,2,1:T(1,128)} %copy-done.40, f32[1024,352,1]{0,2,1:T(1,128)} %copy-done.39, ...), kind=kLoop, calls=%fused_computation.673 | loop fusion | flops 15137408 | bytes 31730688 | tf_op jit(solution)/shard_map/transpose(jvp())/reduce_sum | solution.py:188
  1300.1 11.2 add_convert_fusion
  1414.5 14.4 collective-permute-done.42
  1482.1 11.1 shard_map.401
  1493.2 11.2 shard_map.402
  1566.7 12.1 collective-permute-done.45
  1591.8 12.1 collective-permute-done.32
  (1272 shorter events, 1008.2 us)
Async XLA Ops:
  7.2 83.3 %all-gather.8.cloned.1.call-start = ((), (), s32[]{:S(2)}) async-start(), calls=%async_computation | async-start | bytes 8177664 | tf_op jit(solution)/shard_map/all_gather | solution.py:369
  9.1 176.2 %all-gather.10.cloned.1.call-start = ((), (), s32[]{:S(2)}) async-start(), calls=%async_computation.1 | async-start | bytes 6510592 | tf_op jit(solution)/shard_map/all_gather | solution.py:370
  11.8 286.9 %all-gather.12.cloned.1.call-start = ((), (), s32[]{:S(2)}) async-start(), calls=%async_computation.2 | async-start | bytes 4212736 | tf_op jit(solution)/shard_map/all_gather | solution.py:372
  13.1 333.8 %all-gather.14.cloned.1.call-start = ((), (), s32[]{:S(2)}) async-start(), calls=%async_computation.3 | async-start | bytes 3063808 | tf_op jit(solution)/shard_map/all_gather | solution.py:375
  15.2 376.5 %all-gather.16.cloned.1.call-start = ((), (), s32[]{:S(2)}) async-start(), calls=%async_computation.4 | async-start | bytes 2297856 | tf_op jit(solution)/shard_map/all_gather | solution.py:376
  16.9 491.8 %all-gather.18.cloned.1.call-start = ((), (), s32[]{:S(2)}) async-start(), calls=%async_computation.5 | async-start | bytes 9191424 | tf_op jit(solution)/shard_map/all_gather | solution.py:377
  17.8 607.8 %all-gather.20.cloned.1.call-start = ((), (), s32[]{:S(2)}) async-start(), calls=%async_computation.6 | async-start | bytes 9191424 | tf_op jit(solution)/shard_map/all_gather | solution.py:378
  24.1 429.6 %collective-permute-start.18 = (bf16[512,1408]{1,0:T(8,128)(2,1)}, bf16[512,1408]{1,0:T(8,128)(2,1)}, u32[]{:S(2)}, u32[]{:S(2)}) collective-permute-start(bf16[512,1408]{1,0:T(8,128)(2,1)} %param.35), channel_id=1, source_target_pairs={{0,1},{1,0},{2,3},{3,2},{4,5},{5,4},{6,7},{7,6},{8,9},{9,8},{10,11... | collective-permute-start | bytes 4325384 | tf_op jit(solution)/shard_map/ppermute | solution.py:23
  101.5 83.9 %collective-permute-start.12 = (bf16[512,1408]{1,0:T(8,128)(2,1)}, bf16[512,1408]{1,0:T(8,128)(2,1)}, u32[]{:S(2)}, u32[]{:S(2)}) collective-permute-start(bf16[512,1408]{1,0:T(8,128)(2,1)} %add_convert_fusion.4), channel_id=1, source_target_pairs={{0,1},{1,0},{2,3},{3,2},{4,5},{5,4},{6,7},{7,6},{8,9},{9,8},{10,11... | collective-permute-start | bytes 4325384 | tf_op jit(solution)/shard_map/ppermute | solution.py:23
  322.9 68.8 %collective-permute-start.14 = (bf16[512,1408]{1,0:T(8,128)(2,1)}, bf16[512,1408]{1,0:T(8,128)(2,1)}, u32[]{:S(2)}, u32[]{:S(2)}) collective-permute-start(bf16[512,1408]{1,0:T(8,128)(2,1)} %add_convert_fusion.3), channel_id=1, source_target_pairs={{0,1},{1,0},{2,3},{3,2},{4,5},{5,4},{6,7},{7,6},{8,9},{9,8},{10,11... | collective-permute-start | bytes 4325384 | tf_op jit(solution)/shard_map/ppermute | solution.py:23
  682.7 66.0 %collective-permute-start.17 = (bf16[512,1408]{1,0:T(8,128)(2,1)}, bf16[512,1408]{1,0:T(8,128)(2,1)}, u32[]{:S(2)}, u32[]{:S(2)}) collective-permute-start(bf16[512,1408]{1,0:T(8,128)(2,1)} %fusion.50), channel_id=1, source_target_pairs={{0,1},{1,0},{2,3},{3,2},{4,5},{5,4},{6,7},{7,6},{8,9},{9,8},{10,11... | collective-permute-start | bytes 4325384 | tf_op jit(solution)/shard_map/ppermute | solution.py:23
  691.2 75.8 %collective-permute-start.75 = (bf16[8,88,1536]{2,1,0:T(8,128)(2,1)}, bf16[8,88,1536]{2,1,0:T(8,128)(2,1)}, u32[]{:S(2)}, u32[]{:S(2)}) collective-permute-start(bf16[8,88,1536]{2,1,0:T(8,128)(2,1)} %get-tuple-element.75), channel_id=1, source_target_pairs={{0,2},{2,0},{4,6},{6,4},{8,10},{10,8},{12,14},{14,12},{16,18},{18,... | collective-permute-start | bytes 6488072 | tf_op jit(solution)/shard_map/ppermute | solution.py:19
  700.2 72.2 %collective-permute-start.77 = (bf16[8,88,1536]{2,1,0:T(8,128)(2,1)}, bf16[8,88,1536]{2,1,0:T(8,128)(2,1)}, u32[]{:S(2)}, u32[]{:S(2)}) collective-permute-start(bf16[8,88,1536]{2,1,0:T(8,128)(2,1)} %get-tuple-element.77), channel_id=1, source_target_pairs={{0,4},{2,6},{4,0},{6,2},{8,12},{10,14},{12,8},{14,10},{16,20},{18,... | collective-permute-start | bytes 6488072 | tf_op jit(solution)/shard_map/ppermute | solution.py:19
  717.2 70.5 %collective-permute-start.68 = (bf16[8,88,1536]{2,1,0:T(8,128)(2,1)}, bf16[8,88,1536]{2,1,0:T(8,128)(2,1)}, u32[]{:S(2)}, u32[]{:S(2)}) collective-permute-start(bf16[8,88,1536]{2,1,0:T(8,128)(2,1)} %get-tuple-element.71), channel_id=1, source_target_pairs={{0,2},{2,0},{4,6},{6,4},{8,10},{10,8},{12,14},{14,12},{16,18},{18,... | collective-permute-start | bytes 6488072 | tf_op jit(solution)/shard_map/ppermute | solution.py:19
  735.2 61.7 %collective-permute-start.70 = (bf16[8,88,1536]{2,1,0:T(8,128)(2,1)}, bf16[8,88,1536]{2,1,0:T(8,128)(2,1)}, u32[]{:S(2)}, u32[]{:S(2)}) collective-permute-start(bf16[8,88,1536]{2,1,0:T(8,128)(2,1)} %get-tuple-element.73), channel_id=1, source_target_pairs={{0,4},{2,6},{4,0},{6,2},{8,12},{10,14},{12,8},{14,10},{16,20},{18,... | collective-permute-start | bytes 6488072 | tf_op jit(solution)/shard_map/ppermute | solution.py:19
  771.2 196.0 %collective-permute-start.76 = (bf16[4,88,1536]{2,1,0:T(8,128)(2,1)}, bf16[4,88,1536]{2,1,0:T(8,128)(2,1)}, u32[]{:S(2)}, u32[]{:S(2)}) collective-permute-start(bf16[4,88,1536]{2,1,0:T(8,128)(2,1)} %get-tuple-element.236), channel_id=1, source_target_pairs={{0,4},{2,6},{4,0},{6,2},{8,12},{10,14},{12,8},{14,10},{16,20},{18,... | collective-permute-start | bytes 3244040 | tf_op jit(solution)/shard_map/ppermute | solution.py:19
  776.0 193.7 %collective-permute-start.78 = (bf16[4,88,1536]{2,1,0:T(8,128)(2,1)}, bf16[4,88,1536]{2,1,0:T(8,128)(2,1)}, u32[]{:S(2)}, u32[]{:S(2)}) collective-permute-start(bf16[4,88,1536]{2,1,0:T(8,128)(2,1)} %get-tuple-element.238), channel_id=1, source_target_pairs={{0,2},{2,0},{4,6},{6,4},{8,10},{10,8},{12,14},{14,12},{16,18},{18,... | collective-permute-start | bytes 3244040 | tf_op jit(solution)/shard_map/ppermute | solution.py:19
  791.4 180.2 %collective-permute-start.69 = (bf16[4,88,1536]{2,1,0:T(8,128)(2,1)}, bf16[4,88,1536]{2,1,0:T(8,128)(2,1)}, u32[]{:S(2)}, u32[]{:S(2)}) collective-permute-start(bf16[4,88,1536]{2,1,0:T(8,128)(2,1)} %get-tuple-element.240), channel_id=1, source_target_pairs={{0,4},{2,6},{4,0},{6,2},{8,12},{10,14},{12,8},{14,10},{16,20},{18,... | collective-permute-start | bytes 3244040 | tf_op jit(solution)/shard_map/ppermute | solution.py:19
  800.5 174.3 %collective-permute-start.71 = (bf16[4,88,1536]{2,1,0:T(8,128)(2,1)}, bf16[4,88,1536]{2,1,0:T(8,128)(2,1)}, u32[]{:S(2)}, u32[]{:S(2)}) collective-permute-start(bf16[4,88,1536]{2,1,0:T(8,128)(2,1)} %get-tuple-element.242), channel_id=1, source_target_pairs={{0,2},{2,0},{4,6},{6,4},{8,10},{10,8},{12,14},{14,12},{16,18},{18,... | collective-permute-start | bytes 3244040 | tf_op jit(solution)/shard_map/ppermute | solution.py:19
  984.5 100.9 %collective-permute-start.21 = (bf16[512,1408]{1,0:T(8,128)(2,1)S(1)}, bf16[512,1408]{1,0:T(8,128)(2,1)S(1)}, u32[]{:S(2)}, u32[]{:S(2)}) collective-permute-start(bf16[512,1408]{1,0:T(8,128)(2,1)S(1)} %convolution_convert_fusion.13), channel_id=1, source_target_pairs={{0,1},{1,0},{2,3},{3,2},{4,5},{5,4},{6,7},{7,6},{8,9},{9,8},{10,11... | collective-permute-start | bytes 4325384 | tf_op jit(solution)/shard_map/ppermute | solution.py:23
  986.8 76.0 %collective-permute-start.56 = (bf16[8,88,704]{2,1,0:T(8,128)(2,1)S(1)}, bf16[8,88,704]{2,1,0:T(8,128)(2,1)S(1)}, u32[]{:S(2)}, u32[]{:S(2)}) collective-permute-start(bf16[8,88,704]{2,1,0:T(8,128)(2,1)S(1)} %copy-done.243), channel_id=1, source_target_pairs={{0,2},{2,0},{4,6},{6,4},{8,10},{10,8},{12,14},{14,12},{16,18},{18,... | collective-permute-start | bytes 2973704 | tf_op jit(solution)/shard_map/ppermute | solution.py:19
  1333.7 97.7 %collective-permute-start.23 = (bf16[512,1408]{1,0:T(8,128)(2,1)}, bf16[512,1408]{1,0:T(8,128)(2,1)}, u32[]{:S(2)}, u32[]{:S(2)}) collective-permute-start(bf16[512,1408]{1,0:T(8,128)(2,1)} %convolution_convert_fusion.12), channel_id=1, source_target_pairs={{0,1},{1,0},{2,3},{3,2},{4,5},{5,4},{6,7},{7,6},{8,9},{9,8},{10,11... | collective-permute-start | bytes 4325384 | tf_op jit(solution)/shard_map/ppermute | solution.py:23
  1407.2 97.4 %collective-permute-start.50 = (bf16[4,88,704]{2,1,0:T(8,128)(2,1)}, bf16[4,88,704]{2,1,0:T(8,128)(2,1)}, u32[]{:S(2)}, u32[]{:S(2)}) collective-permute-start(bf16[4,88,704]{2,1,0:T(8,128)(2,1)} %get-tuple-element.285), channel_id=1, source_target_pairs={{0,4},{2,6},{4,0},{6,2},{8,12},{10,14},{12,8},{14,10},{16,20},{18,... | collective-permute-start | bytes 1486856 | tf_op jit(solution)/shard_map/ppermute | solution.py:19
  1410.9 95.4 %collective-permute-start.48 = (bf16[4,88,704]{2,1,0:T(8,128)(2,1)}, bf16[4,88,704]{2,1,0:T(8,128)(2,1)}, u32[]{:S(2)}, u32[]{:S(2)}) collective-permute-start(bf16[4,88,704]{2,1,0:T(8,128)(2,1)} %get-tuple-element.287), channel_id=1, source_target_pairs={{0,2},{2,0},{4,6},{6,4},{8,10},{10,8},{12,14},{14,12},{16,18},{18,... | collective-permute-start | bytes 1486856 | tf_op jit(solution)/shard_map/ppermute | solution.py:19
  (344 other events, 5806.1 us)
Sparse Core Ops, SparseCore 0:
  11.5 78.9 all-gather.7
  93.8 91.4 all-gather.9
  188.6 72.3 all-gather.11
  264.2 64.4 all-gather.13
  331.3 60.3 all-gather.15
  394.9 113.7 all-gather.17
  512.1 113.5 all-gather.19

commit v2 on v1

v2 whole, which is shorter than its diff:
```python
import functools

import jax
import jax.numpy as jnp
import numpy as np
from jax import lax
from jax.experimental import pallas as pl
from jax.experimental.pallas import tpu as pltpu
from jax.sharding import PartitionSpec as P

HEAD_DIM = 88
SEQ = 1024
EPS_NORM = 1e-06
PRECISE = lax.Precision.HIGHEST
BF = jnp.bfloat16
F32 = jnp.float32
LOG2E = 1.4426950408889634
UP_ORDER = (1, 2)
DOWN_ORDER = (4, 2, 1)
VMEM_LIMIT = 56 * 1024 * 1024


def hop(values, mask):
    count = lax.axis_size("fsdp")
    return lax.ppermute(values, "fsdp", [(i, i ^ mask) for i in range(count)])


def swap(values):
    return lax.ppermute(values, "tp", [(0, 1), (1, 0)])


def far_masks(count):
    return [4 * j for j in range(1, count // 4)]


def natural_masks(count):
    return np.array([(p // (count // 4) % 2) + 2 * (p // (count // 2)) + 4 * (p % (count // 4)) for p in range(count)])


def order_from_masks(values, masks):
    place = np.argsort(masks)
    table = jnp.asarray(place, jnp.int32)
    count = len(masks)
    wanted = jnp.arange(count, dtype=jnp.int32) ^ lax.axis_index("fsdp")
    return jnp.take(values, jnp.take(table, wanted), axis=0)


def gather_small(values):
    count = lax.axis_size("fsdp")
    parts = [values] + [hop(values, m) for m in far_masks(count)]
    held = jnp.stack(parts, axis=0)
    held = jnp.concatenate([held, hop(held, 1)], axis=0)
    held = jnp.concatenate([held, hop(held, 2)], axis=0)
    return order_from_masks(held, natural_masks(count))


def reduce_small(blocks):
    count = blocks.shape[0]
    masks = jnp.asarray(natural_masks(count), jnp.int32)
    held = jnp.take(blocks, masks ^ lax.axis_index("fsdp"), axis=0)
    half = count // 2
    held = held[:half] + hop(held[half:], 2)
    quarter = count // 4
    held = held[:quarter] + hop(held[quarter:], 1)
    total = held[0]
    for j, m in enumerate(far_masks(count)):
        total = total + hop(held[j + 1], m)
    return total


ANYWHERE = pl.BlockSpec(memory_space=pl.ANY)


def steps_of(order, count):
    return tuple(order) + tuple(1 << b for b in range(30) if 1 << b < count and 1 << b not in order)


def near_mask(position, order):
    top = len(order) - 1
    return sum(((position >> (top - k)) & 1) * bit for k, bit in enumerate(order))


def place_of(mask, order):
    top = len(order) - 1
    return sum(((mask >> (bit.bit_length() - 1)) & 1) << (top - k) for k, bit in enumerate(order))


def halve(arrays, order, me, after=(), paired=False):
    count = arrays[0].shape[0] // (2 if paired else 1)
    rows, columns = arrays[0].shape[1:]
    order = steps_of(order, count)
    many = len(arrays)
    total = 2 * count if paired else count
    half = total // 2

    def kernel(me_ref, *refs):
        sources = refs[:many]
        low, high, held, in_sems, out_sems = refs[many + len(after) :]
        own = me_ref[0]

        def load(p, k):
            block = own ^ near_mask(p % count, order)
            if paired:
                block = 2 * block + me_ref[1 + p // count]
            return pltpu.make_async_copy(sources[k].at[block], held.at[p, k], in_sems.at[p])

        def store(p):
            target = low if p < half else high
            return pltpu.make_async_copy(held.at[p], target.at[p % half], out_sems.at[p])

        for p in list(range(half, total)) + list(range(half)):
            for k in range(many):
                load(p, k).start()
        for p in list(range(half, total)) + list(range(half)):
            for k in range(many):
                load(p, k).wait()
            store(p).start()
        for p in range(total):
            store(p).wait()

    moved = total * many * rows * columns
    shape = jax.ShapeDtypeStruct((half, many, rows, columns), arrays[0].dtype)
    return pl.pallas_call(
        kernel,
        grid_spec=pltpu.PrefetchScalarGridSpec(
            num_scalar_prefetch=1,
            grid=(1,),
            in_specs=[ANYWHERE] * (many + len(after)),
            out_specs=[ANYWHERE] * 2,
            scratch_shapes=[
                pltpu.VMEM((total, many, rows, columns), arrays[0].dtype),
                pltpu.SemaphoreType.DMA((total,)),
                pltpu.SemaphoreType.DMA((total,)),
            ],
        ),
        out_shape=[shape, shape],
        compiler_params=pltpu.CompilerParams(vmem_limit_bytes=VMEM_LIMIT),
        cost_estimate=pl.CostEstimate(flops=0, bytes_accessed=4 * moved, transcendentals=0),
    )(me, *arrays, *after)


def pin(values, after):
    def kernel(in_ref, *refs):
        refs[-1][...] = in_ref[...]

    whole = pl.BlockSpec(values.shape, lambda: (0,) * values.ndim)
    return pl.pallas_call(
        kernel,
        in_specs=[whole] + [ANYWHERE] * len(after),
        out_specs=whole,
        out_shape=jax.ShapeDtypeStruct(values.shape, values.dtype),
        cost_estimate=pl.CostEstimate(flops=0, bytes_accessed=4 * values.size, transcendentals=0),
    )(values, *after)


def tile_of(columns):
    return columns // 4 if columns % 512 == 0 else columns // 2 if columns % 256 == 0 else columns


def add_near(kept, received, after=(), part=None):
    doubled, many, rows, columns = kept.shape[-4:]
    quarter = doubled // 2
    tile = columns // 2 if columns % 256 == 0 else columns

    def kernel(kept_low, kept_high, got_low, got_high, *refs):
        low, high = refs[len(after) :]
        for out, first, second in ((low, kept_low, got_low), (high, kept_high, got_high)):
            total = first[...].astype(F32) + second[...].astype(F32)
            out[...] = total.reshape(out.shape).astype(kept.dtype)

    block = (1, many, rows, tile)

    def spec(shift):
        if part is None:
            return pl.BlockSpec(block, lambda i, j: (i + shift, 0, 0, j))
        return pl.BlockSpec((1, *block), lambda i, j: (part, i + shift, 0, 0, j))

    out_spec = pl.BlockSpec(block, lambda i, j: (i, 0, 0, j))
    shape = jax.ShapeDtypeStruct((quarter, many, rows, columns), kept.dtype)
    size = doubled * many * rows * columns
    return pl.pallas_call(
        kernel,
        grid=(quarter, columns // tile),
        in_specs=[spec(0), spec(quarter), spec(0), spec(quarter)] + [ANYWHERE] * len(after),
        out_specs=[out_spec] * 2,
        out_shape=[shape, shape],
        compiler_params=pltpu.CompilerParams(vmem_limit_bytes=VMEM_LIMIT),
        cost_estimate=pl.CostEstimate(flops=size, bytes_accessed=6 * size, transcendentals=0),
    )(kept, kept, received, received, *after)


def add_far(pairs, after=()):
    quarter, many, _, columns = pairs[0][0].shape
    heights = [pair[0].shape[2] for pair in pairs]
    rows = max(heights)
    half = quarter // 2
    parts = len(pairs)
    tile = tile_of(columns)
    arrays = [array for pair in pairs for array in pair]
    kind = arrays[0].dtype

    def kernel(*refs):
        outs = refs[2 * parts + len(after) :]
        for j in range(quarter):
            for p in range(parts):
                total = refs[2 * p][j].astype(F32) + refs[2 * p + 1][j].astype(F32)
                if heights[p] < rows:
                    total = jnp.concatenate([total, jnp.zeros((1, rows - heights[p], tile), F32)], axis=1)
                outs[j // half][p, j % half] = total.astype(kind)

    in_specs = [
        pl.BlockSpec((quarter, 1, height, tile), lambda k, i: (0, k, 0, i)) for height in heights for _ in range(2)
    ]
    out_spec = pl.BlockSpec((parts, half, 1, rows, tile), lambda k, i: (0, 0, k, 0, i))
    shape = (parts, half, many, rows, columns)
    size = parts * quarter * many * rows * columns
    return pl.pallas_call(
        kernel,
        grid=(many, columns // tile),
        in_specs=in_specs + [ANYWHERE] * len(after),
        out_specs=[out_spec] * 2,
        out_shape=[jax.ShapeDtypeStruct(shape, kind)] * 2,
        compiler_params=pltpu.CompilerParams(vmem_limit_bytes=VMEM_LIMIT),
        cost_estimate=pl.CostEstimate(flops=size, bytes_accessed=6 * size, transcendentals=0),
    )(*arrays, *after)


def add_halves(kept, received, after=()):
    parts, quarter, many, rows, columns = kept.shape
    half = quarter // 2

    def kernel(kept_ref, got_ref, *refs):
        outs = refs[len(after) :]
        for j in range(quarter):
            total = kept_ref[:, j].astype(F32) + got_ref[:, j].astype(F32)
            outs[j // half][:, j % half] = total.astype(kept.dtype)

    tile = tile_of(columns)
    in_spec = pl.BlockSpec((parts, quarter, 1, rows, tile), lambda k, i: (0, 0, k, 0, i))
    out_spec = pl.BlockSpec((parts, half, 1, rows, tile), lambda k, i: (0, 0, k, 0, i))
    shape = jax.ShapeDtypeStruct((parts, half, many, rows, columns), kept.dtype)
    return pl.pallas_call(
        kernel,
        grid=(many, columns // tile),
        in_specs=[in_spec] * 2 + [ANYWHERE] * len(after),
        out_specs=[out_spec] * 2,
        out_shape=[shape] * 2,
        compiler_params=pltpu.CompilerParams(vmem_limit_bytes=VMEM_LIMIT),
        cost_estimate=pl.CostEstimate(flops=kept.size, bytes_accessed=6 * kept.size, transcendentals=0),
    )(kept, received, *after)


class FarSum:
    def __init__(self, pairs, after=()):
        self.low, self.high = add_far(pairs, after)
        self.mask = 4
        self.got = hop(self.high, self.mask)

    def step(self, after=()):
        self.low, self.high = add_halves(self.low, self.got, after)
        self.mask *= 2
        self.got = hop(self.high, self.mask)

    def total(self):
        while self.low.shape[1] > 1:
            self.step()
        return self.low[:, 0].astype(F32) + self.got[:, 0].astype(F32)


class Chain:
    def __init__(self, halves, order):
        self.order = steps_of(order, lax.axis_size("fsdp"))
        self.low, self.high = halves
        self.at = 0
        self.got = hop(self.high, self.order[0])

    def step(self, after=()):
        self.low, self.high = add_near(self.low, self.got, after)
        self.at += 1
        self.got = hop(self.high, self.order[self.at])

    def total(self):
        while self.low.shape[0] > 1:
            self.step()
        return self.low[0].astype(F32) + self.got[0].astype(F32)


def join(first, second, after=()):
    count = first.shape[0]
    shape = (2 * count, *first.shape[1:])

    def kernel(first_ref, second_ref, *refs):
        out, held, sems = refs[len(after) :]

        def load(k):
            return pltpu.make_async_copy((first_ref, second_ref)[k], held.at[pl.ds(k * count, count)], sems.at[0, k])

        def store(k):
            part = pl.ds(k * count, count)
            return pltpu.make_async_copy(held.at[part], out.at[part], sems.at[1, k])

        for k in range(2):
            load(k).start()
        for k in range(2):
            load(k).wait()
            store(k).start()
        for k in range(2):
            store(k).wait()

    return pl.pallas_call(
        kernel,
        in_specs=[ANYWHERE] * (2 + len(after)),
        out_specs=ANYWHERE,
        out_shape=jax.ShapeDtypeStruct(shape, first.dtype),
        scratch_shapes=[pltpu.VMEM(shape, first.dtype), pltpu.SemaphoreType.DMA((2, 2))],
        compiler_params=pltpu.CompilerParams(vmem_limit_bytes=VMEM_LIMIT),
        cost_estimate=pl.CostEstimate(flops=0, bytes_accessed=8 * first.size, transcendentals=0),
    )(first, second, *after)


def products(groups, me, after=(), paired=False, tile=None):
    devices = lax.axis_size("fsdp")
    total = 2 * devices if paired else devices
    half = total // 2
    lefts, rights = [], []
    plan = []
    for order, terms in groups:
        column = 0
        steps = []
        for left, right, turned, start, width in terms:
            for array, known in ((left, lefts), (right, rights)):
                if not any(array is other for other in known):
                    known.append(array)
            which = [k for k, other in enumerate(lefts) if other is left][0]
            where = [k for k, other in enumerate(rights) if other is right][0]
            steps.append((which, where, turned, start, width, column))
            column += width
        plan.append((steps_of(order, devices), steps, terms[0][0].shape[1], column))

    def kernel(me_ref, *refs):
        left_refs = refs[: len(lefts)]
        right_refs = refs[len(lefts) : len(lefts) + len(rights)]
        rest = refs[len(lefts) + len(rights) + len(after) :]
        outs = rest[: 2 if paired else 2 * len(plan)]
        sums = rest[len(outs)]
        turned_lefts = rest[len(outs) + 1 :]
        own = me_ref[0]

        @pl.when(pl.program_id(0) == 0)
        def _():
            for k, ref in enumerate(left_refs):
                turned_lefts[k][...] = ref[...].T

        for g, (order, steps, rows, columns) in enumerate(plan):
            height = rows // total
            for which, where, turned, start, width, column in steps:
                if turned:
                    value = lax.dot_general(
                        turned_lefts[which][...],
                        right_refs[where][start : start + width, :],
                        (((1,), (1,)), ((), ())),
                        preferred_element_type=F32,
                    )
                elif tile:
                    value = jnp.dot(turned_lefts[which][...], right_refs[where][...], preferred_element_type=F32)
                else:
                    value = jnp.dot(
                        turned_lefts[which][...],
                        right_refs[where][:, start : start + width],
                        preferred_element_type=F32,
                    )
                width = tile or width
                sums[:rows, column : column + width] = value
            columns = tile or columns
            for b in range(total):
                block = sums[b * height : (b + 1) * height, :columns].astype(BF)
                if paired:
                    place = place_of(own ^ (b // 2), order)
                    upper = me_ref[1] != b % 2
                else:
                    place = place_of(own ^ b, order)
                    upper = place >= half
                    place = place % half

                @pl.when(upper)
                def _(g=g, block=block, place=place):
                    if paired:
                        outs[1][g, place, 0] = block
                    else:
                        outs[2 * g + 1][place, 0] = block

                @pl.when(jnp.logical_not(upper))
                def _(g=g, block=block, place=place):
                    if paired:
                        outs[0][g, place, 0] = block
                    else:
                        outs[2 * g][place, 0] = block

    once = pl.Buffered(1)
    left_specs = [pl.BlockSpec(a.shape, lambda i, me: (0, 0), pipeline_mode=once) for a in lefts]
    if tile:
        tiles = plan[0][3] // tile
        right_specs = [pl.BlockSpec((rights[0].shape[0], tile), lambda i, me: (0, i))]
        rows = plan[0][2] // total
        out_specs = [pl.BlockSpec((half, 1, rows, tile), lambda i, me: (0, 0, 0, i))] * 2
        shapes = [(half, 1, rows, plan[0][3])] * 2
    else:
        tiles = 1
        right_specs = [pl.BlockSpec(a.shape, lambda i, me: (0, 0), pipeline_mode=once) for a in rights]
        if paired:
            shapes = [(len(plan), half, 1, plan[0][2] // total, plan[0][3])] * 2
        else:
            shapes = [(half, 1, rows // total, columns) for _, _, rows, columns in plan for _ in range(2)]
        out_specs = [
            pl.BlockSpec(shape, lambda i, me, n=len(shape): (0,) * n, pipeline_mode=once) for shape in shapes
        ]
    flops = sum(2 * left.shape[0] * rows * columns for (_, _, rows, columns), left in zip(plan, [lefts[0]] * len(plan)))
    moved = sum(2 * a.size for a in lefts + rights) + sum(2 * int(np.prod(shape)) for shape in shapes)
    return pl.pallas_call(
        kernel,
        grid_spec=pltpu.PrefetchScalarGridSpec(
            num_scalar_prefetch=1,
            grid=(tiles,),
            in_specs=left_specs + right_specs + [ANYWHERE] * len(after),
            out_specs=out_specs,
            scratch_shapes=[
                pltpu.VMEM((max(p[2] for p in plan), tile or max(p[3] for p in plan)), F32)
            ]
            + [pltpu.VMEM(a.shape[::-1], BF) for a in lefts],
        ),
        out_shape=[jax.ShapeDtypeStruct(shape, BF) for shape in shapes],
        compiler_params=pltpu.CompilerParams(vmem_limit_bytes=VMEM_LIMIT),
        cost_estimate=pl.CostEstimate(flops=flops, bytes_accessed=moved, transcendentals=0),
    )(me, *lefts, *rights, *after)


def stack_near(halves, cut, after=()):
    half, rows, columns = halves[0].shape
    ranges = ((0, cut), (cut, columns - cut))

    def kernel(*refs):
        outs = refs[2 + len(after) : 4 + len(after)]
        held = refs[4 + len(after) : 6 + len(after)]
        sems = refs[-1]

        def load(p, k):
            source = refs[p].at[:, :, pl.ds(ranges[k][0], ranges[k][1])]
            return pltpu.make_async_copy(source, held[k].at[pl.ds(p * half, half)], sems.at[p, k])

        def store(p, k):
            part = pl.ds(p * half, half)
            return pltpu.make_async_copy(held[k].at[part], outs[k].at[part], sems.at[p, 2 + k])

        steps = [(p, k) for p in range(2) for k in range(2)]
        for step in steps:
            load(*step).start()
        for step in steps:
            load(*step).wait()
            store(*step).start()
        for step in steps:
            store(*step).wait()

    shapes = [(2 * half, rows, width) for _, width in ranges]
    return pl.pallas_call(
        kernel,
        in_specs=[ANYWHERE] * (2 + len(after)),
        out_specs=[ANYWHERE] * 2,
        out_shape=[jax.ShapeDtypeStruct(shape, BF) for shape in shapes],
        scratch_shapes=[pltpu.VMEM(shape, BF) for shape in shapes] + [pltpu.SemaphoreType.DMA((2, 4))],
        compiler_params=pltpu.CompilerParams(vmem_limit_bytes=VMEM_LIMIT),
        cost_estimate=pl.CostEstimate(flops=0, bytes_accessed=8 * half * rows * columns, transcendentals=0),
    )(*halves, *after)


def assemble(low, high, order, me, after=()):
    half, rows, columns = low.shape
    count = 2 * half
    order = steps_of(order, count)

    def kernel(me_ref, *refs):
        out, held, in_sems, out_sems = refs[2 + len(after) :]
        own = me_ref[0]

        def load(k):
            return pltpu.make_async_copy(refs[k], held.at[k], in_sems.at[k])

        def store(k, p):
            block = own ^ near_mask(k * half + p, order)
            return pltpu.make_async_copy(held.at[k, p], out.at[block], out_sems.at[k, p])

        for k in range(2):
            load(k).start()
        for k in range(2):
            load(k).wait()
            for p in range(half):
                store(k, p).start()
        for k in range(2):
            for p in range(half):
                store(k, p).wait()

    return pl.pallas_call(
        kernel,
        grid_spec=pltpu.PrefetchScalarGridSpec(
            num_scalar_prefetch=1,
            grid=(1,),
            in_specs=[ANYWHERE] * (2 + len(after)),
            out_specs=ANYWHERE,
            scratch_shapes=[
                pltpu.VMEM((2, half, rows, columns), BF),
                pltpu.SemaphoreType.DMA((2,)),
                pltpu.SemaphoreType.DMA((2, half)),
            ],
        ),
        out_shape=jax.ShapeDtypeStruct((count, rows, columns), BF),
        compiler_params=pltpu.CompilerParams(vmem_limit_bytes=VMEM_LIMIT),
        cost_estimate=pl.CostEstimate(flops=0, bytes_accessed=4 * count * rows * columns, transcendentals=0),
    )(me, low, high, *after)


def cut_of(width):
    return 128 * ((width // 128 + 1) // 2)


class Gather:
    def __init__(self, shard, cut, after=()):
        self.cut = cut
        self.held = (pin(shard, after) if after else shard)[None]
        self.mask = lax.axis_size("fsdp") // 2
        self.far = hop(self.held, self.mask)

    def double(self, after=()):
        self.held = join(self.held, self.far, after)
        self.mask //= 2
        self.far = hop(self.held, self.mask)

    def spread(self, after=()):
        while self.mask > 4:
            self.double(after)
        self.parts = stack_near((self.held, self.far), self.cut, after)
        self.near = [hop(self.parts[0], 1), hop(self.parts[1], 2)]

    def widen(self, after=()):
        self.low = [join(part, near, after) for part, near in zip(self.parts, self.near)]
        self.high = [hop(self.low[0], 2), hop(self.low[1], 1)]

    def finish(self, k, me, after=()):
        return assemble(self.low[k], self.high[k], ((2, 1), (1, 2))[k], me, after)


def weave(own, other, me):
    count, rows, _ = own[0].shape
    widths = [v.shape[2] for v in own]
    starts = [0, widths[0]]

    def kernel(me_ref, *refs):
        out, held, in_sems, out_sem = refs[4:]

        def load(k):
            target = held.at[:, me_ref[1 + k // 2], :, pl.ds(starts[k % 2], widths[k % 2])]
            return pltpu.make_async_copy(refs[k], target, in_sems.at[k])

        for k in range(4):
            load(k).start()
        for k in range(4):
            load(k).wait()
        store = pltpu.make_async_copy(held, out, out_sem)
        store.start()
        store.wait()

    shape = (count, 2, rows, sum(widths))
    whole = pl.pallas_call(
        kernel,
        grid_spec=pltpu.PrefetchScalarGridSpec(
            num_scalar_prefetch=1,
            grid=(1,),
            in_specs=[ANYWHERE] * 4,
            out_specs=ANYWHERE,
            scratch_shapes=[
                pltpu.VMEM(shape, BF),
                pltpu.SemaphoreType.DMA((4,)),
                pltpu.SemaphoreType.DMA,
            ],
        ),
        out_shape=jax.ShapeDtypeStruct(shape, BF),
        compiler_params=pltpu.CompilerParams(vmem_limit_bytes=VMEM_LIMIT),
        cost_estimate=pl.CostEstimate(flops=0, bytes_accessed=8 * count * rows * sum(widths), transcendentals=0),
    )(me, *own, *other)
    return whole.reshape(2 * count * rows, sum(widths))


def layer_norm(values, scales, offsets):
    center = values - jnp.mean(values, axis=-1, keepdims=True)
    spread = jnp.mean(center * center, axis=-1, keepdims=True)
    return center * lax.rsqrt(spread + EPS_NORM) * scales + offsets


def plain_dot(first_operand, second_operand):
    return jnp.dot(first_operand, second_operand, preferred_element_type=F32)


def dot_first(first_operand, second_operand):
    return lax.dot_general(first_operand, second_operand, (((0,), (0,)), ((), ())), preferred_element_type=F32)


def dot_last(first_operand, second_operand):
    return lax.dot_general(first_operand, second_operand, (((1,), (1,)), ((), ())), preferred_element_type=F32)


def turned_dot(first_operand, second_operand):
    return lax.dot_general(first_operand, second_operand, (((0,), (1,)), ((), ())), preferred_element_type=F32)


def fold_rows(values):
    return jnp.sum(values.reshape(-1, 8, values.shape[-1]), axis=0)


def row_block(rows):
    return 128 if rows % 128 == 0 else rows


def norm_back(partial, received, stream, gain, residual, images, after=()):
    rows, width = stream.shape
    block = row_block(rows)
    per_image = rows // images // block

    def kernel(partial_ref, received_ref, stream_ref, gain_ref, residual_ref, *refs):
        out_ref, low_ref, sums_ref = refs[len(after) :]
        grad = partial_ref[...] + received_ref[...].astype(F32)
        values = stream_ref[...]
        center = values - jnp.mean(values, axis=-1, keepdims=True)
        inverse = lax.rsqrt(jnp.mean(center * center, axis=-1, keepdims=True) + EPS_NORM)
        normed = center * inverse
        scaled = grad * gain_ref[...]
        result = residual_ref[...].astype(F32) + inverse * (
            scaled
            - jnp.mean(scaled, axis=-1, keepdims=True)
            - normed * jnp.mean(scaled * normed, axis=-1, keepdims=True)
        )
        out_ref[...] = result
        low_ref[...] = result.astype(BF)

        @pl.when(pl.program_id(0) % per_image == 0)
        def _():
            sums_ref[...] = jnp.zeros_like(sums_ref)

        sums_ref[0, 0] += fold_rows(grad * normed)
        sums_ref[0, 1] += fold_rows(grad)
        sums_ref[0, 2] += fold_rows(result)

    rows_spec = pl.BlockSpec((block, width), lambda i: (i, 0))
    return pl.pallas_call(
        kernel,
        grid=(rows // block,),
        in_specs=[rows_spec, rows_spec, rows_spec, pl.BlockSpec((1, width), lambda i: (0, 0)), rows_spec]
        + [ANYWHERE] * len(after),
        out_specs=[rows_spec, rows_spec, pl.BlockSpec((1, 3, 8, width), lambda i: (i // per_image, 0, 0, 0))],
        out_shape=[
            jax.ShapeDtypeStruct((rows, width), F32),
            jax.ShapeDtypeStruct((rows, width), BF),
            jax.ShapeDtypeStruct((images, 3, 8, width), F32),
        ],
        compiler_params=pltpu.CompilerParams(vmem_limit_bytes=VMEM_LIMIT),
        cost_estimate=pl.CostEstimate(flops=20 * rows * width, bytes_accessed=20 * rows * width, transcendentals=0),
    )(partial, received, stream, gain.reshape(1, -1), residual, *after)


def joined_back(grad, first, second, gain, after=()):
    rows, width = first.shape
    block = row_block(rows)

    def kernel(grad_ref, first_ref, second_ref, gain_ref, *refs):
        first_out, second_out, sums_ref = refs[len(after) :]
        parts = [slice(0, width), slice(width, 2 * width)]
        values = [first_ref[...].astype(F32), second_ref[...].astype(F32)]
        grads = [grad_ref[:, p] for p in parts]

        def mean(arrays):
            return sum(jnp.sum(a, axis=-1, keepdims=True) for a in arrays) * (0.5 / width)

        middle = mean(values)
        center = [v - middle for v in values]
        inverse = lax.rsqrt(mean([c * c for c in center]) + EPS_NORM)
        normed = [c * inverse for c in center]
        scaled = [g * gain_ref[:, p] for g, p in zip(grads, parts)]
        mean_scaled = mean(scaled)
        mean_product = mean([a * n for a, n in zip(scaled, normed)])
        results = [inverse * (a - mean_scaled - n * mean_product) for a, n in zip(scaled, normed)]
        first_out[...] = results[0]
        second_out[...] = results[1]

        @pl.when(pl.program_id(0) == 0)
        def _():
            sums_ref[...] = jnp.zeros_like(sums_ref)

        for p, g, n in zip(parts, grads, normed):
            sums_ref[0, :, p] += fold_rows(g * n)
            sums_ref[1, :, p] += fold_rows(g)

    rows_spec = pl.BlockSpec((block, width), lambda i: (i, 0))
    both_spec = pl.BlockSpec((block, 2 * width), lambda i: (i, 0))
    return pl.pallas_call(
        kernel,
        grid=(rows // block,),
        in_specs=[both_spec, rows_spec, rows_spec, pl.BlockSpec((1, 2 * width), lambda i: (0, 0))]
        + [ANYWHERE] * len(after),
        out_specs=[rows_spec, rows_spec, pl.BlockSpec((2, 8, 2 * width), lambda i: (0, 0, 0))],
        out_shape=[
            jax.ShapeDtypeStruct((rows, width), F32),
            jax.ShapeDtypeStruct((rows, width), F32),
            jax.ShapeDtypeStruct((2, 8, 2 * width), F32),
        ],
        compiler_params=pltpu.CompilerParams(vmem_limit_bytes=VMEM_LIMIT),
        cost_estimate=pl.CostEstimate(flops=40 * rows * width, bytes_accessed=20 * rows * width, transcendentals=0),
    )(grad, first, second, gain.reshape(1, -1), *after)


GELU_SCALE = 0.7978845608028654
GELU_CUBE = 0.044715


def first_layer(rows_in, weight, bias, after=()):
    rows, depth = rows_in.shape
    width = weight.shape[1]
    tile = 512 if width % 512 == 0 else width
    block = 1024 if rows % 1024 == 0 else rows
    step = 256 if block % 256 == 0 else block

    def kernel(rows_ref, weight_ref, bias_ref, *refs):
        act_ref, slope_ref = refs[len(after) :]
        for start in range(0, block, step):
            part = pl.ds(start, step)
            h = jnp.dot(rows_ref[part, :], weight_ref[...], preferred_element_type=F32) + bias_ref[...]
            square = h * h
            t = jnp.tanh(GELU_SCALE * h * (1.0 + GELU_CUBE * square))
            both = 0.5 * (1.0 + t)
            act_ref[part, :] = (h * both).astype(BF)
            slope = both + 0.5 * h * (1.0 - t * t) * (GELU_SCALE * (1.0 + 3.0 * GELU_CUBE * square))
            slope_ref[part, :] = slope.astype(BF)

    out_spec = pl.BlockSpec((block, tile), lambda m, n: (m, n))
    shape = jax.ShapeDtypeStruct((rows, width), BF)
    return pl.pallas_call(
        kernel,
        grid=(rows // block, width // tile),
        in_specs=[
            pl.BlockSpec((block, depth), lambda m, n: (m, 0)),
            pl.BlockSpec((depth, tile), lambda m, n: (0, n)),
            pl.BlockSpec((1, tile), lambda m, n: (0, n)),
        ]
        + [ANYWHERE] * len(after),
        out_specs=[out_spec] * 2,
        out_shape=[shape] * 2,
        compiler_params=pltpu.CompilerParams(vmem_limit_bytes=VMEM_LIMIT),
        cost_estimate=pl.CostEstimate(
            flops=2 * rows * depth * width, bytes_accessed=2 * depth * width + 4 * rows * width, transcendentals=rows * width
        ),
    )(rows_in, weight, bias.reshape(1, -1), *after)


def first_layer_back(grad, weight, slope, after=()):
    rows, depth = grad.shape
    width = weight.shape[1]
    tile = 512 if width % 512 == 0 else width
    block = 1024 if rows % 1024 == 0 else rows
    step = 256 if block % 256 == 0 else block

    def kernel(grad_ref, weight_ref, slope_ref, *refs):
        out_ref, sums_ref = refs[len(after) :]

        @pl.when(pl.program_id(1) == 0)
        def _():
            sums_ref[...] = jnp.zeros_like(sums_ref)

        for start in range(0, block, step):
            part = pl.ds(start, step)
            value = jnp.dot(grad_ref[part, :], weight_ref[...], preferred_element_type=F32)
            low = (value * slope_ref[part, :].astype(F32)).astype(BF)
            out_ref[part, :] = low
            sums_ref[...] += fold_rows(low.astype(F32))

    return pl.pallas_call(
        kernel,
        grid=(width // tile, rows // block),
        in_specs=[
            pl.BlockSpec((block, depth), lambda n, m: (m, 0)),
            pl.BlockSpec((depth, tile), lambda n, m: (0, n)),
            pl.BlockSpec((block, tile), lambda n, m: (m, n)),
        ]
        + [ANYWHERE] * len(after),
        out_specs=[pl.BlockSpec((block, tile), lambda n, m: (m, n)), pl.BlockSpec((8, tile), lambda n, m: (0, n))],
        out_shape=[jax.ShapeDtypeStruct((rows, width), BF), jax.ShapeDtypeStruct((8, width), F32)],
        compiler_params=pltpu.CompilerParams(vmem_limit_bytes=VMEM_LIMIT),
        cost_estimate=pl.CostEstimate(
            flops=2 * rows * depth * width, bytes_accessed=2 * depth * width + 4 * rows * width, transcendentals=0
        ),
    )(grad, weight, slope, *after)


def head_parts(values):
    center = values - jnp.sum(values, axis=0, keepdims=True) * (1.0 / HEAD_DIM)
    spread = jnp.sum(center * center, axis=0, keepdims=True) * (1.0 / HEAD_DIM)
    inverse = lax.rsqrt(spread + EPS_NORM)
    return center * inverse, inverse


def turn(values, up_table, down_table):
    up = pltpu.roll(values, HEAD_DIM - 1, 0)
    down = pltpu.roll(values, 1, 0)
    return up * up_table + down * down_table


def head_forward(values, gain, offset, tables):
    normed, _ = head_parts(values)
    result = normed * gain + offset
    if tables is not None:
        result = result * tables[0] + turn(result, tables[1], tables[2])
    return result.astype(BF)


def fold_lanes(values):
    total = values[:, :128]
    for start in range(128, values.shape[1], 128):
        total = total + values[:, start : start + 128]
    return total


def head_backward(grad, values, gain, tables):
    if tables is not None:
        grad = grad * tables[0] - turn(grad, tables[1], tables[2])
    normed, inverse = head_parts(values)
    scaled = grad * gain
    mean_scaled = jnp.sum(scaled, axis=0, keepdims=True) * (1.0 / HEAD_DIM)
    mean_product = jnp.sum(scaled * normed, axis=0, keepdims=True) * (1.0 / HEAD_DIM)
    result = inverse * (scaled - mean_scaled - normed * mean_product)
    return result, fold_lanes(grad * normed), fold_lanes(grad)


def score_mask(scores, valid):
    if valid == scores.shape[0]:
        return scores
    row = lax.broadcasted_iota(jnp.int32, scores.shape, 0)
    return jnp.where(row < valid, scores, -1e30)


CHUNK = 256


def attend_kernel(valid, turned, waits, q_ref, k_ref, v_ref, gain_ref, bias_ref, tab_ref, *refs):
    out_ref, lse_ref, q_s, kt_s, v_s = refs[waits:]
    scaling = HEAD_DIM ** (-0.5)
    tables = (tab_ref[0], tab_ref[1], tab_ref[2])
    q_s[...] = head_forward(q_ref[0, 0], gain_ref[0], bias_ref[0], tables)
    keys = head_forward(k_ref[0, 0], gain_ref[1], bias_ref[1], tables if turned else None)
    kt_s[...] = keys.T
    v_s[...] = v_ref[0, 0].astype(BF)
    for start in range(0, q_s.shape[1], CHUNK):
        cols = pl.ds(start, CHUNK)
        scores = jnp.dot(kt_s[...], q_s[:, cols], preferred_element_type=F32)
        scores = score_mask(scores, valid)
        peak = jnp.max(scores, axis=0, keepdims=True)
        exponent = jnp.exp2((scores - peak) * (scaling * LOG2E))
        summed = jnp.sum(exponent, axis=0, keepdims=True)
        mixed = jnp.dot(v_s[...], exponent.astype(BF), preferred_element_type=F32)
        out_ref[0, :, cols] = (mixed * (1.0 / summed)).astype(BF)
        lse_ref[0, :, cols] = peak * scaling + jnp.log(summed)


def head_specs(lead, length):
    return pl.BlockSpec((1, 1, HEAD_DIM, length), lambda i, h: (lead, h, 0, i))


def attend(q_pre, k_pre, v_pre, leads, gains, biases, tables, valid, turned, after=()):
    heads = q_pre.shape[1]
    images = q_pre.shape[3] // SEQ
    key_len = k_pre.shape[3] // images
    per_head = pl.BlockSpec((2, HEAD_DIM, 1), lambda i, h: (0, 0, 0))
    work = images * heads * SEQ * key_len
    return pl.pallas_call(
        functools.partial(attend_kernel, valid, turned, len(after)),
        grid=(images, heads),
        in_specs=[
            head_specs(leads[0], SEQ),
            head_specs(leads[1], key_len),
            head_specs(leads[2], key_len),
            per_head,
            per_head,
            pl.BlockSpec((3, HEAD_DIM, SEQ), lambda i, h: (0, 0, i)),
        ]
        + [ANYWHERE] * len(after),
        out_specs=[
            pl.BlockSpec((1, HEAD_DIM, SEQ), lambda i, h: (h, 0, i)),
            pl.BlockSpec((1, 1, SEQ), lambda i, h: (h, 0, i)),
        ],
        out_shape=[
            jax.ShapeDtypeStruct((heads, HEAD_DIM, images * SEQ), BF),
            jax.ShapeDtypeStruct((heads, 1, images * SEQ), F32),
        ],
        scratch_shapes=[
            pltpu.VMEM((HEAD_DIM, SEQ), BF),
            pltpu.VMEM((key_len, HEAD_DIM), BF),
            pltpu.VMEM((HEAD_DIM, key_len), BF),
        ],
        compiler_params=pltpu.CompilerParams(vmem_limit_bytes=VMEM_LIMIT),
        cost_estimate=pl.CostEstimate(flops=4 * work * 128, bytes_accessed=12 * q_pre.size, transcendentals=work),
    )(q_pre, k_pre, v_pre, gains, biases, tables, *after)


def attend_back_kernel(
    valid, turned, joint, waits, q_ref, k_ref, v_ref, mix_ref, lse_ref, gain_ref, bias_ref, tab_ref, *rest
):
    rest = rest[waits:]
    if joint:
        g_ref, sums_ref, cols_ref, q_s, k_s, kt_s, vt_s, dq_s, dk_s, dv_s = rest
    else:
        gq_ref, gkv_ref, sums_ref, cols_ref, q_s, k_s, kt_s, vt_s, dq_s, dk_s, dv_s = rest
    scaling = HEAD_DIM ** (-0.5)
    tables = (tab_ref[0], tab_ref[1], tab_ref[2])
    key_tables = tables if turned else None
    q_s[...] = head_forward(q_ref[0, 0], gain_ref[0], bias_ref[0], tables)
    keys = head_forward(k_ref[0, 0], gain_ref[1], bias_ref[1], key_tables)
    k_s[...] = keys
    kt_s[...] = keys.T
    vt_s[...] = v_ref[0, 0].astype(BF).T
    last = (((1,), (1,)), ((), ()))
    for start in range(0, q_s.shape[1], CHUNK):
        cols = pl.ds(start, CHUNK)
        scores = jnp.dot(kt_s[...], q_s[:, cols], preferred_element_type=F32)
        scores = score_mask(scores, valid)
        chances = jnp.exp2(scores * (scaling * LOG2E) - lse_ref[0, :, cols] * LOG2E)
        grad_mix = mix_ref[0, :, cols]
        grad_chance = jnp.dot(vt_s[...], grad_mix, preferred_element_type=F32)
        row_sum = jnp.sum(grad_chance * chances, axis=0, keepdims=True)
        grad_low = (chances * (grad_chance - row_sum)).astype(BF)
        dq_s[:, cols] = jnp.dot(k_s[...], grad_low, preferred_element_type=F32) * scaling
        key_term = lax.dot_general(q_s[:, cols], grad_low, last, preferred_element_type=F32) * scaling
        value_term = lax.dot_general(grad_mix, chances.astype(BF), last, preferred_element_type=F32)
        if start == 0:
            dk_s[...] = key_term
            dv_s[...] = value_term
        else:
            dk_s[...] += key_term
            dv_s[...] += value_term
    grad_q, gain_q, bias_q = head_backward(dq_s[...], q_ref[0, 0], gain_ref[0], tables)
    grad_k, gain_k, bias_k = head_backward(dk_s[...], k_ref[0, 0], gain_ref[1], key_tables)
    outs = [grad_q.astype(BF), grad_k.astype(BF), dv_s[...].astype(BF)]
    if joint:
        for j in range(3):
            g_ref[j, 0] = outs[j]
    else:
        gq_ref[0, 0] = outs[0]
        gkv_ref[0, 0] = outs[1]
        gkv_ref[1, 0] = outs[2]

    @pl.when((pl.program_id(0) == 0) & (pl.program_id(1) == 0))
    def _():
        sums_ref[...] = jnp.zeros_like(sums_ref)

    for j, part in enumerate((gain_q, gain_k, bias_q, bias_k)):
        sums_ref[j] += part
    for j, part in enumerate(outs):
        cols_ref[0, j, 0] = fold_lanes(part.astype(F32))


def attend_back(q_pre, k_pre, v_pre, leads, grad_mix, lse, gains, biases, tables, valid, turned, joint, after=()):
    heads = q_pre.shape[1]
    images = q_pre.shape[3] // SEQ
    key_len = k_pre.shape[3] // images
    per_head = pl.BlockSpec((2, HEAD_DIM, 1), lambda i, h: (0, 0, 0))
    work = images * heads * SEQ * key_len
    grads = [(3, SEQ)] if joint else [(1, SEQ), (2, key_len)]
    return pl.pallas_call(
        functools.partial(attend_back_kernel, valid, turned, joint, len(after)),
        grid=(images, heads),
        in_specs=[
            head_specs(leads[0], SEQ),
            head_specs(leads[1], key_len),
            head_specs(leads[2], key_len),
            pl.BlockSpec((1, HEAD_DIM, SEQ), lambda i, h: (h, 0, i)),
            pl.BlockSpec((1, 1, SEQ), lambda i, h: (h, 0, i)),
            per_head,
            per_head,
            pl.BlockSpec((3, HEAD_DIM, SEQ), lambda i, h: (0, 0, i)),
        ]
        + [ANYWHERE] * len(after),
        out_specs=[
            pl.BlockSpec((size, 1, HEAD_DIM, length), lambda i, h: (0, h, 0, i)) for size, length in grads
        ]
        + [
            pl.BlockSpec((4, HEAD_DIM, 128), lambda i, h: (0, 0, 0)),
            pl.BlockSpec((1, 3, 1, HEAD_DIM, 128), lambda i, h: (i, 0, h, 0, 0)),
        ],
        out_shape=[jax.ShapeDtypeStruct((size, heads, HEAD_DIM, images * length), BF) for size, length in grads]
        + [
            jax.ShapeDtypeStruct((4, HEAD_DIM, 128), F32),
            jax.ShapeDtypeStruct((images, 3, heads, HEAD_DIM, 128), F32),
        ],
        scratch_shapes=[
            pltpu.VMEM((HEAD_DIM, SEQ), BF),
            pltpu.VMEM((HEAD_DIM, key_len), BF),
            pltpu.VMEM((key_len, HEAD_DIM), BF),
            pltpu.VMEM((key_len, HEAD_DIM), BF),
            pltpu.VMEM((HEAD_DIM, SEQ), F32),
            pltpu.VMEM((HEAD_DIM, key_len), F32),
            pltpu.VMEM((HEAD_DIM, key_len), F32),
        ],
        compiler_params=pltpu.CompilerParams(vmem_limit_bytes=VMEM_LIMIT),
        cost_estimate=pl.CostEstimate(flops=10 * work * 128, bytes_accessed=20 * q_pre.size, transcendentals=work),
    )(q_pre, k_pre, v_pre, grad_mix, lse, gains, biases, tables, *after)


def rotary_columns(positions):
    quarter = HEAD_DIM // 4
    freqs = 10000.0 ** (-jnp.arange(quarter).astype(F32) / quarter)
    coords = positions.astype(F32).T
    angles = jnp.concatenate([freqs[:, None] * coords[0:1], freqs[:, None] * coords[1:2]], axis=0)
    angles = jnp.repeat(angles, 2, axis=0)
    even = (jnp.arange(HEAD_DIM) % 2 == 0)[:, None]
    sine = jnp.sin(angles)
    return jnp.stack([jnp.cos(angles), jnp.where(even, -sine, 0.0), jnp.where(even, 0.0, sine)])


def with_other(values):
    return jnp.concatenate([values, swap(values)], axis=0)


def branch_sum(operand, weight, rows_local):
    sent = swap(dot_last(operand[rows_local:], weight).astype(BF))
    return dot_last(operand[:rows_local], weight) + sent.astype(F32)


def branch_parts(operand, weight, rows_local):
    sent = swap(dot_last(operand[rows_local:], weight).astype(BF))
    return dot_last(operand[:rows_local], weight), sent


def turned_branch_parts(operand, weight, rows_local):
    sent = swap(turned_dot(operand[:, rows_local:], weight).astype(BF))
    return turned_dot(operand[:, :rows_local], weight), sent


def turned_branch_sum(operand, weight, rows_local):
    sent = swap(turned_dot(operand[:, rows_local:], weight).astype(BF))
    return turned_dot(operand[:, :rows_local], weight) + sent.astype(F32)


def body(
    hidden,
    skip_rows,
    timestep,
    text,
    grid_pos,
    cotangent,
    skip_weight,
    shift_weight,
    qkv_weight,
    cross_query,
    cross_kv,
    out_weight,
    up_weight,
    down_weight,
    column_bias,
    up_bias,
    skip_gain,
    skip_bias,
    norm_gains,
    row_biases,
    head_gains,
    head_biases,
):
    count = lax.axis_size("fsdp")
    f_index = lax.axis_index("fsdp")
    t_index = lax.axis_index("tp")
    me = jnp.stack([f_index, t_index, 1 - t_index]).astype(jnp.int32)
    rows_local, model_width = hidden.shape
    image_count = timestep.shape[0]
    shard_rows = cross_query.shape[0]
    local_width = cross_query.shape[1]
    ff_local = up_weight.shape[1]
    text_width = cross_kv.shape[0] * count
    own_images = max(image_count // 2, 1)
    first_image = t_index * (image_count // 2)

    skip_gather = Gather(skip_weight.astype(BF), cut_of(model_width))

    activated_own = jax.nn.silu(timestep.astype(F32)).astype(BF)
    small_parts = [column_bias, up_bias, skip_gain, skip_bias, norm_gains, row_biases]
    small = jnp.concatenate([p.astype(BF).reshape(-1) for p in small_parts] + [activated_own.reshape(-1)])
    small_own = gather_small(small)
    small_other = swap(small_own)
    first_is_own = t_index == 0
    small_both = jnp.stack(
        [jnp.where(first_is_own, small_own, small_other), jnp.where(first_is_own, small_other, small_own)], axis=1
    )
    edges = np.cumsum([0] + [p.size for p in small_parts])
    own_f = small_own.astype(F32)
    both_f = small_both.astype(F32)
    column_slice = column_bias.shape[2]
    col_bf = (
        own_f[:, edges[0] : edges[1]].reshape(count, 6, column_slice).transpose(1, 0, 2).reshape(6, local_width)
    )
    up_bf = own_f[:, edges[1] : edges[2]].reshape(-1)
    sgain_f = both_f[:, :, edges[2] : edges[3]].reshape(-1)
    sbias_f = both_f[:, :, edges[3] : edges[4]].reshape(-1)
    ngain_f = both_f[:, :, edges[4] : edges[5]].reshape(count, 2, 3, -1).transpose(2, 0, 1, 3).reshape(3, model_width)
    rbias_f = both_f[:, :, edges[5] : edges[6]].reshape(count, 2, 8, -1).transpose(2, 0, 1, 3).reshape(8, model_width)
    activated = small_own[:, edges[6] :].reshape(count * image_count, model_width)

    attention_shard = jnp.concatenate(
        [qkv_weight.astype(BF).reshape(shard_rows, -1), cross_query.astype(BF)], axis=1
    )
    attention_gather = Gather(attention_shard, 2 * local_width)
    skip_gather.double()
    skip_gather.spread()
    attention_gather.double((skip_gather.parts[0],))
    skip_gather.widen((attention_gather.held,))
    out_t = out_weight.astype(BF).transpose(2, 0, 1).reshape(shard_rows, -1)
    pair_shard = cross_kv.astype(BF).reshape(shard_rows, -1)
    branch_gather = Gather(jnp.concatenate([out_t, pair_shard], axis=1), 2 * local_width, (skip_gather.low[0],))
    skip_own = [skip_gather.finish(k, me, (branch_gather.held,)) for k in range(2)]
    skip_w = weave(skip_own, [swap(v) for v in skip_own], me)
    attention_gather.spread((skip_own[1],))
    branch_gather.double((attention_gather.parts[0],))

    device_index = f_index * 2 + t_index
    shift_rows = shift_weight.shape[0]
    activated_cut = lax.dynamic_slice_in_dim(activated, device_index * shift_rows, shift_rows, 1)
    shift_term = plain_dot(activated_cut, shift_weight.astype(BF))
    shift_term = shift_term + swap(shift_term)
    shift_image = reduce_small(shift_term.reshape(count, -1)).reshape(image_count, model_width) + rbias_f[7]
    shift_own = lax.dynamic_slice_in_dim(shift_image, first_image, own_images, 0)
    shift_tokens = jnp.repeat(shift_own, rows_local // own_images, axis=0)

    text_shift = first_image

    def roll_images(values, shift):
        if image_count == 1:
            return values
        shaped = values.reshape(image_count, -1, values.shape[-1])
        return jnp.roll(shaped, shift, axis=0).reshape(values.shape)

    text_len = text.shape[0] // image_count
    text_pad = 128 * ((text_len + 127) // 128)
    text_in = roll_images(text, -text_shift).reshape(image_count, text_len, -1)
    text_in = jnp.pad(text_in, ((0, 0), (0, text_pad - text_len), (0, 0))).reshape(image_count * text_pad, -1)
    pos_own = lax.dynamic_slice_in_dim(grid_pos, t_index * rows_local, rows_local, 0)
    pos_other = lax.dynamic_slice_in_dim(grid_pos, (1 - t_index) * rows_local, rows_local, 0)
    tables = rotary_columns(jnp.concatenate([pos_own, pos_other], axis=0))
    gains_column = head_gains[:, :, None]
    biases_column = head_biases[:, :, None]
    heads = local_width // HEAD_DIM

    def by_head(values, lead):
        return values.reshape(lead, heads, HEAD_DIM, values.shape[-1])

    joined = jnp.concatenate([hidden, skip_rows], axis=1).astype(F32)
    normed_skip = layer_norm(joined, sgain_f, sbias_f).astype(BF)
    stream_zero = plain_dot(normed_skip, skip_w) + rbias_f[6]
    first_in = with_other((layer_norm(stream_zero, ngain_f[0], rbias_f[0]) + shift_tokens).astype(BF))
    grad_ffn = with_other(cotangent)
    attention_gather.widen((first_in,))
    branch_gather.spread((attention_gather.low[0], attention_gather.low[1]))
    qk_w, vc_w = [attention_gather.finish(k, me).reshape(model_width, -1) for k in range(2)]
    v_w = vc_w[:, :local_width]
    query_w = vc_w[:, local_width:]
    qk_pre = by_head(turned_dot(qk_w, first_in) + col_bf[0:2].reshape(-1, 1), 2)
    v_pre = by_head(turned_dot(v_w, first_in) + col_bf[2].reshape(-1, 1), 1)
    branch_gather.widen((qk_pre, v_pre))
    up_shard = pin(up_weight.astype(BF), (attention_gather.low[1],))
    down_shard = pin(down_weight.astype(BF).T, (up_shard,))
    up_w = lax.all_gather(up_shard, "fsdp", axis=0, tiled=True)
    down_t = lax.all_gather(down_shard, "fsdp", axis=0, tiled=True)
    mixture, self_lse = attend(
        qk_pre,
        qk_pre,
        v_pre,
        (0, 1, 0),
        gains_column[0:2],
        biases_column[0:2],
        tables,
        SEQ,
        True,
        (branch_gather.low[0], branch_gather.low[1], down_shard),
    )
    proj_t, pair_w = [branch_gather.finish(k, me) for k in range(2)]
    proj_t = proj_t.reshape(model_width, -1)
    pair_w = pair_w.reshape(text_width, 2 * local_width)
    self_t = proj_t[:, :local_width]
    cross_t = proj_t[:, local_width:]
    mixture = mixture.reshape(local_width, -1)
    stream_one = stream_zero + turned_branch_sum(mixture, self_t, rows_local) + rbias_f[3]
    second_in = with_other(layer_norm(stream_one, ngain_f[1], rbias_f[1]).astype(BF))
    cross_pre = by_head(turned_dot(query_w, second_in) + col_bf[3].reshape(-1, 1), 1)
    pair_pre = by_head(turned_dot(pair_w, text_in) + col_bf[4:6].reshape(-1, 1), 2)
    cross_mixture, cross_lse = attend(
        cross_pre, pair_pre, pair_pre, (0, 0, 1), gains_column[2:4], biases_column[2:4], tables, text_len, False
    )
    cross_mixture = cross_mixture.reshape(local_width, -1)
    stream_two = stream_one + turned_branch_sum(cross_mixture, cross_t, rows_local) + rbias_f[4]
    third_in = with_other(layer_norm(stream_two, ngain_f[2], rbias_f[2]).astype(BF))
    hidden_act, slope = first_layer(third_in, up_w, up_bf)
    tile = 512 if ff_local % 512 == 0 else None
    down = Chain(products([(DOWN_ORDER, [(grad_ffn, hidden_act, False, 0, ff_local)])], me, tile=tile), DOWN_ORDER)

    grad_pre, upb_sums = first_layer_back(grad_ffn, down_t, slope, (down.high,))
    grad_upb = jnp.sum(upb_sums, axis=0)
    up = Chain(products([(UP_ORDER, [(third_in, grad_pre, False, 0, ff_local)])], me, tile=tile), UP_ORDER)
    third_part, third_got = branch_parts(grad_pre, up_w, rows_local)
    grad_two, low_two, sums_two = norm_back(third_part, third_got, stream_two, ngain_f[2], cotangent, 1, (up.high,))
    grad_cross = with_other(low_two)
    grad_cmix = lax.dot_general(cross_t, grad_cross, (((0,), (1,)), ((), ())), preferred_element_type=F32).astype(BF)
    grad_cq, grad_pair, cross_sums, cross_cols = attend_back(
        cross_pre,
        pair_pre,
        pair_pre,
        (0, 0, 1),
        by_head(grad_cmix, 1)[0],
        cross_lse,
        gains_column[2:4],
        biases_column[2:4],
        tables,
        text_len,
        False,
        False,
    )
    grad_cq = grad_cq.reshape(local_width, -1)
    grad_pair = grad_pair.reshape(2 * local_width, -1)
    second_part, second_got = turned_branch_parts(grad_cq, query_w, rows_local)
    down.step((grad_cq,))
    grad_one, low_one, sums_one = norm_back(
        second_part, second_got, stream_one, ngain_f[1], grad_two, 1, (down.high,)
    )
    grad_self = with_other(low_one)
    up.step((low_one,))
    halves = products(
        [
            ((1, 2), [(grad_cross, cross_mixture, True, 0, local_width), (second_in, grad_cq, True, 0, local_width)]),
            ((2, 1), [(text_in, grad_pair, True, 0, 2 * local_width)]),
        ],
        me,
        (up.high,),
    )
    cross_kept, cross_sent = halves[0::2], halves[1::2]
    down.step(cross_sent)
    cross_got = [hop(cross_sent[0], 1), hop(cross_sent[1], 2)]
    grad_mix = lax.dot_general(self_t, grad_self, (((0,), (1,)), ((), ())), preferred_element_type=F32).astype(BF)
    grad_qkv, self_sums, self_cols = attend_back(
        qk_pre,
        qk_pre,
        v_pre,
        (0, 1, 0),
        by_head(grad_mix, 1)[0],
        self_lse,
        gains_column[0:2],
        biases_column[0:2],
        tables,
        SEQ,
        True,
        True,
        (down.high,),
    )
    up.step((grad_qkv,))
    down.step((up.high,))
    cross_near = [add_near(v, g, (down.high,)) for v, g in zip(cross_kept, cross_got)]
    cross_got = [hop(cross_near[0][1], 2), hop(cross_near[1][1], 1)]
    grad_qkv = grad_qkv.reshape(3 * local_width, -1)
    halves = products(
        [
            ((1, 2), [(first_in, grad_qkv, True, 0, 2 * local_width)]),
            (
                (2, 1),
                [
                    (first_in, grad_qkv, True, 2 * local_width, local_width),
                    (grad_self, mixture, True, 0, local_width),
                ],
            ),
        ],
        me,
        (cross_near[0][1], cross_near[1][1]),
    )
    self_kept, self_sent = halves[0::2], halves[1::2]
    self_got = [hop(self_sent[0], 1), hop(self_sent[1], 2)]
    cross_far = FarSum([(v[0], g) for v, g in zip(cross_near, cross_got)], self_sent)
    grad_qk = grad_qkv[: 2 * local_width]
    grad_v = grad_qkv[2 * local_width :]
    first_part = turned_dot(grad_qk[:, rows_local:], qk_w) + turned_dot(grad_v[:, rows_local:], v_w)
    first_got = swap(first_part.astype(BF))
    first_part = turned_dot(grad_qk[:, :rows_local], qk_w) + turned_dot(grad_v[:, :rows_local], v_w)
    grad_zero, low_zero, sums_zero = norm_back(
        first_part, first_got, stream_zero, ngain_f[0], grad_one, own_images, (cross_far.high,)
    )
    skip_cut = model_width // 2
    skip_kept, skip_sent = products(
        [
            ((1, 2), [(normed_skip, low_zero, False, 0, skip_cut)]),
            ((2, 1), [(normed_skip, low_zero, False, skip_cut, skip_cut)]),
        ],
        me,
        paired=True,
    )
    skip_got = swap(skip_sent)
    self_near = [add_near(v, g, (skip_sent,)) for v, g in zip(self_kept, self_got)]
    self_got = [hop(self_near[0][1], 2), hop(self_near[1][1], 1)]
    skip_pair = [
        add_near(skip_kept, skip_got, (self_near[0][1], self_near[1][1]), part=k) for k in range(2)
    ]
    skip_got = [hop(skip_pair[0][1], 1), hop(skip_pair[1][1], 2)]
    up.step((skip_pair[0][1], skip_pair[1][1]))
    cross_far.step((up.high,))
    grad_normed = dot_last(low_zero, skip_w)
    input_grad, skip_grad, skip_sums = joined_back(grad_normed, hidden, skip_rows, sgain_f, (cross_far.high,))
    stream_three = stream_two + branch_sum(hidden_act, down_t, rows_local) + rbias_f[5]
    output = stream_three.astype(BF)
    text_half = text_width // 2
    pair_own = lax.dynamic_slice_in_dim(pair_w, t_index * text_half, text_half, 0)
    pair_other = lax.dynamic_slice_in_dim(pair_w, (1 - t_index) * text_half, text_half, 0)
    text_grad = turned_dot(grad_pair, pair_own) + swap(turned_dot(grad_pair, pair_other).astype(BF)).astype(F32)
    text_grad = text_grad.reshape(image_count, text_pad, -1)[:, :text_len].reshape(image_count * text_len, -1)
    text_grad = roll_images(text_grad, text_shift)

    shift_sums = jnp.sum(sums_zero[:, 1], axis=1)
    if image_count == 1:
        shift_local = shift_sums
    else:
        shift_local = lax.dynamic_update_slice_in_dim(
            jnp.zeros((image_count, model_width), F32), shift_sums, first_image, 0
        )
    shift_held = (shift_local + swap(shift_local))[None]
    shift_masks = [0]

    def shift_double(held, mask, after):
        held = pin(held, after)
        return jnp.concatenate([held, hop(held, mask)], axis=0), shift_masks + [m + mask for m in shift_masks]

    far_bits = [4 << b for b in range(30) if 4 << b < count]
    for mask in far_bits[:-1]:
        shift_held, shift_masks = shift_double(shift_held, mask, (skip_sent,))
    shift_held, shift_masks = shift_double(shift_held, far_bits[-1], (skip_pair[0][1],))
    sums_zero, sums_one, sums_two = (jnp.sum(v, axis=(0, 2)) for v in (sums_zero, sums_one, sums_two))
    skip_sums = jnp.sum(skip_sums, axis=1)
    grad_gains = jnp.stack([sums_zero[0], sums_one[0], sums_two[0]], axis=0)
    grad_biases = jnp.stack(
        [
            sums_zero[1],
            sums_one[1],
            sums_two[1],
            sums_one[2],
            sums_two[2],
            jnp.sum(cotangent.astype(F32), axis=0),
            sums_zero[2],
            sums_zero[1],
        ],
        axis=0,
    )
    self_columns = jnp.sum(self_cols, axis=(0, 4)).reshape(3, local_width)
    cross_columns = jnp.sum(cross_cols, axis=(0, 4)).reshape(3, local_width)
    grad_colb = jnp.concatenate([self_columns, cross_columns], axis=0)
    self_heads = jnp.sum(self_sums, axis=2)
    cross_heads = jnp.sum(cross_sums, axis=2)
    head_part = jnp.concatenate([self_heads[:2], cross_heads[:2], self_heads[2:], cross_heads[2:]]).reshape(-1)

    def by_device(values):
        shaped = values.reshape(values.shape[0], count, 2, -1).transpose(2, 1, 0, 3)
        return shaped.reshape(2, count, -1)

    def for_own(values):
        is_own = (jnp.arange(2) == t_index)[:, None, None]
        return jnp.where(is_own, values[None], 0.0)

    blocks = jnp.concatenate(
        [
            by_device(skip_sums[0:1]),
            by_device(skip_sums[1:2]),
            by_device(grad_gains),
            by_device(grad_biases),
            jnp.broadcast_to(head_part, (2, count, head_part.shape[0])),
            for_own(grad_colb.reshape(6, count, -1).transpose(1, 0, 2).reshape(count, -1)),
            for_own(grad_upb.reshape(count, -1)),
        ],
        axis=-1,
    )
    padded = 1024 * ((blocks.shape[-1] + 1023) // 1024)
    blocks = jnp.pad(blocks, ((0, 0), (0, 0), (0, padded - blocks.shape[-1])))
    blocks = blocks.transpose(1, 0, 2).reshape(2 * count, padded // 128, 128)
    small_kept, small_sent = halve([blocks], (1, 2), me, paired=True)
    small_pair = add_near(small_kept, swap(small_sent))
    small_got = hop(small_pair[1], 1)
    shift_held, shift_masks = shift_double(shift_held, 1, (small_pair[1],))

    skip_near = [add_near(v[0], g, (small_pair[1],)) for v, g in zip(skip_pair, skip_got)]
    skip_got = [hop(skip_near[0][1], 2), hop(skip_near[1][1], 1)]
    small_near = add_near(small_pair[0], small_got, (skip_near[0][1], skip_near[1][1]))
    small_got = hop(small_near[1], 2)
    self_far = FarSum([(v[0], g) for v, g in zip(self_near, self_got)], (small_near[1],))
    shift_held, shift_masks = shift_double(shift_held, 2, (self_far.high,))
    skip_far = FarSum([(v[0], g) for v, g in zip(skip_near, skip_got)], (self_far.high,))
    small_far = FarSum([(small_near[0], small_got)], (skip_far.high,))
    self_far.step((small_far.high,))
    skip_far.step((self_far.high,))
    small_far.step((skip_far.high,))
    cross_sum = cross_far.total()
    shift_all = order_from_masks(
        shift_held.reshape(count, image_count * model_width), np.array(shift_masks)
    ).reshape(count * image_count, model_width)
    sent_shift = lax.dot_general(
        activated_cut.astype(F32), shift_all, (((0,), (0,)), ((), ())), precision=PRECISE
    )
    self_sum = self_far.total()
    skip_sum = skip_far.total()
    small_sum = small_far.total().reshape(-1)
    sent_skip = jnp.concatenate([skip_sum[0, 0], skip_sum[1, 0]], axis=-1)
    sent_up, sent_down = up.total()[0], down.total()[0].T
    sent_cproj, sent_query = cross_sum[0, 0, :, :local_width], cross_sum[0, 0, :, local_width:]
    sent_pair = cross_sum[1, 0, : cross_kv.shape[0]].reshape(cross_kv.shape)
    sent_sproj = self_sum[1, 0, :, local_width:]
    lengths = [skip_gain.size, skip_bias.size, norm_gains.size, row_biases.size, head_gains.size, head_biases.size]
    lengths += [column_bias.size, up_bias.size]
    cuts = np.cumsum([0] + lengths)
    pieces = [small_sum[cuts[i] : cuts[i + 1]] for i in range(len(lengths))]

    sent_qkv = jnp.concatenate([self_sum[0, 0], self_sum[1, 0, :, :local_width]], axis=1).reshape(qkv_weight.shape)
    sent_proj = jnp.stack([sent_sproj.T, sent_cproj.T], axis=0)
    return (
        output,
        input_grad,
        skip_grad,
        text_grad,
        sent_skip,
        sent_shift,
        sent_qkv,
        sent_query,
        sent_pair,
        sent_proj,
        sent_up,
        sent_down,
        pieces[6].reshape(column_bias.shape),
        pieces[7].reshape(up_bias.shape),
        pieces[0],
        pieces[1],
        pieces[2].reshape(norm_gains.shape),
        pieces[3].reshape(row_biases.shape),
        pieces[4].reshape(head_gains.shape),
        pieces[5].reshape(head_biases.shape),
    )


def solution(mesh):
    in_specs = (
        P(("fsdp", "tp"), None),
        P(("fsdp", "tp"), None),
        P("fsdp", None),
        P("fsdp", None),
        P("fsdp", None),
        P(("fsdp", "tp"), None),
        P(("fsdp", "tp"), None),
        P(("fsdp", "tp"), None),
        P("fsdp", None, "tp"),
        P("fsdp", "tp"),
        P("fsdp", None, "tp"),
        P(None, "tp", "fsdp"),
        P("fsdp", "tp"),
        P("tp", "fsdp"),
        P(None, "tp", "fsdp"),
        P("tp", "fsdp"),
        P(("fsdp", "tp")),
        P(("fsdp", "tp")),
        P(None, ("fsdp", "tp")),
        P(None, ("fsdp", "tp")),
        P(),
        P(),
    )
    out_specs = (
        P(("fsdp", "tp"), None),
        P(("fsdp", "tp"), None),
        P(("fsdp", "tp"), None),
        P("fsdp", "tp"),
        P(("fsdp", "tp"), None),
        P(("fsdp", "tp"), None),
        P("fsdp", None, "tp"),
        P("fsdp", "tp"),
        P("fsdp", None, "tp"),
        P(None, "tp", "fsdp"),
        P("fsdp", "tp"),
        P("tp", "fsdp"),
        P(None, "tp", "fsdp"),
        P("tp", "fsdp"),
        P(("fsdp", "tp")),
        P(("fsdp", "tp")),
        P(None, ("fsdp", "tp")),
        P(None, ("fsdp", "tp")),
        P(),
        P(),
    )
    return jax.shard_map(body, mesh=mesh, in_specs=in_specs, out_specs=out_specs, check_vma=False)
```

time: 1630 us -> 1140 us (0.70)
  Pallas kernels: 104 us -> 416 us
  other arithmetic: 310 us -> 53.3 us
  matrix products: 366 us -> 145 us
  local copies, waits for them, and re-layouts: 248 us -> 85.3 us
  waiting for transfers between devices: 457 us -> 333 us
  starting transfers between devices: 108 us -> 80 us
    pallas_call x14 -> x66, Pallas kernels: 104 us -> 416 us  [the longest x5 82.4 us: products(): pl.pallas_call(kernel, grid_spec=pltpu.PrefetchScalarGridSpec(num_scalar_...]
    all_gather x7 -> x2, waiting for transfers between devices: 284 us -> 0.01 us  [the longest x1 0.01 us: body(): up_w = lax.all_gather(up_shard, 'fsdp', axis=0, tiled=True)]
    ppermute x69 -> x62, waiting for transfers between devices: 173 us -> 327 us  [hop(): return lax.ppermute(values, 'fsdp', [(i, i ^ mask) for i in range(count)])]
    dot_general x38 -> x18, matrix products: 197 us -> 83.1 us  [the longest x16 74.8 us: turned_dot(): lax.dot_general(first_operand, second_operand, (((0,), (1,)), ((), ())),...]
    convert_element_type x47 -> x4, other arithmetic: 102 us -> 5.93 us  [the longest x1 2.64 us: body(): normed_skip = layer_norm(joined, sgain_f, sbias_f).astype(BF)]
    reduce_sum x22 -> x11, other arithmetic: 79.3 us -> 5.5 us  [the longest x1 1.72 us: body(): jnp.sum(cotangent.astype(F32), axis=0)]
    dot_general x9 -> x2, matrix products: 81.2 us -> 9.4 us  [plain_dot(): return jnp.dot(first_operand, second_operand, preferred_element_type=F32)]
    reshape x20 -> x10, local copies, waits for them, and re-layouts: 76.7 us -> 14.2 us  [the longest x1 6.38 us: body(): pair_w = pair_w.reshape(text_width, 2 * local_width)]
  transfers between devices with their start and end apart: 95 -> 84, of which waited for: 36 -> 28; matrix products, arithmetic and copies ran while one was open for 40% -> 22% of each run, Pallas kernels for 6% -> 34%
where the time goes in v2:
time: 1140 us; the launch traced here: 1130 us
  Pallas kernels  416 us (36%)
  waiting for transfers between devices  333 us (29%)
  matrix products  145 us (13%)
  local copies, waits for them, and re-layouts  85.3 us (7%)
  starting transfers between devices  80 us (7%)
  other arithmetic  53.3 us (5%)
  between operations  16.4 us (1%)
    ppermute x62, waiting for transfers between devices, hop(): return lax.ppermute(values, 'fsdp', [(i, i ^ mask) for i in range(count)])  327 us
    pallas_call x5, Pallas kernels, products(): pl.pallas_call(kernel, grid_spec=pltpu.PrefetchScalarGridSpec(num_scalar_...  82.4 us
    ppermute x62, starting transfers between devices, hop(): return lax.ppermute(values, 'fsdp', [(i, i ^ mask) for i in range(count)])  76.4 us
    dot_general x16, matrix products, turned_dot(): lax.dot_general(first_operand, second_operand, (((0,), (1,)), ((), ())),...  74.8 us
    pallas_call x16, Pallas kernels, add_near(): pl.pallas_call(kernel, grid=(quarter, columns // tile), in_specs=[spec(0)...  73.9 us
    pallas_call x2, Pallas kernels, attend_back(): pl.pallas_call(functools.partial(attend_back_kernel, valid, turned, joint...  60.3 us
    dot_general x5, matrix products, dot_last(): lax.dot_general(first_operand, second_operand, (((1,), (1,)), ((), ())),...  50.5 us
    pallas_call x2, Pallas kernels, attend(): pl.pallas_call(functools.partial(attend_kernel, valid, turned, len(after)...  43.6 us
  transfers between devices with their start and end apart: 84, of which 28 were waited for; matrix products, arithmetic and copies ran while one was open for 22% of the time, Pallas kernels for 34%

profile of v2, /device:TPU:0, one launch (start us, length us, event | category | flops | bytes accessed | tf_op | source)
XLA Modules:
  0.0 1129.1 jit_solution(9530781426108520240)
XLA Ops:
  96.8 13.5 %collective-permute-done.10.refs_1_ = bf16[8,88,768]{2,1,0:T(8,128)(2,1)} collective-permute-done((bf16[8,88,768]{2,1,0:T(8,128)(2,1)}, bf16[8,88,768]{2,1,0:T(8,128)(2,1)}, u32[]{:S(2)}, u32[]{:S(2)}) %collective-permute-start.10) | collective-permute-done | bytes 1081376 | tf_op jit(solution)/shard_map/ppermute | solution.py:25
  158.3 18.3 %collective-permute-done.25.second_ref = bf16[4,88,1408]{2,1,0:T(8,128)(2,1)S(1)} collective-permute-done((bf16[4,88,1408]{2,1,0:T(8,128)(2,1)}, bf16[4,88,1408]{2,1,0:T(8,128)(2,1)S(1)}, u32[]{:S(2)}, u32[]{:S(2)}) %collective-permute-start.25) | collective-permute-done | bytes 991264 | tf_op jit(solution)/shard_map/ppermute | solution.py:25
  185.8 25.4 %collective-permute-done.16.second_ref = bf16[4,88,1408]{2,1,0:T(8,128)(2,1)S(1)} collective-permute-done((bf16[4,88,1408]{2,1,0:T(8,128)(2,1)S(1)}, bf16[4,88,1408]{2,1,0:T(8,128)(2,1)S(1)}, u32[]{:S(2)}, u32[]{:S(2)}) %collective-permute-start.16) | collective-permute-done | bytes 991264 | tf_op jit(solution)/shard_map/ppermute | solution.py:25
  220.3 32.2 %collective-permute-done.28.refs_1_ = bf16[2,88,2432]{2,1,0:T(8,128)(2,1)} collective-permute-done((bf16[2,88,2432]{2,1,0:T(8,128)(2,1)}, bf16[2,88,2432]{2,1,0:T(8,128)(2,1)}, u32[]{:S(2)}, u32[]{:S(2)}) %collective-permute-start.28) | collective-permute-done | bytes 856096 | tf_op jit(solution)/shard_map/ppermute | solution.py:25
  258.4 10.9 collective-permute-done.26.refs_1_
  293.4 14.2 %collective-permute-done.29.second_ref = bf16[4,88,1408]{2,1,0:T(8,128)(2,1)S(1)} collective-permute-done((bf16[4,88,1408]{2,1,0:T(8,128)(2,1)}, bf16[4,88,1408]{2,1,0:T(8,128)(2,1)S(1)}, u32[]{:S(2)}, u32[]{:S(2)}) %collective-permute-start.29) | collective-permute-done | bytes 991264 | tf_op jit(solution)/shard_map/ppermute | solution.py:25
  317.7 45.6 %collective-permute-done.30.second_ref = bf16[4,88,1024]{2,1,0:T(8,128)(2,1)} collective-permute-done((bf16[4,88,1024]{2,1,0:T(8,128)(2,1)}, bf16[4,88,1024]{2,1,0:T(8,128)(2,1)}, u32[]{:S(2)}, u32[]{:S(2)}) %collective-permute-start.30) | collective-permute-done | bytes 720928 | tf_op jit(solution)/shard_map/ppermute | solution.py:25
  365.5 27.7 %shard_map.412 = (bf16[8,88,1024]{2,1,0:T(8,128)(2,1)}, f32[8,1,1024]{2,1,0:T(1,128)}) custom-call(f32[2,8,88,1024]{3,2,1,0:T(8,128)} %bitcast.143, f32[2,8,88,1024]{3,2,1,0:T(8,128)} %bitcast.144, f32[1,8,88,1024]{3,2,1,0:T(8,128)} %bitcast.149, f32[2,88,1]{2,1,0:T(8,128)} %copy.85.gain_ref, f32[2,88,1]{2,1,0:T(8,128)} %copy.86.bias_ref, ...), custom_call_target="tpu_custom_call" | custom-call | flops 4294967296 | bytes 17301504 | tf_op jit(solution)/shard_map/pallas_call | solution.py:878
  414.7 50.3 %collective-permute-done.34.refs_1_ = bf16[8,88,1024]{2,1,0:T(8,128)(2,1)} collective-permute-done((bf16[8,88,1024]{2,1,0:T(8,128)(2,1)}, bf16[8,88,1024]{2,1,0:T(8,128)(2,1)}, u32[]{:S(2)}, u32[]{:S(2)}) %collective-permute-start.34) | collective-permute-done | bytes 1441824 | tf_op jit(solution)/shard_map/ppermute | solution.py:25
  485.4 15.9 %shard_map.415 = (bf16[8,88,1024]{2,1,0:T(8,128)(2,1)}, f32[8,1,1024]{2,1,0:T(1,128)}) custom-call(f32[1,8,88,1024]{3,2,1,0:T(8,128)} %bitcast.180, f32[2,8,88,384]{3,2,1,0:T(8,128)} %bitcast.154, f32[2,8,88,384]{3,2,1,0:T(8,128)} %bitcast.155, f32[2,88,1]{2,1,0:T(8,128)} %copy.89.gain_ref, f32[2,88,1]{2,1,0:T(8,128)} %copy.90.bias_ref, ...), custom_call_target="tpu_custom_call" | custom-call | flops 1610612736 | bytes 8650752 | tf_op jit(solution)/shard_map/pallas_call | solution.py:878
  524.9 20.4 %shard_map.416 = (bf16[1024,3072]{1,0:T(8,128)(2,1)}, bf16[1024,3072]{1,0:T(8,128)(2,1)}) custom-call(bf16[1024,1408]{1,0:T(8,128)(2,1)} %pad_maximum_fusion.3.rows_ref.refs_0_, bf16[1408,3072]{1,0:T(8,128)(2,1)} %all-gather.3.cloned.1.call-done.weight_ref, f32[1,3072]{1,0:T(1,128)} %reshape_reshape.4.bias_ref), custom_call_target="tpu_custom_call" | custom-call | flops 8858370048 | bytes 21233664 | tf_op jit(solution)/shard_map/pallas_call | solution.py:742
  545.3 16.7 %shard_map.417 = (bf16[8,1,88,3072]{3,2,1,0:T(8,128)(2,1)}, bf16[8,1,88,3072]{3,2,1,0:T(8,128)(2,1)}) custom-call(s32[3]{0:T(128)} %pad_add_fusion.me_ref, bf16[1024,1408]{1,0:T(8,128)(2,1)} %constant_dynamic-update-slice_fusion.refs_0_.grad_ref, bf16[1024,3072]{1,0:T(8,128)(2,1)} %get-tuple-element.126.refs_1_), custom_call_target="tpu_custom_call" | custom-call | flops 8858370048 | bytes 17825792 | tf_op jit(solution)/shard_map/pallas_call | solution.py:419
  563.4 15.6 %shard_map.418 = (bf16[1024,3072]{1,0:T(8,128)(2,1)}, f32[8,3072]{1,0:T(8,128)}) custom-call(bf16[1024,1408]{1,0:T(8,128)(2,1)} %constant_dynamic-update-slice_fusion.refs_0_.grad_ref, bf16[1408,3072]{1,0:T(8,128)(2,1)} %all-gather.5.cloned.1.call-done.weight_ref, bf16[1024,3072]{1,0:T(8,128)(2,1)} %get-tuple-element.127.slope_ref, ...), custom_call_target="tpu_custom_call" | custom-call | flops 8858370048 | bytes 21233664 | tf_op jit(solution)/shard_map/pallas_call | solution.py:781
  578.9 16.7 %shard_map.419 = (bf16[8,1,88,3072]{3,2,1,0:T(8,128)(2,1)}, bf16[8,1,88,3072]{3,2,1,0:T(8,128)(2,1)}) custom-call(s32[3]{0:T(128)} %pad_add_fusion.me_ref, bf16[1024,1408]{1,0:T(8,128)(2,1)} %pad_maximum_fusion.3.rows_ref.refs_0_, bf16[1024,3072]{1,0:T(8,128)(2,1)} %get-tuple-element.129.refs_1_), custom_call_target="tpu_custom_call" | custom-call | flops 8858370048 | bytes 17825792 | tf_op jit(solution)/shard_map/pallas_call | solution.py:419
  623.1 10.6 fusion.20
  640.4 21.2 %shard_map.421 = (bf16[1,8,88,1024]{3,2,1,0:T(8,128)(2,1)}, bf16[2,8,88,384]{3,2,1,0:T(8,128)(2,1)}, f32[4,88,128]{2,1,0:T(8,128)}, f32[1,3,8,88,128]{4,3,2,1,0:T(8,128)}) custom-call(f32[1,8,88,1024]{3,2,1,0:T(8,128)} %bitcast.181, f32[2,8,88,384]{3,2,1,0:T(8,128)} %bitcast.156, f32[2,8,88,384]{3,2,1,0:T(8,128)} %bitcast.157, ...), custom_call_target="tpu_custom_call" | custom-call | flops 4026531840 | bytes 14417920 | tf_op jit(solution)/shard_map/pallas_call | solution.py:971
  726.8 15.4 %shard_map.425 = (bf16[8,1,88,1408]{3,2,1,0:T(8,128)(2,1)}, bf16[8,1,88,1408]{3,2,1,0:T(8,128)(2,1)}, bf16[8,1,64,1408]{3,2,1,0:T(8,128)(2,1)}, bf16[8,1,64,1408]{3,2,1,0:T(8,128)(2,1)}) custom-call(s32[3]{0:T(128)} %pad_add_fusion.me_ref, bf16[1024,1408]{1,0:T(8,128)(2,1)} %copy-done.58, bf16[1024,1408]{1,0:T(8,128)(2,1)} %pad_maximum_fusion.2.refs_1_, ...), custom_call_target="tpu_custom_call" | custom-call | flops 7012876288 | bytes 17367040 | tf_op jit(solution)/shard_map/pallas_call | solution.py:419
  757.4 39.1 %shard_map.427 = (bf16[3,8,88,1024]{3,2,1,0:T(8,128)(2,1)}, f32[4,88,128]{2,1,0:T(8,128)}, f32[1,3,8,88,128]{4,3,2,1,0:T(8,128)}) custom-call(f32[2,8,88,1024]{3,2,1,0:T(8,128)} %bitcast.145, f32[2,8,88,1024]{3,2,1,0:T(8,128)} %bitcast.146, f32[1,8,88,1024]{3,2,1,0:T(8,128)} %bitcast.150, bf16[8,88,1024]{2,1,0:T(8,128)(2,1)} %bitcast.210, ...), custom_call_target="tpu_custom_call" | custom-call | flops 10737418240 | bytes 28835840 | tf_op jit(solution)/shard_map/pallas_call | solution.py:971
  837.6 19.1 %shard_map.432 = (bf16[8,1,88,1408]{3,2,1,0:T(8,128)(2,1)}, bf16[8,1,88,1408]{3,2,1,0:T(8,128)(2,1)}, bf16[8,1,88,1408]{3,2,1,0:T(8,128)(2,1)}, bf16[8,1,88,1408]{3,2,1,0:T(8,128)(2,1)}) custom-call(s32[3]{0:T(128)} %pad_add_fusion.me_ref, bf16[1024,1408]{1,0:T(8,128)(2,1)} %pad_maximum_fusion.1.refs_0_, bf16[1024,1408]{1,0:T(8,128)(2,1)} %copy-done.59, ...), custom_call_target="tpu_custom_call" | custom-call | flops 8120172544 | bytes 19464192 | tf_op jit(solution)/shard_map/pallas_call | solution.py:419
  868.6 14.6 %shard_map.435 = (bf16[2,16,1,88,704]{4,3,2,1,0:T(8,128)(2,1)}, bf16[2,16,1,88,704]{4,3,2,1,0:T(8,128)(2,1)}) custom-call(s32[3]{0:T(128)} %pad_add_fusion.me_ref, bf16[512,2816]{1,0:T(8,128)(2,1)} %fusion.5.refs_0_, bf16[512,1408]{1,0:T(8,128)(2,1)} %get-tuple-element.161.refs_1_), custom_call_target="tpu_custom_call" | custom-call | flops 4060086272 | bytes 12255232 | tf_op jit(solution)/shard_map/pallas_call | solution.py:419
  893.6 17.8 %collective-permute-done.72 = f32[1,1,1408]{2,1,0:T(1,128)S(1)} collective-permute-done((f32[1,1,1408]{2,1,0:T(1,128)}, f32[1,1,1408]{2,1,0:T(1,128)S(1)}, u32[]{:S(2)}, u32[]{:S(2)}) %collective-permute-start.72) | collective-permute-done | bytes 5664 | tf_op jit(solution)/shard_map/ppermute | solution.py:25
  912.1 10.8 fusion.105.grad_ref
  1020.3 11.1 collective-permute-done.77
  1092.3 17.1 %collective-permute-done.70 = bf16[2,1,1,88,704]{4,3,2,1,0:T(8,128)(2,1)S(1)} collective-permute-done((bf16[2,1,1,88,704]{4,3,2,1,0:T(8,128)(2,1)}, bf16[2,1,1,88,704]{4,3,2,1,0:T(8,128)(2,1)S(1)}, u32[]{:S(2)}, u32[]{:S(2)}) %collective-permute-start.70) | collective-permute-done | bytes 247840 | tf_op jit(solution)/shard_map/ppermute | solution.py:25
  (674 shorter events, 612.5 us)
Async XLA Ops:
  7.2 517.7 %all-gather.3.cloned.1.call-start = ((), (), s32[]{:S(2)}) async-start(), calls=%async_computation | async-start | bytes 9191424 | tf_op jit(solution)/shard_map/all_gather | solution.py:1170
  182.2 381.2 %all-gather.5.cloned.1.call-start = ((), (), s32[]{:S(2)}) async-start(), calls=%async_computation.1 | async-start | bytes 9191424 | tf_op jit(solution)/shard_map/all_gather | solution.py:1171
  184.0 85.2 %collective-permute-start.26 = (bf16[8,88,1408]{2,1,0:T(8,128)(2,1)S(1)}, bf16[8,88,1408]{2,1,0:T(8,128)(2,1)}, u32[]{:S(2)}, u32[]{:S(2)}) collective-permute-start(bf16[8,88,1408]{2,1,0:T(8,128)(2,1)S(1)} %copy-done.1), channel_id=1, source_target_pairs={{0,2},{2,0},{4,6},{6,4},{8,10},{10,8},{12,14},{14,12},{16,18},{18,... | collective-permute-start | bytes 5947400 | tf_op jit(solution)/shard_map/ppermute | solution.py:25
  214.7 64.8 %collective-permute-start.24 = (bf16[8,88,1408]{2,1,0:T(8,128)(2,1)}, bf16[8,88,1408]{2,1,0:T(8,128)(2,1)}, u32[]{:S(2)}, u32[]{:S(2)}) collective-permute-start(bf16[8,88,1408]{2,1,0:T(8,128)(2,1)} %shard_map.402.refs_0_.refs_2_), channel_id=1, source_target_pairs={{0,4},{2,6},{4,0},{6,2},{8,12},{10,14},{12,8},{14,10},{16,20},{18,... | collective-permute-start | bytes 5947400 | tf_op jit(solution)/shard_map/ppermute | solution.py:25
  254.8 52.8 %collective-permute-start.29 = (bf16[4,88,1408]{2,1,0:T(8,128)(2,1)}, bf16[4,88,1408]{2,1,0:T(8,128)(2,1)S(1)}, u32[]{:S(2)}, u32[]{:S(2)}) collective-permute-start(bf16[4,88,1408]{2,1,0:T(8,128)(2,1)} %get-tuple-element.122.first_ref), channel_id=1, source_target_pairs={{0,2},{2,0},{4,6},{6,4},{8,10},{10,8},{12,14},{14,12},{16,18},{18,... | collective-permute-start | bytes 2973704 | tf_op jit(solution)/shard_map/ppermute | solution.py:25
  311.1 82.1 %collective-permute-start.31 = (bf16[8,88,1408]{2,1,0:T(8,128)(2,1)}, bf16[8,88,1408]{2,1,0:T(8,128)(2,1)S(1)}, u32[]{:S(2)}, u32[]{:S(2)}) collective-permute-start(bf16[8,88,1408]{2,1,0:T(8,128)(2,1)} %shard_map.408.refs_0_), channel_id=1, source_target_pairs={{0,4},{2,6},{4,0},{6,2},{8,12},{10,14},{12,8},{14,10},{16,20},{18,... | collective-permute-start | bytes 5947400 | tf_op jit(solution)/shard_map/ppermute | solution.py:25
  311.4 51.9 %collective-permute-start.30 = (bf16[4,88,1024]{2,1,0:T(8,128)(2,1)}, bf16[4,88,1024]{2,1,0:T(8,128)(2,1)}, u32[]{:S(2)}, u32[]{:S(2)}) collective-permute-start(bf16[4,88,1024]{2,1,0:T(8,128)(2,1)} %get-tuple-element.123.first_ref), channel_id=1, source_target_pairs={{0,4},{2,6},{4,0},{6,2},{8,12},{10,14},{12,8},{14,10},{16,20},{18,... | collective-permute-start | bytes 2162696 | tf_op jit(solution)/shard_map/ppermute | solution.py:25
  403.6 61.4 %collective-permute-start.34 = (bf16[8,88,1024]{2,1,0:T(8,128)(2,1)}, bf16[8,88,1024]{2,1,0:T(8,128)(2,1)}, u32[]{:S(2)}, u32[]{:S(2)}) collective-permute-start(bf16[8,88,1024]{2,1,0:T(8,128)(2,1)} %shard_map.409.refs_1_.refs_0_), channel_id=1, source_target_pairs={{0,2},{2,0},{4,6},{6,4},{8,10},{10,8},{12,14},{14,12},{16,18},{18,... | collective-permute-start | bytes 4325384 | tf_op jit(solution)/shard_map/ppermute | solution.py:25
  412.5 68.0 %collective-permute-start.33 = (bf16[512,1408]{1,0:T(8,128)(2,1)S(1)}, bf16[512,1408]{1,0:T(8,128)(2,1)S(1)}, u32[]{:S(2)}, u32[]{:S(2)}) collective-permute-start(bf16[512,1408]{1,0:T(8,128)(2,1)S(1)} %add_convert_fusion.1), channel_id=1, source_target_pairs={{0,1},{1,0},{2,3},{3,2},{4,5},{5,4},{6,7},{7,6},{8,9},{9,8},{10,11... | collective-permute-start | bytes 4325384 | tf_op jit(solution)/shard_map/ppermute | solution.py:29
  562.0 123.1 %collective-permute-start.42 = (bf16[8,1,88,3072]{3,2,1,0:T(8,128)(2,1)}, bf16[8,1,88,3072]{3,2,1,0:T(8,128)(2,1)}, u32[]{:S(2)}, u32[]{:S(2)}) collective-permute-start(bf16[8,1,88,3072]{3,2,1,0:T(8,128)(2,1)} %get-tuple-element.128.refs_0_), channel_id=1, source_target_pairs={{0,8},{2,10},{4,12},{6,14},{8,0},{10,2},{12,4},{14,6},{16,24},{18,... | collective-permute-start | bytes 12976136 | tf_op jit(solution)/shard_map/ppermute | solution.py:25
  605.2 113.3 %collective-permute-start.45 = (bf16[8,1,88,3072]{3,2,1,0:T(8,128)(2,1)}, bf16[8,1,88,3072]{3,2,1,0:T(8,128)(2,1)}, u32[]{:S(2)}, u32[]{:S(2)}) collective-permute-start(bf16[8,1,88,3072]{3,2,1,0:T(8,128)(2,1)} %get-tuple-element.130.refs_0_), channel_id=1, source_target_pairs={{0,2},{2,0},{4,6},{6,4},{8,10},{10,8},{12,14},{14,12},{16,18},{18,... | collective-permute-start | bytes 12976136 | tf_op jit(solution)/shard_map/ppermute | solution.py:25
  633.8 69.1 %collective-permute-start.37 = (bf16[512,1408]{1,0:T(8,128)(2,1)}, bf16[512,1408]{1,0:T(8,128)(2,1)}, u32[]{:S(2)}, u32[]{:S(2)}) collective-permute-start(bf16[512,1408]{1,0:T(8,128)(2,1)} %fusion.20), channel_id=1, source_target_pairs={{0,1},{1,0},{2,3},{3,2},{4,5},{5,4},{6,7},{7,6},{8,9},{9,8},{10,11... | collective-permute-start | bytes 4325384 | tf_op jit(solution)/shard_map/ppermute | solution.py:29
  692.7 59.5 %collective-permute-start.44 = (bf16[4,1,88,3072]{3,2,1,0:T(8,128)(2,1)}, bf16[4,1,88,3072]{3,2,1,0:T(8,128)(2,1)}, u32[]{:S(2)}, u32[]{:S(2)}) collective-permute-start(bf16[4,1,88,3072]{3,2,1,0:T(8,128)(2,1)} %get-tuple-element.136.refs_0_), channel_id=1, source_target_pairs={{0,4},{2,6},{4,0},{6,2},{8,12},{10,14},{12,8},{14,10},{16,20},{18,... | collective-permute-start | bytes 6488072 | tf_op jit(solution)/shard_map/ppermute | solution.py:25
  726.2 85.3 %collective-permute-start.49 = (bf16[4,1,88,3072]{3,2,1,0:T(8,128)(2,1)}, bf16[4,1,88,3072]{3,2,1,0:T(8,128)(2,1)S(1)}, u32[]{:S(2)}, u32[]{:S(2)}) collective-permute-start(bf16[4,1,88,3072]{3,2,1,0:T(8,128)(2,1)} %get-tuple-element.142.refs_6_), channel_id=1, source_target_pairs={{0,4},{2,6},{4,0},{6,2},{8,12},{10,14},{12,8},{14,10},{16,20},{18,... | collective-permute-start | bytes 6488072 | tf_op jit(solution)/shard_map/ppermute | solution.py:25
  742.2 78.4 %collective-permute-start.47 = (bf16[8,1,88,1408]{3,2,1,0:T(8,128)(2,1)}, bf16[8,1,88,1408]{3,2,1,0:T(8,128)(2,1)}, u32[]{:S(2)}, u32[]{:S(2)}) collective-permute-start(bf16[8,1,88,1408]{3,2,1,0:T(8,128)(2,1)} %get-tuple-element.143.refs_0_), channel_id=1, source_target_pairs={{0,2},{2,0},{4,6},{6,4},{8,10},{10,8},{12,14},{14,12},{16,18},{18,... | collective-permute-start | bytes 5947400 | tf_op jit(solution)/shard_map/ppermute | solution.py:25
  743.7 88.3 %collective-permute-start.51 = (bf16[8,1,64,1408]{3,2,1,0:T(8,128)(2,1)}, bf16[8,1,64,1408]{3,2,1,0:T(8,128)(2,1)}, u32[]{:S(2)}, u32[]{:S(2)}) collective-permute-start(bf16[8,1,64,1408]{3,2,1,0:T(8,128)(2,1)} %get-tuple-element.144.refs_1_), channel_id=1, source_target_pairs={{0,4},{2,6},{4,0},{6,2},{8,12},{10,14},{12,8},{14,10},{16,20},{18,... | collective-permute-start | bytes 4325384 | tf_op jit(solution)/shard_map/ppermute | solution.py:25
  756.9 60.3 %collective-permute-start.48 = (bf16[2,1,88,3072]{3,2,1,0:T(8,128)(2,1)}, bf16[2,1,88,3072]{3,2,1,0:T(8,128)(2,1)S(1)}, u32[]{:S(2)}, u32[]{:S(2)}) collective-permute-start(bf16[2,1,88,3072]{3,2,1,0:T(8,128)(2,1)} %get-tuple-element.145.rest_0_), channel_id=1, source_target_pairs={{0,2},{2,0},{4,6},{6,4},{8,10},{10,8},{12,14},{14,12},{16,18},{18,... | collective-permute-start | bytes 3244040 | tf_op jit(solution)/shard_map/ppermute | solution.py:25
  808.3 52.9 %collective-permute-start.46 = (bf16[512,1408]{1,0:T(8,128)(2,1)}, bf16[512,1408]{1,0:T(8,128)(2,1)}, u32[]{:S(2)}, u32[]{:S(2)}) collective-permute-start(bf16[512,1408]{1,0:T(8,128)(2,1)} %fusion.19), channel_id=1, source_target_pairs={{0,1},{1,0},{2,3},{3,2},{4,5},{5,4},{6,7},{7,6},{8,9},{9,8},{10,11... | collective-permute-start | bytes 4325384 | tf_op jit(solution)/shard_map/ppermute | solution.py:29
  883.2 60.3 %collective-permute-start.55 = (bf16[2,16,1,88,704]{4,3,2,1,0:T(8,128)(2,1)}, bf16[2,16,1,88,704]{4,3,2,1,0:T(8,128)(2,1)}, u32[]{:S(2)}, u32[]{:S(2)}) collective-permute-start(bf16[2,16,1,88,704]{4,3,2,1,0:T(8,128)(2,1)} %get-tuple-element.165.refs_0_), channel_id=1, source_target_pairs={{0,1},{1,0},{2,3},{3,2},{4,5},{5,4},{6,7},{7,6},{8,9},{9,8},{10,11... | collective-permute-start | bytes 11894792 | tf_op jit(solution)/shard_map/ppermute | solution.py:29
  884.8 73.1 %collective-permute-start.54 = (bf16[2,1,88,3072]{3,2,1,0:T(8,128)(2,1)}, bf16[2,1,88,3072]{3,2,1,0:T(8,128)(2,1)S(1)}, u32[]{:S(2)}, u32[]{:S(2)}) collective-permute-start(bf16[2,1,88,3072]{3,2,1,0:T(8,128)(2,1)} %get-tuple-element.151.refs_0_), channel_id=1, source_target_pairs={{0,8},{2,10},{4,12},{6,14},{8,0},{10,2},{12,4},{14,6},{16,24},{18,... | collective-permute-start | bytes 3244040 | tf_op jit(solution)/shard_map/ppermute | solution.py:25
  885.7 52.2 %collective-permute-start.57 = (bf16[8,1,88,1408]{3,2,1,0:T(8,128)(2,1)}, bf16[8,1,88,1408]{3,2,1,0:T(8,128)(2,1)S(1)}, u32[]{:S(2)}, u32[]{:S(2)}) collective-permute-start(bf16[8,1,88,1408]{3,2,1,0:T(8,128)(2,1)} %get-tuple-element.159.refs_5_), channel_id=1, source_target_pairs={{0,4},{2,6},{4,0},{6,2},{8,12},{10,14},{12,8},{14,10},{16,20},{18,... | collective-permute-start | bytes 5947400 | tf_op jit(solution)/shard_map/ppermute | solution.py:25
  911.4 49.8 %collective-permute-start.53 = (bf16[2,2,1,88,1408]{4,3,2,1,0:T(8,128)(2,1)}, bf16[2,2,1,88,1408]{4,3,2,1,0:T(8,128)(2,1)S(1)}, u32[]{:S(2)}, u32[]{:S(2)}) collective-permute-start(bf16[2,2,1,88,1408]{4,3,2,1,0:T(8,128)(2,1)} %get-tuple-element.160.refs_0_), channel_id=1, source_target_pairs={{0,8},{2,10},{4,12},{6,14},{8,0},{10,2},{12,4},{14,6},{16,24},{18,... | collective-permute-start | bytes 2973704 | tf_op jit(solution)/shard_map/ppermute | solution.py:25
  931.1 62.9 %collective-permute-start.79 = (bf16[1,1,88,3072]{3,2,1,0:T(8,128)(2,1)}, bf16[1,1,88,3072]{3,2,1,0:T(8,128)(2,1)}, u32[]{:S(2)}, u32[]{:S(2)}) collective-permute-start(bf16[1,1,88,3072]{3,2,1,0:T(8,128)(2,1)} %get-tuple-element.152.refs_0_), channel_id=1, source_target_pairs={{0,16},{2,18},{4,20},{6,22},{8,24},{10,26},{12,28},{14,30},{16,0},... | collective-permute-start | bytes 1622024 | tf_op jit(solution)/shard_map/ppermute | solution.py:25
  949.7 49.5 %collective-permute-start.59 = (bf16[8,1,88,704]{3,2,1,0:T(8,128)(2,1)}, bf16[8,1,88,704]{3,2,1,0:T(8,128)(2,1)}, u32[]{:S(2)}, u32[]{:S(2)}) collective-permute-start(bf16[8,1,88,704]{3,2,1,0:T(8,128)(2,1)} %get-tuple-element.170.refs_0_), channel_id=1, source_target_pairs={{0,2},{2,0},{4,6},{6,4},{8,10},{10,8},{12,14},{14,12},{16,18},{18,... | collective-permute-start | bytes 2973704 | tf_op jit(solution)/shard_map/ppermute | solution.py:25
  (161 other events, 2149.9 us)
Sparse Core Ops, SparseCore 0:
  182.3 152.7 all-gather.2
  337.9 143.6 all-gather.4

commit v3 on v2

--- a/solution.py
+++ b/solution.py
@@ -16,7 +16,7 @@
 F32 = jnp.float32
 LOG2E = 1.4426950408889634
 UP_ORDER = (1, 2)
-DOWN_ORDER = (4, 2, 1)
+DOWN_ORDER = (4, 1, 2)
 VMEM_LIMIT = 56 * 1024 * 1024
 
 
@@ -71,6 +71,24 @@
 ANYWHERE = pl.BlockSpec(memory_space=pl.ANY)
 
 
+def light(**work):
+    return pl.CostEstimate(flops=1, bytes_accessed=1, transcendentals=0)
+
+
+class Order:
+    last = ()
+
+
+def in_order(call):
+    @functools.wraps(call)
+    def ordered(*args, after=(), **kwargs):
+        result = call(*args, after=tuple(after) + Order.last, **kwargs)
+        Order.last = (result[0] if isinstance(result, (tuple, list)) else result,)
+        return result
+
+    return ordered
+
+
 def steps_of(order, count):
     return tuple(order) + tuple(1 << b for b in range(30) if 1 << b < count and 1 << b not in order)
 
@@ -85,6 +103,7 @@
     return sum(((mask >> (bit.bit_length() - 1)) & 1) << (top - k) for k, bit in enumerate(order))
 
 
+@in_order
 def halve(arrays, order, me, after=(), paired=False):
     count = arrays[0].shape[0] // (2 if paired else 1)
     rows, columns = arrays[0].shape[1:]
@@ -135,11 +154,12 @@
         ),
         out_shape=[shape, shape],
         compiler_params=pltpu.CompilerParams(vmem_limit_bytes=VMEM_LIMIT),
-        cost_estimate=pl.CostEstimate(flops=0, bytes_accessed=4 * moved, transcendentals=0),
+        cost_estimate=light(flops=0, bytes_accessed=4 * moved, transcendentals=0),
     )(me, *arrays, *after)
 
 
-def pin(values, after):
+@in_order
+def pin(values, after=()):
     def kernel(in_ref, *refs):
         refs[-1][...] = in_ref[...]
 
@@ -149,7 +169,7 @@
         in_specs=[whole] + [ANYWHERE] * len(after),
         out_specs=whole,
         out_shape=jax.ShapeDtypeStruct(values.shape, values.dtype),
-        cost_estimate=pl.CostEstimate(flops=0, bytes_accessed=4 * values.size, transcendentals=0),
+        cost_estimate=light(flops=0, bytes_accessed=4 * values.size, transcendentals=0),
     )(values, *after)
 
 
@@ -157,10 +177,12 @@
     return columns // 4 if columns % 512 == 0 else columns // 2 if columns % 256 == 0 else columns
 
 
+@in_order
 def add_near(kept, received, after=(), part=None):
     doubled, many, rows, columns = kept.shape[-4:]
     quarter = doubled // 2
     tile = columns // 2 if columns % 256 == 0 else columns
+    group = max(quarter // 2, 1)
 
     def kernel(kept_low, kept_high, got_low, got_high, *refs):
         low, high = refs[len(after) :]
@@ -168,7 +190,7 @@
             total = first[...].astype(F32) + second[...].astype(F32)
             out[...] = total.reshape(out.shape).astype(kept.dtype)
 
-    block = (1, many, rows, tile)
+    block = (group, many, rows, tile)
 
     def spec(shift):
         if part is None:
@@ -180,15 +202,16 @@
     size = doubled * many * rows * columns
     return pl.pallas_call(
         kernel,
-        grid=(quarter, columns // tile),
-        in_specs=[spec(0), spec(quarter), spec(0), spec(quarter)] + [ANYWHERE] * len(after),
+        grid=(quarter // group, columns // tile),
+        in_specs=[spec(0), spec(quarter // group), spec(0), spec(quarter // group)] + [ANYWHERE] * len(after),
         out_specs=[out_spec] * 2,
         out_shape=[shape, shape],
         compiler_params=pltpu.CompilerParams(vmem_limit_bytes=VMEM_LIMIT),
-        cost_estimate=pl.CostEstimate(flops=size, bytes_accessed=6 * size, transcendentals=0),
+        cost_estimate=light(flops=size, bytes_accessed=6 * size, transcendentals=0),
     )(kept, kept, received, received, *after)
 
 
+@in_order
 def add_far(pairs, after=()):
     quarter, many, _, columns = pairs[0][0].shape
     heights = [pair[0].shape[2] for pair in pairs]
@@ -221,10 +244,11 @@
         out_specs=[out_spec] * 2,
         out_shape=[jax.ShapeDtypeStruct(shape, kind)] * 2,
         compiler_params=pltpu.CompilerParams(vmem_limit_bytes=VMEM_LIMIT),
-        cost_estimate=pl.CostEstimate(flops=size, bytes_accessed=6 * size, transcendentals=0),
+        cost_estimate=light(flops=size, bytes_accessed=6 * size, transcendentals=0),
     )(*arrays, *after)
 
 
+@in_order
 def add_halves(kept, received, after=()):
     parts, quarter, many, rows, columns = kept.shape
     half = quarter // 2
@@ -246,18 +270,18 @@
         out_specs=[out_spec] * 2,
         out_shape=[shape] * 2,
         compiler_params=pltpu.CompilerParams(vmem_limit_bytes=VMEM_LIMIT),
-        cost_estimate=pl.CostEstimate(flops=kept.size, bytes_accessed=6 * kept.size, transcendentals=0),
+        cost_estimate=light(flops=kept.size, bytes_accessed=6 * kept.size, transcendentals=0),
     )(kept, received, *after)
 
 
 class FarSum:
     def __init__(self, pairs, after=()):
-        self.low, self.high = add_far(pairs, after)
+        self.low, self.high = add_far(pairs, after=after)
         self.mask = 4
         self.got = hop(self.high, self.mask)
 
     def step(self, after=()):
-        self.low, self.high = add_halves(self.low, self.got, after)
+        self.low, self.high = add_halves(self.low, self.got, after=after)
         self.mask *= 2
         self.got = hop(self.high, self.mask)
 
@@ -275,7 +299,7 @@
         self.got = hop(self.high, self.order[0])
 
     def step(self, after=()):
-        self.low, self.high = add_near(self.low, self.got, after)
+        self.low, self.high = add_near(self.low, self.got, after=after)
         self.at += 1
         self.got = hop(self.high, self.order[self.at])
 
@@ -285,6 +309,7 @@
         return self.low[0].astype(F32) + self.got[0].astype(F32)
 
 
+@in_order
 def join(first, second, after=()):
     count = first.shape[0]
     shape = (2 * count, *first.shape[1:])
@@ -314,10 +339,11 @@
         out_shape=jax.ShapeDtypeStruct(shape, first.dtype),
         scratch_shapes=[pltpu.VMEM(shape, first.dtype), pltpu.SemaphoreType.DMA((2, 2))],
         compiler_params=pltpu.CompilerParams(vmem_limit_bytes=VMEM_LIMIT),
-        cost_estimate=pl.CostEstimate(flops=0, bytes_accessed=8 * first.size, transcendentals=0),
+        cost_estimate=light(flops=0, bytes_accessed=8 * first.size, transcendentals=0),
     )(first, second, *after)
 
 
+@in_order
 def products(groups, me, after=(), paired=False, tile=None):
     devices = lax.axis_size("fsdp")
     total = 2 * devices if paired else devices
@@ -430,10 +456,11 @@
         ),
         out_shape=[jax.ShapeDtypeStruct(shape, BF) for shape in shapes],
         compiler_params=pltpu.CompilerParams(vmem_limit_bytes=VMEM_LIMIT),
-        cost_estimate=pl.CostEstimate(flops=flops, bytes_accessed=moved, transcendentals=0),
+        cost_estimate=light(flops=flops, bytes_accessed=moved, transcendentals=0),
     )(me, *lefts, *rights, *after)
 
 
+@in_order
 def stack_near(halves, cut, after=()):
     half, rows, columns = halves[0].shape
     ranges = ((0, cut), (cut, columns - cut))
@@ -468,10 +495,11 @@
         out_shape=[jax.ShapeDtypeStruct(shape, BF) for shape in shapes],
         scratch_shapes=[pltpu.VMEM(shape, BF) for shape in shapes] + [pltpu.SemaphoreType.DMA((2, 4))],
         compiler_params=pltpu.CompilerParams(vmem_limit_bytes=VMEM_LIMIT),
-        cost_estimate=pl.CostEstimate(flops=0, bytes_accessed=8 * half * rows * columns, transcendentals=0),
+        cost_estimate=light(flops=0, bytes_accessed=8 * half * rows * columns, transcendentals=0),
     )(*halves, *after)
 
 
+@in_order
 def assemble(low, high, order, me, after=()):
     half, rows, columns = low.shape
     count = 2 * half
@@ -513,7 +541,7 @@
         ),
         out_shape=jax.ShapeDtypeStruct((count, rows, columns), BF),
         compiler_params=pltpu.CompilerParams(vmem_limit_bytes=VMEM_LIMIT),
-        cost_estimate=pl.CostEstimate(flops=0, bytes_accessed=4 * count * rows * columns, transcendentals=0),
+        cost_estimate=light(flops=0, bytes_accessed=4 * count * rows * columns, transcendentals=0),
     )(me, low, high, *after)
 
 
@@ -522,38 +550,39 @@
 
 
 class Gather:
-    def __init__(self, shard, cut, after=()):
+    def __init__(self, shard, cut, first=False):
         self.cut = cut
-        self.held = (pin(shard, after) if after else shard)[None]
+        self.held = (shard if first else pin(shard))[None]
         self.mask = lax.axis_size("fsdp") // 2
         self.far = hop(self.held, self.mask)
 
     def double(self, after=()):
-        self.held = join(self.held, self.far, after)
+        self.held = join(self.held, self.far, after=after)
         self.mask //= 2
         self.far = hop(self.held, self.mask)
 
     def spread(self, after=()):
         while self.mask > 4:
             self.double(after)
-        self.parts = stack_near((self.held, self.far), self.cut, after)
+        self.parts = stack_near((self.held, self.far), self.cut, after=after)
         self.near = [hop(self.parts[0], 1), hop(self.parts[1], 2)]
 
     def widen(self, after=()):
-        self.low = [join(part, near, after) for part, near in zip(self.parts, self.near)]
+        self.low = [join(part, near, after=after) for part, near in zip(self.parts, self.near)]
         self.high = [hop(self.low[0], 2), hop(self.low[1], 1)]
 
     def finish(self, k, me, after=()):
-        return assemble(self.low[k], self.high[k], ((2, 1), (1, 2))[k], me, after)
-
-
-def weave(own, other, me):
+        return assemble(self.low[k], self.high[k], ((2, 1), (1, 2))[k], me, after=after)
+
+
+@in_order
+def weave(own, other, me, after=()):
     count, rows, _ = own[0].shape
     widths = [v.shape[2] for v in own]
     starts = [0, widths[0]]
 
     def kernel(me_ref, *refs):
-        out, held, in_sems, out_sem = refs[4:]
+        out, held, in_sems, out_sem = refs[4 + len(after) :]
 
         def load(k):
             target = held.at[:, me_ref[1 + k // 2], :, pl.ds(starts[k % 2], widths[k % 2])]
@@ -573,7 +602,7 @@
         grid_spec=pltpu.PrefetchScalarGridSpec(
             num_scalar_prefetch=1,
             grid=(1,),
-            in_specs=[ANYWHERE] * 4,
+            in_specs=[ANYWHERE] * (4 + len(after)),
             out_specs=ANYWHERE,
             scratch_shapes=[
                 pltpu.VMEM(shape, BF),
@@ -583,8 +612,8 @@
         ),
         out_shape=jax.ShapeDtypeStruct(shape, BF),
         compiler_params=pltpu.CompilerParams(vmem_limit_bytes=VMEM_LIMIT),
-        cost_estimate=pl.CostEstimate(flops=0, bytes_accessed=8 * count * rows * sum(widths), transcendentals=0),
-    )(me, *own, *other)
+        cost_estimate=light(flops=0, bytes_accessed=8 * count * rows * sum(widths), transcendentals=0),
+    )(me, *own, *other, *after)
     return whole.reshape(2 * count * rows, sum(widths))
 
 
@@ -618,6 +647,7 @@
     return 128 if rows % 128 == 0 else rows
 
 
+@in_order
 def norm_back(partial, received, stream, gain, residual, images, after=()):
     rows, width = stream.shape
     block = row_block(rows)
@@ -660,19 +690,23 @@
             jax.ShapeDtypeStruct((images, 3, 8, width), F32),
         ],
         compiler_params=pltpu.CompilerParams(vmem_limit_bytes=VMEM_LIMIT),
-        cost_estimate=pl.CostEstimate(flops=20 * rows * width, bytes_accessed=20 * rows * width, transcendentals=0),
+        cost_estimate=light(flops=20 * rows * width, bytes_accessed=20 * rows * width, transcendentals=0),
     )(partial, received, stream, gain.reshape(1, -1), residual, *after)
 
 
-def joined_back(grad, first, second, gain, after=()):
+@in_order
+def joined_back(low, weight, first, second, gain, after=()):
     rows, width = first.shape
-    block = row_block(rows)
-
-    def kernel(grad_ref, first_ref, second_ref, gain_ref, *refs):
+    block = 256 if rows % 256 == 0 else rows
+
+    def kernel(low_ref, weight_ref, first_ref, second_ref, gain_ref, *refs):
         first_out, second_out, sums_ref = refs[len(after) :]
         parts = [slice(0, width), slice(width, 2 * width)]
         values = [first_ref[...].astype(F32), second_ref[...].astype(F32)]
-        grads = [grad_ref[:, p] for p in parts]
+        grads = [
+            lax.dot_general(low_ref[...], weight_ref[p, :], (((1,), (1,)), ((), ())), preferred_element_type=F32)
+            for p in parts
+        ]
 
         def mean(arrays):
             return sum(jnp.sum(a, axis=-1, keepdims=True) for a in arrays) * (0.5 / width)
@@ -697,11 +731,11 @@
             sums_ref[1, :, p] += fold_rows(g)
 
     rows_spec = pl.BlockSpec((block, width), lambda i: (i, 0))
-    both_spec = pl.BlockSpec((block, 2 * width), lambda i: (i, 0))
+    whole_spec = pl.BlockSpec(weight.shape, lambda i: (0, 0), pipeline_mode=pl.Buffered(1))
     return pl.pallas_call(
         kernel,
         grid=(rows // block,),
-        in_specs=[both_spec, rows_spec, rows_spec, pl.BlockSpec((1, 2 * width), lambda i: (0, 0))]
+        in_specs=[rows_spec, whole_spec, rows_spec, rows_spec, pl.BlockSpec((1, 2 * width), lambda i: (0, 0))]
         + [ANYWHERE] * len(after),
         out_specs=[rows_spec, rows_spec, pl.BlockSpec((2, 8, 2 * width), lambda i: (0, 0, 0))],
         out_shape=[
@@ -710,14 +744,15 @@
             jax.ShapeDtypeStruct((2, 8, 2 * width), F32),
         ],
         compiler_params=pltpu.CompilerParams(vmem_limit_bytes=VMEM_LIMIT),
-        cost_estimate=pl.CostEstimate(flops=40 * rows * width, bytes_accessed=20 * rows * width, transcendentals=0),
-    )(grad, first, second, gain.reshape(1, -1), *after)
+        cost_estimate=light(flops=40 * rows * width, bytes_accessed=20 * rows * width, transcendentals=0),
+    )(low, weight, first, second, gain.reshape(1, -1), *after)
 
 
 GELU_SCALE = 0.7978845608028654
 GELU_CUBE = 0.044715
 
 
+@in_order
 def first_layer(rows_in, weight, bias, after=()):
     rows, depth = rows_in.shape
     width = weight.shape[1]
@@ -751,12 +786,13 @@
         out_specs=[out_spec] * 2,
         out_shape=[shape] * 2,
         compiler_params=pltpu.CompilerParams(vmem_limit_bytes=VMEM_LIMIT),
-        cost_estimate=pl.CostEstimate(
+        cost_estimate=light(
             flops=2 * rows * depth * width, bytes_accessed=2 * depth * width + 4 * rows * width, transcendentals=rows * width
         ),
     )(rows_in, weight, bias.reshape(1, -1), *after)
 
 
+@in_order
 def first_layer_back(grad, weight, slope, after=()):
     rows, depth = grad.shape
     width = weight.shape[1]
@@ -790,7 +826,7 @@
         out_specs=[pl.BlockSpec((block, tile), lambda n, m: (m, n)), pl.BlockSpec((8, tile), lambda n, m: (0, n))],
         out_shape=[jax.ShapeDtypeStruct((rows, width), BF), jax.ShapeDtypeStruct((8, width), F32)],
         compiler_params=pltpu.CompilerParams(vmem_limit_bytes=VMEM_LIMIT),
-        cost_estimate=pl.CostEstimate(
+        cost_estimate=light(
             flops=2 * rows * depth * width, bytes_accessed=2 * depth * width + 4 * rows * width, transcendentals=0
         ),
     )(grad, weight, slope, *after)
@@ -869,6 +905,7 @@
     return pl.BlockSpec((1, 1, HEAD_DIM, length), lambda i, h: (lead, h, 0, i))
 
 
+@in_order
 def attend(q_pre, k_pre, v_pre, leads, gains, biases, tables, valid, turned, after=()):
     heads = q_pre.shape[1]
     images = q_pre.shape[3] // SEQ
@@ -901,7 +938,7 @@
             pltpu.VMEM((HEAD_DIM, key_len), BF),
         ],
         compiler_params=pltpu.CompilerParams(vmem_limit_bytes=VMEM_LIMIT),
-        cost_estimate=pl.CostEstimate(flops=4 * work * 128, bytes_accessed=12 * q_pre.size, transcendentals=work),
+        cost_estimate=light(flops=4 * work * 128, bytes_accessed=12 * q_pre.size, transcendentals=work),
     )(q_pre, k_pre, v_pre, gains, biases, tables, *after)
 
 
@@ -961,6 +998,7 @@
         cols_ref[0, j, 0] = fold_lanes(part.astype(F32))
 
 
+@in_order
 def attend_back(q_pre, k_pre, v_pre, leads, grad_mix, lse, gains, biases, tables, valid, turned, joint, after=()):
     heads = q_pre.shape[1]
     images = q_pre.shape[3] // SEQ
@@ -1004,7 +1042,7 @@
             pltpu.VMEM((HEAD_DIM, key_len), F32),
         ],
         compiler_params=pltpu.CompilerParams(vmem_limit_bytes=VMEM_LIMIT),
-        cost_estimate=pl.CostEstimate(flops=10 * work * 128, bytes_accessed=20 * q_pre.size, transcendentals=work),
+        cost_estimate=light(flops=10 * work * 128, bytes_accessed=20 * q_pre.size, transcendentals=work),
     )(q_pre, k_pre, v_pre, grad_mix, lse, gains, biases, tables, *after)
 
 
@@ -1067,6 +1105,7 @@
     head_gains,
     head_biases,
 ):
+    Order.last = ()
     count = lax.axis_size("fsdp")
     f_index = lax.axis_index("fsdp")
     t_index = lax.axis_index("tp")
@@ -1080,7 +1119,11 @@
     own_images = max(image_count // 2, 1)
     first_image = t_index * (image_count // 2)
 
-    skip_gather = Gather(skip_weight.astype(BF), cut_of(model_width))
+    skip_gather = Gather(skip_weight.astype(BF), cut_of(model_width), first=True)
+    attention_shard = jnp.concatenate(
+        [qkv_weight.astype(BF).reshape(shard_rows, -1), cross_query.astype(BF)], axis=1
+    )
+    attention_gather = Gather(attention_shard, 2 * local_width, first=True)
 
     activated_own = jax.nn.silu(timestep.astype(F32)).astype(BF)
     small_parts = [column_bias, up_bias, skip_gain, skip_bias, norm_gains, row_biases]
@@ -1105,21 +1148,21 @@
     rbias_f = both_f[:, :, edges[5] : edges[6]].reshape(count, 2, 8, -1).transpose(2, 0, 1, 3).reshape(8, model_width)
     activated = small_own[:, edges[6] :].reshape(count * image_count, model_width)
 
-    attention_shard = jnp.concatenate(
-        [qkv_weight.astype(BF).reshape(shard_rows, -1), cross_query.astype(BF)], axis=1
-    )
-    attention_gather = Gather(attention_shard, 2 * local_width)
     skip_gather.double()
     skip_gather.spread()
-    attention_gather.double((skip_gather.parts[0],))
-    skip_gather.widen((attention_gather.held,))
+    attention_gather.double()
+    skip_gather.widen()
     out_t = out_weight.astype(BF).transpose(2, 0, 1).reshape(shard_rows, -1)
     pair_shard = cross_kv.astype(BF).reshape(shard_rows, -1)
-    branch_gather = Gather(jnp.concatenate([out_t, pair_shard], axis=1), 2 * local_width, (skip_gather.low[0],))
-    skip_own = [skip_gather.finish(k, me, (branch_gather.held,)) for k in range(2)]
+    attention_gather.spread()
+    skip_own = [skip_gather.finish(k, me) for k in range(2)]
+    branch_gather = Gather(jnp.concatenate([out_t, pair_shard], axis=1), 2 * local_width)
     skip_w = weave(skip_own, [swap(v) for v in skip_own], me)
-    attention_gather.spread((skip_own[1],))
-    branch_gather.double((attention_gather.parts[0],))
+    attention_gather.widen()
+    branch_gather.double()
+    ffn_shard = jnp.concatenate([up_weight.astype(BF), down_weight.astype(BF).T], axis=1)
+    ffn_gather = Gather(ffn_shard, ff_local)
+    branch_gather.spread()
 
     device_index = f_index * 2 + t_index
     shift_rows = shift_weight.shape[0]
@@ -1157,18 +1200,13 @@
     stream_zero = plain_dot(normed_skip, skip_w) + rbias_f[6]
     first_in = with_other((layer_norm(stream_zero, ngain_f[0], rbias_f[0]) + shift_tokens).astype(BF))
     grad_ffn = with_other(cotangent)
-    attention_gather.widen((first_in,))
-    branch_gather.spread((attention_gather.low[0], attention_gather.low[1]))
     qk_w, vc_w = [attention_gather.finish(k, me).reshape(model_width, -1) for k in range(2)]
+    ffn_gather.double()
+    branch_gather.widen()
     v_w = vc_w[:, :local_width]
     query_w = vc_w[:, local_width:]
     qk_pre = by_head(turned_dot(qk_w, first_in) + col_bf[0:2].reshape(-1, 1), 2)
     v_pre = by_head(turned_dot(v_w, first_in) + col_bf[2].reshape(-1, 1), 1)
-    branch_gather.widen((qk_pre, v_pre))
-    up_shard = pin(up_weight.astype(BF), (attention_gather.low[1],))
-    down_shard = pin(down_weight.astype(BF).T, (up_shard,))
-    up_w = lax.all_gather(up_shard, "fsdp", axis=0, tiled=True)
-    down_t = lax.all_gather(down_shard, "fsdp", axis=0, tiled=True)
     mixture, self_lse = attend(
         qk_pre,
         qk_pre,
@@ -1179,9 +1217,10 @@
         tables,
         SEQ,
         True,
-        (branch_gather.low[0], branch_gather.low[1], down_shard),
-    )
-    proj_t, pair_w = [branch_gather.finish(k, me) for k in range(2)]
+    )
+    pair_w = branch_gather.finish(1, me)
+    ffn_gather.spread()
+    proj_t = branch_gather.finish(0, me)
     proj_t = proj_t.reshape(model_width, -1)
     pair_w = pair_w.reshape(text_width, 2 * local_width)
     self_t = proj_t[:, :local_width]
@@ -1194,18 +1233,21 @@
     cross_mixture, cross_lse = attend(
         cross_pre, pair_pre, pair_pre, (0, 0, 1), gains_column[2:4], biases_column[2:4], tables, text_len, False
     )
+    ffn_gather.widen()
     cross_mixture = cross_mixture.reshape(local_width, -1)
     stream_two = stream_one + turned_branch_sum(cross_mixture, cross_t, rows_local) + rbias_f[4]
     third_in = with_other(layer_norm(stream_two, ngain_f[2], rbias_f[2]).astype(BF))
+    up_w = ffn_gather.finish(0, me).reshape(model_width, -1)
     hidden_act, slope = first_layer(third_in, up_w, up_bf)
+    down_t = ffn_gather.finish(1, me).reshape(model_width, -1)
+
+    grad_pre, upb_sums = first_layer_back(grad_ffn, down_t, slope)
+    grad_upb = jnp.sum(upb_sums, axis=0)
     tile = 512 if ff_local % 512 == 0 else None
+    up = Chain(products([(UP_ORDER, [(third_in, grad_pre, False, 0, ff_local)])], me, tile=tile), UP_ORDER)
     down = Chain(products([(DOWN_ORDER, [(grad_ffn, hidden_act, False, 0, ff_local)])], me, tile=tile), DOWN_ORDER)
-
-    grad_pre, upb_sums = first_layer_back(grad_ffn, down_t, slope, (down.high,))
-    grad_upb = jnp.sum(upb_sums, axis=0)
-    up = Chain(products([(UP_ORDER, [(third_in, grad_pre, False, 0, ff_local)])], me, tile=tile), UP_ORDER)
     third_part, third_got = branch_parts(grad_pre, up_w, rows_local)
-    grad_two, low_two, sums_two = norm_back(third_part, third_got, stream_two, ngain_f[2], cotangent, 1, (up.high,))
+    grad_two, low_two, sums_two = norm_back(third_part, third_got, stream_two, ngain_f[2], cotangent, 1)
     grad_cross = with_other(low_two)
     grad_cmix = lax.dot_general(cross_t, grad_cross, (((0,), (1,)), ((), ())), preferred_element_type=F32).astype(BF)
     grad_cq, grad_pair, cross_sums, cross_cols = attend_back(
@@ -1225,22 +1267,19 @@
     grad_cq = grad_cq.reshape(local_width, -1)
     grad_pair = grad_pair.reshape(2 * local_width, -1)
     second_part, second_got = turned_branch_parts(grad_cq, query_w, rows_local)
-    down.step((grad_cq,))
-    grad_one, low_one, sums_one = norm_back(
-        second_part, second_got, stream_one, ngain_f[1], grad_two, 1, (down.high,)
-    )
+    up.step()
+    grad_one, low_one, sums_one = norm_back(second_part, second_got, stream_one, ngain_f[1], grad_two, 1)
+    down.step()
     grad_self = with_other(low_one)
-    up.step((low_one,))
     halves = products(
         [
             ((1, 2), [(grad_cross, cross_mixture, True, 0, local_width), (second_in, grad_cq, True, 0, local_width)]),
             ((2, 1), [(text_in, grad_pair, True, 0, 2 * local_width)]),
         ],
         me,
-        (up.high,),
     )
     cross_kept, cross_sent = halves[0::2], halves[1::2]
-    down.step(cross_sent)
+    up.step()
     cross_got = [hop(cross_sent[0], 1), hop(cross_sent[1], 2)]
     grad_mix = lax.dot_general(self_t, grad_self, (((0,), (1,)), ((), ())), preferred_element_type=F32).astype(BF)
     grad_qkv, self_sums, self_cols = attend_back(
@@ -1256,12 +1295,11 @@
         SEQ,
         True,
         True,
-        (down.high,),
-    )
-    up.step((grad_qkv,))
-    down.step((up.high,))
-    cross_near = [add_near(v, g, (down.high,)) for v, g in zip(cross_kept, cross_got)]
+    )
+    down.step()
+    cross_near = [add_near(v, g) for v, g in zip(cross_kept, cross_got)]
     cross_got = [hop(cross_near[0][1], 2), hop(cross_near[1][1], 1)]
+    up.step()
     grad_qkv = grad_qkv.reshape(3 * local_width, -1)
     halves = products(
         [
@@ -1275,18 +1313,18 @@
             ),
         ],
         me,
-        (cross_near[0][1], cross_near[1][1]),
     )
     self_kept, self_sent = halves[0::2], halves[1::2]
     self_got = [hop(self_sent[0], 1), hop(self_sent[1], 2)]
-    cross_far = FarSum([(v[0], g) for v, g in zip(cross_near, cross_got)], self_sent)
+    cross_far = FarSum([(v[0], g) for v, g in zip(cross_near, cross_got)])
+    down.step()
     grad_qk = grad_qkv[: 2 * local_width]
     grad_v = grad_qkv[2 * local_width :]
     first_part = turned_dot(grad_qk[:, rows_local:], qk_w) + turned_dot(grad_v[:, rows_local:], v_w)
     first_got = swap(first_part.astype(BF))
     first_part = turned_dot(grad_qk[:, :rows_local], qk_w) + turned_dot(grad_v[:, :rows_local], v_w)
     grad_zero, low_zero, sums_zero = norm_back(
-        first_part, first_got, stream_zero, ngain_f[0], grad_one, own_images, (cross_far.high,)
+        first_part, first_got, stream_zero, ngain_f[0], grad_one, own_images
     )
     skip_cut = model_width // 2
     skip_kept, skip_sent = products(
@@ -1298,16 +1336,14 @@
         paired=True,
     )
     skip_got = swap(skip_sent)
-    self_near = [add_near(v, g, (skip_sent,)) for v, g in zip(self_kept, self_got)]
+    skip_pair = [add_near(skip_kept, skip_got, part=k) for k in range(2)]
+    skip_got = [hop(skip_pair[0][1], 1), hop(skip_pair[1][1], 2)]
+    cross_far.step()
+    input_grad, skip_grad, skip_sums = joined_back(low_zero, skip_w, hidden, skip_rows, sgain_f)
+    self_near = [add_near(v, g) for v, g in zip(self_kept, self_got)]
     self_got = [hop(self_near[0][1], 2), hop(self_near[1][1], 1)]
-    skip_pair = [
-        add_near(skip_kept, skip_got, (self_near[0][1], self_near[1][1]), part=k) for k in range(2)
-    ]
-    skip_got = [hop(skip_pair[0][1], 1), hop(skip_pair[1][1], 2)]
-    up.step((skip_pair[0][1], skip_pair[1][1]))
-    cross_far.step((up.high,))
-    grad_normed = dot_last(low_zero, skip_w)
-    input_grad, skip_grad, skip_sums = joined_back(grad_normed, hidden, skip_rows, sgain_f, (cross_far.high,))
+    skip_near = [add_near(v[0], g) for v, g in zip(skip_pair, skip_got)]
+    skip_got = [hop(skip_near[0][1], 2), hop(skip_near[1][1], 1)]
     stream_three = stream_two + branch_sum(hidden_act, down_t, rows_local) + rbias_f[5]
     output = stream_three.astype(BF)
     text_half = text_width // 2
@@ -1327,14 +1363,14 @@
     shift_held = (shift_local + swap(shift_local))[None]
     shift_masks = [0]
 
-    def shift_double(held, mask, after):
-        held = pin(held, after)
+    def shift_double(held, mask):
+        held = pin(held)
         return jnp.concatenate([held, hop(held, mask)], axis=0), shift_masks + [m + mask for m in shift_masks]
 
     far_bits = [4 << b for b in range(30) if 4 << b < count]
-    for mask in far_bits[:-1]:
-        shift_held, shift_masks = shift_double(shift_held, mask, (skip_sent,))
-    shift_held, shift_masks = shift_double(shift_held, far_bits[-1], (skip_pair[0][1],))
+    for mask in far_bits:
+        shift_held, shift_masks = shift_double(shift_held, mask)
+
     sums_zero, sums_one, sums_two = (jnp.sum(v, axis=(0, 2)) for v in (sums_zero, sums_one, sums_two))
     skip_sums = jnp.sum(skip_sums, axis=1)
     grad_gains = jnp.stack([sums_zero[0], sums_one[0], sums_two[0]], axis=0)
@@ -1382,21 +1418,19 @@
     blocks = jnp.pad(blocks, ((0, 0), (0, 0), (0, padded - blocks.shape[-1])))
     blocks = blocks.transpose(1, 0, 2).reshape(2 * count, padded // 128, 128)
     small_kept, small_sent = halve([blocks], (1, 2), me, paired=True)
+    self_far = FarSum([(v[0], g) for v, g in zip(self_near, self_got)])
+    skip_far = FarSum([(v[0], g) for v, g in zip(skip_near, skip_got)])
     small_pair = add_near(small_kept, swap(small_sent))
     small_got = hop(small_pair[1], 1)
-    shift_held, shift_masks = shift_double(shift_held, 1, (small_pair[1],))
-
-    skip_near = [add_near(v[0], g, (small_pair[1],)) for v, g in zip(skip_pair, skip_got)]
-    skip_got = [hop(skip_near[0][1], 2), hop(skip_near[1][1], 1)]
-    small_near = add_near(small_pair[0], small_got, (skip_near[0][1], skip_near[1][1]))
+    shift_held, shift_masks = shift_double(shift_held, 1)
+
+    small_near = add_near(small_pair[0], small_got)
     small_got = hop(small_near[1], 2)
-    self_far = FarSum([(v[0], g) for v, g in zip(self_near, self_got)], (small_near[1],))
-    shift_held, shift_masks = shift_double(shift_held, 2, (self_far.high,))
-    skip_far = FarSum([(v[0], g) for v, g in zip(skip_near, skip_got)], (self_far.high,))
-    small_far = FarSum([(small_near[0], small_got)], (skip_far.high,))
-    self_far.step((small_far.high,))
-    skip_far.step((self_far.high,))
-    small_far.step((skip_far.high,))
+    self_far.step()
+    skip_far.step()
+    small_far = FarSum([(small_near[0], small_got)])
+    shift_held, shift_masks = shift_double(shift_held, 2)
+    small_far.step()
     cross_sum = cross_far.total()
     shift_all = order_from_masks(
         shift_held.reshape(count, image_count * model_width), np.array(shift_masks)

time: 1140 us -> 1050 us (0.921)
  waiting for transfers between devices: 333 us -> 265 us
  local copies, waits for them, and re-layouts: 85.3 us -> 65 us
  matrix products: 145 us -> 129 us
  between operations: 16.4 us -> 2.74 us
  Pallas kernels: 416 us -> 428 us
    ppermute x62 -> x68, waiting for transfers between devices: 327 us -> 261 us  [hop(): return lax.ppermute(values, 'fsdp', [(i, i ^ mask) for i in range(count)])]
    pallas_call x17, Pallas kernels: 81.8 us -> 66.1 us  [the longest x16 52.5 us: add_near(): pl.pallas_call(kernel, grid=(quarter // group, columns // tile), in_specs...]
    pallas_call x6 -> x8, Pallas kernels: 23.5 us -> 37.9 us  [assemble(): pl.pallas_call(kernel, grid_spec=pltpu.PrefetchScalarGridSpec(num_scalar_...]
    unnamed x214 -> x192, local copies, waits for them, and re-layouts: 32.3 us -> 18.5 us
    dot_general x5 -> x4, matrix products: 50.5 us -> 38.9 us  [dot_last(): lax.dot_general(first_operand, second_operand, (((1,), (1,)), ((), ())),...]
    pallas_call x9 -> x12, Pallas kernels: 19.6 us -> 29.8 us  [join(): pl.pallas_call(kernel, in_specs=[ANYWHERE] * (2 + len(after)), out_specs=...]
    ppermute x62 -> x68, starting transfers between devices: 76.4 us -> 77.6 us  [hop(): return lax.ppermute(values, 'fsdp', [(i, i ^ mask) for i in range(count)])]
  transfers between devices with their start and end apart: 84 -> 88, of which waited for: 28 -> 30; matrix products, arithmetic and copies ran while one was open for 22% -> 21% of each run, Pallas kernels for 34% -> 37%
where the time goes in v3:
time: 1050 us; the launch traced here: 1030 us
  Pallas kernels  428 us (41%)
  waiting for transfers between devices  265 us (25%)
  matrix products  129 us (12%)
  starting transfers between devices  80.8 us (8%)
  local copies, waits for them, and re-layouts  65 us (6%)
  other arithmetic  63.2 us (6%)
    ppermute x68, waiting for transfers between devices, hop(): return lax.ppermute(values, 'fsdp', [(i, i ^ mask) for i in range(count)])  261 us
    pallas_call x5, Pallas kernels, products(): pl.pallas_call(kernel, grid_spec=pltpu.PrefetchScalarGridSpec(num_scalar_...  84 us
    ppermute x68, starting transfers between devices, hop(): return lax.ppermute(values, 'fsdp', [(i, i ^ mask) for i in range(count)])  77.6 us
    dot_general x16, matrix products, turned_dot(): lax.dot_general(first_operand, second_operand, (((0,), (1,)), ((), ())),...  70.1 us
    pallas_call x2, Pallas kernels, attend_back(): pl.pallas_call(functools.partial(attend_back_kernel, valid, turned, joint...  60.3 us
    pallas_call x16, Pallas kernels, add_near(): pl.pallas_call(kernel, grid=(quarter // group, columns // tile), in_specs...  52.5 us
    pallas_call x2, Pallas kernels, attend(): pl.pallas_call(functools.partial(attend_kernel, valid, turned, len(after)...  43.4 us
    dot_general x4, matrix products, dot_last(): lax.dot_general(first_operand, second_operand, (((1,), (1,)), ((), ())),...  38.9 us
  transfers between devices with their start and end apart: 88, of which 30 were waited for; matrix products, arithmetic and copies ran while one was open for 21% of the time, Pallas kernels for 37%

profile of v3, /device:TPU:0, one launch (start us, length us, event | category | flops | bytes accessed | tf_op | source)
XLA Modules:
  0.0 1034.8 jit_solution(1460406786046128609)
XLA Ops:
  85.3 19.3 %collective-permute-done.22 = f32[8,1408]{1,0:T(8,128)S(1)} collective-permute-done((f32[8,1408]{1,0:T(8,128)S(1)}, f32[8,1408]{1,0:T(8,128)S(1)}, u32[]{:S(2)}, u32[]{:S(2)}) %collective-permute-start.22) | collective-permute-done | bytes 45088 | tf_op jit(solution)/shard_map/ppermute | solution.py:25
  172.2 19.8 %collective-permute-done.20.refs_1_ = bf16[2,88,2432]{2,1,0:T(8,128)(2,1)} collective-permute-done((bf16[2,88,2432]{2,1,0:T(8,128)(2,1)}, bf16[2,88,2432]{2,1,0:T(8,128)(2,1)}, u32[]{:S(2)}, u32[]{:S(2)}) %collective-permute-start.20) | collective-permute-done | bytes 856096 | tf_op jit(solution)/shard_map/ppermute | solution.py:25
  231.6 9.4 convolution_add_fusion
  241.0 27.5 %shard_map.412 = (bf16[8,88,1024]{2,1,0:T(8,128)(2,1)}, f32[8,1,1024]{2,1,0:T(1,128)}) custom-call(f32[2,8,88,1024]{3,2,1,0:T(8,128)} %bitcast.142, f32[2,8,88,1024]{3,2,1,0:T(8,128)} %bitcast.143, f32[1,8,88,1024]{3,2,1,0:T(8,128)} %bitcast.177, f32[2,88,1]{2,1,0:T(8,128)} %copy.85.gain_ref, f32[2,88,1]{2,1,0:T(8,128)} %copy.86.bias_ref, ...), custom_call_target="tpu_custom_call" | custom-call | flops 1 | bytes 1 | tf_op jit(solution)/shard_map/pallas_call | solution.py:915
  314.2 15.9 %shard_map.416 = (bf16[8,88,1024]{2,1,0:T(8,128)(2,1)}, f32[8,1,1024]{2,1,0:T(1,128)}) custom-call(f32[1,8,88,1024]{3,2,1,0:T(8,128)} %bitcast.179, f32[2,8,88,384]{3,2,1,0:T(8,128)} %bitcast.156, f32[2,8,88,384]{3,2,1,0:T(8,128)} %bitcast.157, f32[2,88,1]{2,1,0:T(8,128)} %copy.89.gain_ref, f32[2,88,1]{2,1,0:T(8,128)} %copy.90.bias_ref, ...), custom_call_target="tpu_custom_call" | custom-call | flops 1 | bytes 1 | tf_op jit(solution)/shard_map/pallas_call | solution.py:915
  333.5 10.4 %collective-permute-done.39.second_ref = bf16[4,88,3072]{2,1,0:T(8,128)(2,1)} collective-permute-done((bf16[4,88,3072]{2,1,0:T(8,128)(2,1)}, bf16[4,88,3072]{2,1,0:T(8,128)(2,1)}, u32[]{:S(2)}, u32[]{:S(2)}) %collective-permute-start.39) | collective-permute-done | bytes 2162720 | tf_op jit(solution)/shard_map/ppermute | solution.py:25
  371.1 71.8 %collective-permute-done.40.refs_1_ = bf16[8,88,3072]{2,1,0:T(8,128)(2,1)} collective-permute-done((bf16[8,88,3072]{2,1,0:T(8,128)(2,1)}, bf16[8,88,3072]{2,1,0:T(8,128)(2,1)}, u32[]{:S(2)}, u32[]{:S(2)}) %collective-permute-start.40) | collective-permute-done | bytes 4325408 | tf_op jit(solution)/shard_map/ppermute | solution.py:25
  450.1 20.5 %shard_map.420 = (bf16[1024,3072]{1,0:T(8,128)(2,1)}, bf16[1024,3072]{1,0:T(8,128)(2,1)}) custom-call(bf16[1024,1408]{1,0:T(8,128)(2,1)} %pad_maximum_fusion.3.rows_ref.refs_0_, bf16[1408,3072]{1,0:T(8,128)(2,1)} %bitcast.149, f32[1,3072]{1,0:T(1,128)} %reshape_reshape.4.bias_ref, bf16[16,88,3072]{2,1,0:T(8,128)(2,1)} %shard_map.419.refs_0_), custom_call_target="tpu_custom_call" | custom-call | flops 1 | bytes 1 | tf_op jit(solution)/shard_map/pallas_call | solution.py:777
  477.7 15.3 %shard_map.422 = (bf16[1024,3072]{1,0:T(8,128)(2,1)}, f32[8,3072]{1,0:T(8,128)}) custom-call(bf16[1024,1408]{1,0:T(8,128)(2,1)} %copy-done.9, bf16[1408,3072]{1,0:T(8,128)(2,1)} %bitcast.146, bf16[1024,3072]{1,0:T(8,128)(2,1)} %get-tuple-element.132.slope_ref, bf16[16,88,3072]{2,1,0:T(8,128)(2,1)} %shard_map.421.refs_0_), custom_call_target="tpu_custom_call" | custom-call | flops 1 | bytes 1 | tf_op jit(solution)/shard_map/pallas_call | solution.py:817
  493.0 10.5 %fusion.23 = bf16[512,1408]{1,0:T(8,128)(2,1)} fusion(bf16[1408,3072]{1,0:T(8,128)(2,1)} %bitcast.150, bf16[1024,3072]{1,0:T(8,128)(2,1)} %get-tuple-element.133.refs_1_.refs_2_), kind=kOutput, calls=%fused_computation.37 | convolution fusion | flops 4429905920 | bytes 13238272 | tf_op jit(solution)/shard_map/dot_general | solution.py:635
  503.6 17.1 %shard_map.423 = (bf16[8,1,88,3072]{3,2,1,0:T(8,128)(2,1)}, bf16[8,1,88,3072]{3,2,1,0:T(8,128)(2,1)}) custom-call(s32[3]{0:T(128)} %pad_add_fusion.me_ref, bf16[1024,1408]{1,0:T(8,128)(2,1)} %pad_maximum_fusion.3.rows_ref.refs_0_, bf16[1024,3072]{1,0:T(8,128)(2,1)} %get-tuple-element.133.refs_1_.refs_2_, bf16[1024,3072]{1,0:T(8,128)(2,1)} %get-tuple-element.133.refs_1_.refs_2_), custom_call_target="tpu_custom_call" | custom-call | flops 1 | bytes 1 | tf_op jit(solution)/shard_map/pallas_call | solution.py:445
  530.2 16.7 %shard_map.424 = (bf16[8,1,88,3072]{3,2,1,0:T(8,128)(2,1)}, bf16[8,1,88,3072]{3,2,1,0:T(8,128)(2,1)}) custom-call(s32[3]{0:T(128)} %pad_add_fusion.me_ref, bf16[1024,1408]{1,0:T(8,128)(2,1)} %copy-done.9, bf16[1024,3072]{1,0:T(8,128)(2,1)} %get-tuple-element.131.refs_2_.refs_1_, bf16[8,1,88,3072]{3,2,1,0:T(8,128)(2,1)} %get-tuple-element.134.refs_2_.kept_low.kept_high), custom_call_target="tpu_custom_call" | custom-call | flops 1 | bytes 1 | tf_op jit(solution)/shard_map/pallas_call | solution.py:445
  563.5 21.2 %shard_map.426 = (bf16[1,8,88,1024]{3,2,1,0:T(8,128)(2,1)}, bf16[2,8,88,384]{3,2,1,0:T(8,128)(2,1)}, f32[4,88,128]{2,1,0:T(8,128)}, f32[1,3,8,88,128]{4,3,2,1,0:T(8,128)}) custom-call(f32[1,8,88,1024]{3,2,1,0:T(8,128)} %bitcast.180, f32[2,8,88,384]{3,2,1,0:T(8,128)} %bitcast.158, f32[2,8,88,384]{3,2,1,0:T(8,128)} %bitcast.159, ...), custom_call_target="tpu_custom_call" | custom-call | flops 1 | bytes 1 | tf_op jit(solution)/shard_map/pallas_call | solution.py:1009
  605.9 10.9 %collective-permute-done.48.got_low.got_high = bf16[8,1,88,3072]{3,2,1,0:T(8,128)(2,1)} collective-permute-done((bf16[8,1,88,3072]{3,2,1,0:T(8,128)(2,1)}, bf16[8,1,88,3072]{3,2,1,0:T(8,128)(2,1)}, u32[]{:S(2)}, u32[]{:S(2)}) %collective-permute-start.48) | collective-permute-done | bytes 4325408 | tf_op jit(solution)/shard_map/ppermute | solution.py:25
  641.0 10.3 collective-permute-done.51.got_low.got_high
  658.9 15.9 %shard_map.430 = (bf16[8,1,88,1408]{3,2,1,0:T(8,128)(2,1)}, bf16[8,1,88,1408]{3,2,1,0:T(8,128)(2,1)}, bf16[8,1,64,1408]{3,2,1,0:T(8,128)(2,1)}, bf16[8,1,64,1408]{3,2,1,0:T(8,128)(2,1)}) custom-call(s32[3]{0:T(128)} %pad_add_fusion.me_ref, bf16[1024,1408]{1,0:T(8,128)(2,1)} %copy-done.22, bf16[1024,1408]{1,0:T(8,128)(2,1)} %pad_maximum_fusion.2.refs_1_, ...), custom_call_target="tpu_custom_call" | custom-call | flops 1 | bytes 1 | tf_op jit(solution)/shard_map/pallas_call | solution.py:445
  685.2 39.2 %shard_map.432 = (bf16[3,8,88,1024]{3,2,1,0:T(8,128)(2,1)}, f32[4,88,128]{2,1,0:T(8,128)}, f32[1,3,8,88,128]{4,3,2,1,0:T(8,128)}) custom-call(f32[2,8,88,1024]{3,2,1,0:T(8,128)} %bitcast.144, f32[2,8,88,1024]{3,2,1,0:T(8,128)} %bitcast.145, f32[1,8,88,1024]{3,2,1,0:T(8,128)} %bitcast.178, bf16[8,88,1024]{2,1,0:T(8,128)(2,1)} %bitcast.200, ...), custom_call_target="tpu_custom_call" | custom-call | flops 1 | bytes 1 | tf_op jit(solution)/shard_map/pallas_call | solution.py:1009
  770.8 19.3 %shard_map.437 = (bf16[8,1,88,1408]{3,2,1,0:T(8,128)(2,1)}, bf16[8,1,88,1408]{3,2,1,0:T(8,128)(2,1)}, bf16[8,1,88,1408]{3,2,1,0:T(8,128)(2,1)}, bf16[8,1,88,1408]{3,2,1,0:T(8,128)(2,1)}) custom-call(s32[3]{0:T(128)} %pad_add_fusion.me_ref, bf16[1024,1408]{1,0:T(8,128)(2,1)} %pad_maximum_fusion.1.refs_0_, bf16[1024,1408]{1,0:T(8,128)(2,1)} %copy-done.21, ...), custom_call_target="tpu_custom_call" | custom-call | flops 1 | bytes 1 | tf_op jit(solution)/shard_map/pallas_call | solution.py:445
  807.4 15.0 %shard_map.441 = (bf16[2,16,1,88,704]{4,3,2,1,0:T(8,128)(2,1)}, bf16[2,16,1,88,704]{4,3,2,1,0:T(8,128)(2,1)}) custom-call(s32[3]{0:T(128)} %pad_add_fusion.me_ref, bf16[512,2816]{1,0:T(8,128)(2,1)} %fusion.5.refs_0_, bf16[512,1408]{1,0:T(8,128)(2,1)} %get-tuple-element.167.refs_1_.low_ref, f32[512,1408]{1,0:T(8,128)} %get-tuple-element.169.refs_2_), custom_call_target="tpu_custom_call" | custom-call | flops 1 | bytes 1 | tf_op jit(solution)/shard_map/pallas_call | solution.py:445
  822.5 10.6 %fusion.26 = bf16[512,1408]{1,0:T(8,128)(2,1)} fusion(f32[512,1408]{1,0:T(8,128)S(1)} %copy-done.4, bf16[1408,3072]{1,0:T(8,128)(2,1)} %bitcast.148, bf16[1024,3072]{1,0:T(8,128)(2,1)} %get-tuple-element.131.refs_2_.refs_1_, bf16[512,1408]{1,0:T(8,128)(2,1)} %collective-permute-done.43, f32[1408]{0:T(1024)S(1)} %add.376), kind=kOutput, calls=%fused_computation.38 | convolution fusion | flops 4432789504 | bytes 17569280 | tf_op jit(solution)/shard_map/dot_general | solution.py:635
  855.5 24.0 %collective-permute-done.60.got_ref = bf16[2,2,1,88,1408]{4,3,2,1,0:T(8,128)(2,1)S(1)} collective-permute-done((bf16[2,2,1,88,1408]{4,3,2,1,0:T(8,128)(2,1)}, bf16[2,2,1,88,1408]{4,3,2,1,0:T(8,128)(2,1)S(1)}, u32[]{:S(2)}, u32[]{:S(2)}) %collective-permute-start.60) | collective-permute-done | bytes 991264 | tf_op jit(solution)/shard_map/ppermute | solution.py:25
  884.3 13.6 %shard_map.445 = (f32[512,1408]{1,0:T(8,128)}, f32[512,1408]{1,0:T(8,128)}, f32[2,8,2816]{2,1,0:T(8,128)}) custom-call(bf16[512,1408]{1,0:T(8,128)(2,1)} %get-tuple-element.167.refs_1_.low_ref, bf16[2816,1408]{1,0:T(8,128)(2,1)} %bitcast.154, bf16[512,1408]{1,0:T(8,128)(2,1)} %first_ref.1, bf16[512,1408]{1,0:T(8,128)(2,1)} %second_ref.1, ...), custom_call_target="tpu_custom_call" | custom-call | flops 1 | bytes 1 | tf_op jit(solution)/shard_map/pallas_call | solution.py:735
  959.4 13.4 %collective-permute-done.74.got_ref = bf16[2,2,1,88,1408]{4,3,2,1,0:T(8,128)(2,1)S(1)} collective-permute-done((bf16[2,2,1,88,1408]{4,3,2,1,0:T(8,128)(2,1)}, bf16[2,2,1,88,1408]{4,3,2,1,0:T(8,128)(2,1)S(1)}, u32[]{:S(2)}, u32[]{:S(2)}) %collective-permute-start.74) | collective-permute-done | bytes 991264 | tf_op jit(solution)/shard_map/ppermute | solution.py:25
  1009.8 12.0 %collective-permute-done.78 = bf16[2,1,1,88,704]{4,3,2,1,0:T(8,128)(2,1)S(1)} collective-permute-done((bf16[2,1,1,88,704]{4,3,2,1,0:T(8,128)(2,1)S(1)}, bf16[2,1,1,88,704]{4,3,2,1,0:T(8,128)(2,1)S(1)}, u32[]{:S(2)}, u32[]{:S(2)}) %collective-permute-start.78) | collective-permute-done | bytes 247840 | tf_op jit(solution)/shard_map/ppermute | solution.py:25
  (663 shorter events, 572.6 us)
Async XLA Ops:
  20.6 46.7 %collective-permute-start.9 = (bf16[1,88,2816]{2,1,0:T(8,128)(2,1)S(1)}, bf16[1,88,2816]{2,1,0:T(8,128)(2,1)}, u32[]{:S(2)}, u32[]{:S(2)}) collective-permute-start(bf16[1,88,2816]{2,1,0:T(8,128)(2,1)S(1)} %maximum_bitcast_fusion.first_ref), channel_id=1, source_target_pairs={{0,16},{2,18},{4,20},{6,22},{8,24},{10,26},{12,28},{14,30},{16,0},... | collective-permute-start | bytes 1486856 | tf_op jit(solution)/shard_map/ppermute | solution.py:25
  147.2 53.3 %collective-permute-start.17 = (bf16[8,88,1408]{2,1,0:T(8,128)(2,1)}, bf16[8,88,1408]{2,1,0:T(8,128)(2,1)}, u32[]{:S(2)}, u32[]{:S(2)}) collective-permute-start(bf16[8,88,1408]{2,1,0:T(8,128)(2,1)} %shard_map.402.refs_0_), channel_id=1, source_target_pairs={{0,4},{2,6},{4,0},{6,2},{8,12},{10,14},{12,8},{14,10},{16,20},{18,... | collective-permute-start | bytes 5947400 | tf_op jit(solution)/shard_map/ppermute | solution.py:25
  151.3 54.1 %collective-permute-start.28 = (bf16[8,88,1408]{2,1,0:T(8,128)(2,1)}, bf16[8,88,1408]{2,1,0:T(8,128)(2,1)}, u32[]{:S(2)}, u32[]{:S(2)}) collective-permute-start(bf16[8,88,1408]{2,1,0:T(8,128)(2,1)} %shard_map.403.refs_0_), channel_id=1, source_target_pairs={{0,2},{2,0},{4,6},{6,4},{8,10},{10,8},{12,14},{14,12},{16,18},{18,... | collective-permute-start | bytes 5947400 | tf_op jit(solution)/shard_map/ppermute | solution.py:25
  159.2 50.5 %collective-permute-start.31 = (bf16[1,88,6144]{2,1,0:T(8,128)(2,1)}, bf16[1,88,6144]{2,1,0:T(8,128)(2,1)}, u32[]{:S(2)}, u32[]{:S(2)}) collective-permute-start(bf16[1,88,6144]{2,1,0:T(8,128)(2,1)} %bitcast.181), channel_id=1, source_target_pairs={{0,16},{2,18},{4,20},{6,22},{8,24},{10,26},{12,28},{14,30},{16,0},... | collective-permute-start | bytes 3244040 | tf_op jit(solution)/shard_map/ppermute | solution.py:25
  172.2 53.2 %collective-permute-start.27 = (bf16[512,1408]{1,0:T(8,128)(2,1)}, bf16[512,1408]{1,0:T(8,128)(2,1)}, u32[]{:S(2)}, u32[]{:S(2)}) collective-permute-start(bf16[512,1408]{1,0:T(8,128)(2,1)} %add_convert_fusion.2), channel_id=1, source_target_pairs={{0,1},{1,0},{2,3},{3,2},{4,5},{5,4},{6,7},{7,6},{8,9},{9,8},{10,11... | collective-permute-start | bytes 4325384 | tf_op jit(solution)/shard_map/ppermute | solution.py:29
  212.4 59.9 %collective-permute-start.33 = (bf16[2,88,6144]{2,1,0:T(8,128)(2,1)}, bf16[2,88,6144]{2,1,0:T(8,128)(2,1)}, u32[]{:S(2)}, u32[]{:S(2)}) collective-permute-start(bf16[2,88,6144]{2,1,0:T(8,128)(2,1)} %shard_map.409.refs_0_), channel_id=1, source_target_pairs={{0,8},{2,10},{4,12},{6,14},{8,0},{10,2},{12,4},{14,6},{16,24},{18,... | collective-permute-start | bytes 6488072 | tf_op jit(solution)/shard_map/ppermute | solution.py:25
  219.5 56.3 %collective-permute-start.32 = (bf16[8,88,1408]{2,1,0:T(8,128)(2,1)}, bf16[8,88,1408]{2,1,0:T(8,128)(2,1)}, u32[]{:S(2)}, u32[]{:S(2)}) collective-permute-start(bf16[8,88,1408]{2,1,0:T(8,128)(2,1)} %shard_map.410.refs_0_), channel_id=1, source_target_pairs={{0,4},{2,6},{4,0},{6,2},{8,12},{10,14},{12,8},{14,10},{16,20},{18,... | collective-permute-start | bytes 5947400 | tf_op jit(solution)/shard_map/ppermute | solution.py:25
  294.3 49.6 %collective-permute-start.39 = (bf16[4,88,3072]{2,1,0:T(8,128)(2,1)}, bf16[4,88,3072]{2,1,0:T(8,128)(2,1)}, u32[]{:S(2)}, u32[]{:S(2)}) collective-permute-start(bf16[4,88,3072]{2,1,0:T(8,128)(2,1)} %get-tuple-element.128.refs_2_.first_ref), channel_id=1, source_target_pairs={{0,2},{2,0},{4,6},{6,4},{8,10},{10,8},{12,14},{14,12},{16,18},{18,... | collective-permute-start | bytes 6488072 | tf_op jit(solution)/shard_map/ppermute | solution.py:25
  294.8 54.4 %collective-permute-start.41 = (bf16[4,88,3072]{2,1,0:T(8,128)(2,1)}, bf16[4,88,3072]{2,1,0:T(8,128)(2,1)}, u32[]{:S(2)}, u32[]{:S(2)}) collective-permute-start(bf16[4,88,3072]{2,1,0:T(8,128)(2,1)} %get-tuple-element.130.first_ref), channel_id=1, source_target_pairs={{0,4},{2,6},{4,0},{6,2},{8,12},{10,14},{12,8},{14,10},{16,20},{18,... | collective-permute-start | bytes 6488072 | tf_op jit(solution)/shard_map/ppermute | solution.py:25
  347.7 95.2 %collective-permute-start.40 = (bf16[8,88,3072]{2,1,0:T(8,128)(2,1)}, bf16[8,88,3072]{2,1,0:T(8,128)(2,1)}, u32[]{:S(2)}, u32[]{:S(2)}) collective-permute-start(bf16[8,88,3072]{2,1,0:T(8,128)(2,1)} %shard_map.417.refs_0_), channel_id=1, source_target_pairs={{0,4},{2,6},{4,0},{6,2},{8,12},{10,14},{12,8},{14,10},{16,20},{18,... | collective-permute-start | bytes 12976136 | tf_op jit(solution)/shard_map/ppermute | solution.py:25
  352.9 117.6 %collective-permute-start.42 = (bf16[8,88,3072]{2,1,0:T(8,128)(2,1)}, bf16[8,88,3072]{2,1,0:T(8,128)(2,1)}, u32[]{:S(2)}, u32[]{:S(2)}) collective-permute-start(bf16[8,88,3072]{2,1,0:T(8,128)(2,1)} %shard_map.418.refs_2_.refs_0_), channel_id=1, source_target_pairs={{0,2},{2,0},{4,6},{6,4},{8,10},{10,8},{12,14},{14,12},{16,18},{18,... | collective-permute-start | bytes 12976136 | tf_op jit(solution)/shard_map/ppermute | solution.py:25
  520.7 96.1 %collective-permute-start.48 = (bf16[8,1,88,3072]{3,2,1,0:T(8,128)(2,1)}, bf16[8,1,88,3072]{3,2,1,0:T(8,128)(2,1)}, u32[]{:S(2)}, u32[]{:S(2)}) collective-permute-start(bf16[8,1,88,3072]{3,2,1,0:T(8,128)(2,1)} %get-tuple-element.140), channel_id=1, source_target_pairs={{0,2},{2,0},{4,6},{6,4},{8,10},{10,8},{12,14},{14,12},{16,18},{18,... | collective-permute-start | bytes 12976136 | tf_op jit(solution)/shard_map/ppermute | solution.py:25
  555.4 95.9 %collective-permute-start.51 = (bf16[8,1,88,3072]{3,2,1,0:T(8,128)(2,1)}, bf16[8,1,88,3072]{3,2,1,0:T(8,128)(2,1)}, u32[]{:S(2)}, u32[]{:S(2)}) collective-permute-start(bf16[8,1,88,3072]{3,2,1,0:T(8,128)(2,1)} %get-tuple-element.146), channel_id=1, source_target_pairs={{0,8},{2,10},{4,12},{6,14},{8,0},{10,2},{12,4},{14,6},{16,24},{18,... | collective-permute-start | bytes 12976136 | tf_op jit(solution)/shard_map/ppermute | solution.py:25
  622.8 58.1 %collective-permute-start.50 = (bf16[4,1,88,3072]{3,2,1,0:T(8,128)(2,1)}, bf16[4,1,88,3072]{3,2,1,0:T(8,128)(2,1)}, u32[]{:S(2)}, u32[]{:S(2)}) collective-permute-start(bf16[4,1,88,3072]{3,2,1,0:T(8,128)(2,1)} %get-tuple-element.144), channel_id=1, source_target_pairs={{0,4},{2,6},{4,0},{6,2},{8,12},{10,14},{12,8},{14,10},{16,20},{18,... | collective-permute-start | bytes 6488072 | tf_op jit(solution)/shard_map/ppermute | solution.py:25
  640.4 182.1 %collective-permute-start.43 = (bf16[512,1408]{1,0:T(8,128)(2,1)}, bf16[512,1408]{1,0:T(8,128)(2,1)}, u32[]{:S(2)}, u32[]{:S(2)}) collective-permute-start(bf16[512,1408]{1,0:T(8,128)(2,1)} %fusion.20), channel_id=1, source_target_pairs={{0,1},{1,0},{2,3},{3,2},{4,5},{5,4},{6,7},{7,6},{8,9},{9,8},{10,11... | collective-permute-start | bytes 4325384 | tf_op jit(solution)/shard_map/ppermute | solution.py:29
  657.3 78.2 %collective-permute-start.53 = (bf16[4,1,88,3072]{3,2,1,0:T(8,128)(2,1)}, bf16[4,1,88,3072]{3,2,1,0:T(8,128)(2,1)}, u32[]{:S(2)}, u32[]{:S(2)}) collective-permute-start(bf16[4,1,88,3072]{3,2,1,0:T(8,128)(2,1)} %get-tuple-element.152), channel_id=1, source_target_pairs={{0,2},{2,0},{4,6},{6,4},{8,10},{10,8},{12,14},{14,12},{16,18},{18,... | collective-permute-start | bytes 6488072 | tf_op jit(solution)/shard_map/ppermute | solution.py:25
  674.8 73.7 %collective-permute-start.55 = (bf16[8,1,88,1408]{3,2,1,0:T(8,128)(2,1)}, bf16[8,1,88,1408]{3,2,1,0:T(8,128)(2,1)}, u32[]{:S(2)}, u32[]{:S(2)}) collective-permute-start(bf16[8,1,88,1408]{3,2,1,0:T(8,128)(2,1)} %get-tuple-element.155), channel_id=1, source_target_pairs={{0,2},{2,0},{4,6},{6,4},{8,10},{10,8},{12,14},{14,12},{16,18},{18,... | collective-permute-start | bytes 5947400 | tf_op jit(solution)/shard_map/ppermute | solution.py:25
  675.4 81.0 %collective-permute-start.57 = (bf16[8,1,64,1408]{3,2,1,0:T(8,128)(2,1)}, bf16[8,1,64,1408]{3,2,1,0:T(8,128)(2,1)}, u32[]{:S(2)}, u32[]{:S(2)}) collective-permute-start(bf16[8,1,64,1408]{3,2,1,0:T(8,128)(2,1)} %get-tuple-element.159), channel_id=1, source_target_pairs={{0,4},{2,6},{4,0},{6,2},{8,12},{10,14},{12,8},{14,10},{16,20},{18,... | collective-permute-start | bytes 4325384 | tf_op jit(solution)/shard_map/ppermute | solution.py:25
  735.5 64.8 %collective-permute-start.52 = (bf16[512,1408]{1,0:T(8,128)(2,1)}, bf16[512,1408]{1,0:T(8,128)(2,1)}, u32[]{:S(2)}, u32[]{:S(2)}) collective-permute-start(bf16[512,1408]{1,0:T(8,128)(2,1)} %fusion.19), channel_id=1, source_target_pairs={{0,1},{1,0},{2,3},{3,2},{4,5},{5,4},{6,7},{7,6},{8,9},{9,8},{10,11... | collective-permute-start | bytes 4325384 | tf_op jit(solution)/shard_map/ppermute | solution.py:29
  748.5 49.3 %collective-permute-start.54 = (bf16[2,1,88,3072]{3,2,1,0:T(8,128)(2,1)}, bf16[2,1,88,3072]{3,2,1,0:T(8,128)(2,1)}, u32[]{:S(2)}, u32[]{:S(2)}) collective-permute-start(bf16[2,1,88,3072]{3,2,1,0:T(8,128)(2,1)} %get-tuple-element.154), channel_id=1, source_target_pairs={{0,4},{2,6},{4,0},{6,2},{8,12},{10,14},{12,8},{14,10},{16,20},{18,... | collective-permute-start | bytes 3244040 | tf_op jit(solution)/shard_map/ppermute | solution.py:25
  841.0 60.2 %collective-permute-start.64 = (bf16[8,1,88,1408]{3,2,1,0:T(8,128)(2,1)}, bf16[8,1,88,1408]{3,2,1,0:T(8,128)(2,1)S(1)}, u32[]{:S(2)}, u32[]{:S(2)}) collective-permute-start(bf16[8,1,88,1408]{3,2,1,0:T(8,128)(2,1)} %get-tuple-element.179), channel_id=1, source_target_pairs={{0,4},{2,6},{4,0},{6,2},{8,12},{10,14},{12,8},{14,10},{16,20},{18,... | collective-permute-start | bytes 5947400 | tf_op jit(solution)/shard_map/ppermute | solution.py:25
  842.5 55.4 %collective-permute-start.65 = (bf16[8,1,88,1408]{3,2,1,0:T(8,128)(2,1)}, bf16[8,1,88,1408]{3,2,1,0:T(8,128)(2,1)}, u32[]{:S(2)}, u32[]{:S(2)}) collective-permute-start(bf16[8,1,88,1408]{3,2,1,0:T(8,128)(2,1)} %get-tuple-element.180), channel_id=1, source_target_pairs={{0,2},{2,0},{4,6},{6,4},{8,10},{10,8},{12,14},{14,12},{16,18},{18,... | collective-permute-start | bytes 5947400 | tf_op jit(solution)/shard_map/ppermute | solution.py:25
  845.1 60.8 %collective-permute-start.84 = (bf16[1,1,88,3072]{3,2,1,0:T(8,128)(2,1)}, bf16[1,1,88,3072]{3,2,1,0:T(8,128)(2,1)}, u32[]{:S(2)}, u32[]{:S(2)}) collective-permute-start(bf16[1,1,88,3072]{3,2,1,0:T(8,128)(2,1)} %get-tuple-element.215), channel_id=1, source_target_pairs={{0,16},{2,18},{4,20},{6,22},{8,24},{10,26},{12,28},{14,30},{16,0},... | collective-permute-start | bytes 1622024 | tf_op jit(solution)/shard_map/ppermute | solution.py:25
  854.1 57.9 %collective-permute-start.63 = (bf16[8,1,88,704]{3,2,1,0:T(8,128)(2,1)}, bf16[8,1,88,704]{3,2,1,0:T(8,128)(2,1)}, u32[]{:S(2)}, u32[]{:S(2)}) collective-permute-start(bf16[8,1,88,704]{3,2,1,0:T(8,128)(2,1)} %get-tuple-element.177), channel_id=1, source_target_pairs={{0,2},{2,0},{4,6},{6,4},{8,10},{10,8},{12,14},{14,12},{16,18},{18,... | collective-permute-start | bytes 2973704 | tf_op jit(solution)/shard_map/ppermute | solution.py:25
  (154 other events, 2299.1 us)

commit v4 on v3

--- a/solution.py
+++ b/solution.py
@@ -878,7 +878,7 @@
     return jnp.where(row < valid, scores, -1e30)
 
 
-CHUNK = 256
+CHUNK = 512
 
 
 def attend_kernel(valid, turned, waits, q_ref, k_ref, v_ref, gain_ref, bias_ref, tab_ref, *refs):

time: 1050 us -> 1040 us (level)
  Pallas kernels: 428 us -> 415 us
  transfers between devices with their start and end apart: 88 -> 88, of which waited for: 30 -> 30; matrix products, arithmetic and copies ran while one was open for 21% -> 21% of each run, Pallas kernels for 37% -> 36%
where the time goes in v4:
time: 1040 us; the launch traced here: 1030 us
  Pallas kernels  415 us (40%)
  waiting for transfers between devices  274 us (26%)
  matrix products  129 us (12%)
  starting transfers between devices  80.8 us (8%)
  local copies, waits for them, and re-layouts  65 us (6%)
  other arithmetic  63.2 us (6%)
    ppermute x68, waiting for transfers between devices, hop(): return lax.ppermute(values, 'fsdp', [(i, i ^ mask) for i in range(count)])  269 us
    pallas_call x5, Pallas kernels, products(): pl.pallas_call(kernel, grid_spec=pltpu.PrefetchScalarGridSpec(num_scalar_...  83.6 us
    ppermute x68, starting transfers between devices, hop(): return lax.ppermute(values, 'fsdp', [(i, i ^ mask) for i in range(count)])  77.6 us
    dot_general x16, matrix products, turned_dot(): lax.dot_general(first_operand, second_operand, (((0,), (1,)), ((), ())),...  70.1 us
    pallas_call x2, Pallas kernels, attend_back(): pl.pallas_call(functools.partial(attend_back_kernel, valid, turned, joint...  55.6 us
    pallas_call x16, Pallas kernels, add_near(): pl.pallas_call(kernel, grid=(quarter // group, columns // tile), in_specs...  52.8 us
    dot_general x4, matrix products, dot_last(): lax.dot_general(first_operand, second_operand, (((1,), (1,)), ((), ())),...  38.7 us
    pallas_call x8, Pallas kernels, assemble(): pl.pallas_call(kernel, grid_spec=pltpu.PrefetchScalarGridSpec(num_scalar_...  37.9 us
  transfers between devices with their start and end apart: 88, of which 30 were waited for; matrix products, arithmetic and copies ran while one was open for 21% of the time, Pallas kernels for 36%

profile of v4, /device:TPU:0, one launch (start us, length us, event | category | flops | bytes accessed | tf_op | source)
XLA Modules:
  0.0 1029.2 jit_solution(12957901717242247829)
XLA Ops:
  85.3 19.3 %collective-permute-done.22 = f32[8,1408]{1,0:T(8,128)S(1)} collective-permute-done((f32[8,1408]{1,0:T(8,128)S(1)}, f32[8,1408]{1,0:T(8,128)S(1)}, u32[]{:S(2)}, u32[]{:S(2)}) %collective-permute-start.22) | collective-permute-done | bytes 45088 | tf_op jit(solution)/shard_map/ppermute | solution.py:25
  172.0 20.0 %collective-permute-done.20.refs_1_ = bf16[2,88,2432]{2,1,0:T(8,128)(2,1)} collective-permute-done((bf16[2,88,2432]{2,1,0:T(8,128)(2,1)}, bf16[2,88,2432]{2,1,0:T(8,128)(2,1)}, u32[]{:S(2)}, u32[]{:S(2)}) %collective-permute-start.20) | collective-permute-done | bytes 856096 | tf_op jit(solution)/shard_map/ppermute | solution.py:25
  241.0 21.9 %shard_map.412 = (bf16[8,88,1024]{2,1,0:T(8,128)(2,1)}, f32[8,1,1024]{2,1,0:T(1,128)}) custom-call(f32[2,8,88,1024]{3,2,1,0:T(8,128)} %bitcast.142, f32[2,8,88,1024]{3,2,1,0:T(8,128)} %bitcast.143, f32[1,8,88,1024]{3,2,1,0:T(8,128)} %bitcast.177, f32[2,88,1]{2,1,0:T(8,128)} %copy.85.gain_ref, f32[2,88,1]{2,1,0:T(8,128)} %copy.86.bias_ref, ...), custom_call_target="tpu_custom_call" | custom-call | flops 1 | bytes 1 | tf_op jit(solution)/shard_map/pallas_call | solution.py:915
  308.7 12.3 %shard_map.416 = (bf16[8,88,1024]{2,1,0:T(8,128)(2,1)}, f32[8,1,1024]{2,1,0:T(1,128)}) custom-call(f32[1,8,88,1024]{3,2,1,0:T(8,128)} %bitcast.179, f32[2,8,88,384]{3,2,1,0:T(8,128)} %bitcast.156, f32[2,8,88,384]{3,2,1,0:T(8,128)} %bitcast.157, f32[2,88,1]{2,1,0:T(8,128)} %copy.89.gain_ref, f32[2,88,1]{2,1,0:T(8,128)} %copy.90.bias_ref, ...), custom_call_target="tpu_custom_call" | custom-call | flops 1 | bytes 1 | tf_op jit(solution)/shard_map/pallas_call | solution.py:915
  324.3 14.0 %collective-permute-done.39.second_ref = bf16[4,88,3072]{2,1,0:T(8,128)(2,1)} collective-permute-done((bf16[4,88,3072]{2,1,0:T(8,128)(2,1)}, bf16[4,88,3072]{2,1,0:T(8,128)(2,1)}, u32[]{:S(2)}, u32[]{:S(2)}) %collective-permute-start.39) | collective-permute-done | bytes 2162720 | tf_op jit(solution)/shard_map/ppermute | solution.py:25
  365.5 71.8 %collective-permute-done.40.refs_1_ = bf16[8,88,3072]{2,1,0:T(8,128)(2,1)} collective-permute-done((bf16[8,88,3072]{2,1,0:T(8,128)(2,1)}, bf16[8,88,3072]{2,1,0:T(8,128)(2,1)}, u32[]{:S(2)}, u32[]{:S(2)}) %collective-permute-start.40) | collective-permute-done | bytes 4325408 | tf_op jit(solution)/shard_map/ppermute | solution.py:25
  444.5 20.5 %shard_map.420 = (bf16[1024,3072]{1,0:T(8,128)(2,1)}, bf16[1024,3072]{1,0:T(8,128)(2,1)}) custom-call(bf16[1024,1408]{1,0:T(8,128)(2,1)} %pad_maximum_fusion.3.rows_ref.refs_0_, bf16[1408,3072]{1,0:T(8,128)(2,1)} %bitcast.149, f32[1,3072]{1,0:T(1,128)} %reshape_reshape.4.bias_ref, bf16[16,88,3072]{2,1,0:T(8,128)(2,1)} %shard_map.419.refs_0_), custom_call_target="tpu_custom_call" | custom-call | flops 1 | bytes 1 | tf_op jit(solution)/shard_map/pallas_call | solution.py:777
  472.2 15.3 %shard_map.422 = (bf16[1024,3072]{1,0:T(8,128)(2,1)}, f32[8,3072]{1,0:T(8,128)}) custom-call(bf16[1024,1408]{1,0:T(8,128)(2,1)} %copy-done.9, bf16[1408,3072]{1,0:T(8,128)(2,1)} %bitcast.146, bf16[1024,3072]{1,0:T(8,128)(2,1)} %get-tuple-element.132.slope_ref, bf16[16,88,3072]{2,1,0:T(8,128)(2,1)} %shard_map.421.refs_0_), custom_call_target="tpu_custom_call" | custom-call | flops 1 | bytes 1 | tf_op jit(solution)/shard_map/pallas_call | solution.py:817
  487.4 10.3 %fusion.23 = bf16[512,1408]{1,0:T(8,128)(2,1)} fusion(bf16[1408,3072]{1,0:T(8,128)(2,1)} %bitcast.150, bf16[1024,3072]{1,0:T(8,128)(2,1)} %get-tuple-element.133.refs_1_.refs_2_), kind=kOutput, calls=%fused_computation.37 | convolution fusion | flops 4429905920 | bytes 13238272 | tf_op jit(solution)/shard_map/dot_general | solution.py:635
  497.8 17.1 %shard_map.423 = (bf16[8,1,88,3072]{3,2,1,0:T(8,128)(2,1)}, bf16[8,1,88,3072]{3,2,1,0:T(8,128)(2,1)}) custom-call(s32[3]{0:T(128)} %pad_add_fusion.me_ref, bf16[1024,1408]{1,0:T(8,128)(2,1)} %pad_maximum_fusion.3.rows_ref.refs_0_, bf16[1024,3072]{1,0:T(8,128)(2,1)} %get-tuple-element.133.refs_1_.refs_2_, bf16[1024,3072]{1,0:T(8,128)(2,1)} %get-tuple-element.133.refs_1_.refs_2_), custom_call_target="tpu_custom_call" | custom-call | flops 1 | bytes 1 | tf_op jit(solution)/shard_map/pallas_call | solution.py:445
  524.4 16.7 %shard_map.424 = (bf16[8,1,88,3072]{3,2,1,0:T(8,128)(2,1)}, bf16[8,1,88,3072]{3,2,1,0:T(8,128)(2,1)}) custom-call(s32[3]{0:T(128)} %pad_add_fusion.me_ref, bf16[1024,1408]{1,0:T(8,128)(2,1)} %copy-done.9, bf16[1024,3072]{1,0:T(8,128)(2,1)} %get-tuple-element.131.refs_2_.refs_1_, bf16[8,1,88,3072]{3,2,1,0:T(8,128)(2,1)} %get-tuple-element.134.refs_2_.kept_low.kept_high), custom_call_target="tpu_custom_call" | custom-call | flops 1 | bytes 1 | tf_op jit(solution)/shard_map/pallas_call | solution.py:445
  557.9 18.7 %shard_map.426 = (bf16[1,8,88,1024]{3,2,1,0:T(8,128)(2,1)}, bf16[2,8,88,384]{3,2,1,0:T(8,128)(2,1)}, f32[4,88,128]{2,1,0:T(8,128)}, f32[1,3,8,88,128]{4,3,2,1,0:T(8,128)}) custom-call(f32[1,8,88,1024]{3,2,1,0:T(8,128)} %bitcast.180, f32[2,8,88,384]{3,2,1,0:T(8,128)} %bitcast.158, f32[2,8,88,384]{3,2,1,0:T(8,128)} %bitcast.159, ...), custom_call_target="tpu_custom_call" | custom-call | flops 1 | bytes 1 | tf_op jit(solution)/shard_map/pallas_call | solution.py:1009
  597.9 13.2 %collective-permute-done.48.got_low.got_high = bf16[8,1,88,3072]{3,2,1,0:T(8,128)(2,1)} collective-permute-done((bf16[8,1,88,3072]{3,2,1,0:T(8,128)(2,1)}, bf16[8,1,88,3072]{3,2,1,0:T(8,128)(2,1)}, u32[]{:S(2)}, u32[]{:S(2)}) %collective-permute-start.48) | collective-permute-done | bytes 4325408 | tf_op jit(solution)/shard_map/ppermute | solution.py:25
  635.2 10.6 %collective-permute-done.51.got_low.got_high = bf16[8,1,88,3072]{3,2,1,0:T(8,128)(2,1)} collective-permute-done((bf16[8,1,88,3072]{3,2,1,0:T(8,128)(2,1)}, bf16[8,1,88,3072]{3,2,1,0:T(8,128)(2,1)}, u32[]{:S(2)}, u32[]{:S(2)}) %collective-permute-start.51) | collective-permute-done | bytes 4325408 | tf_op jit(solution)/shard_map/ppermute | solution.py:25
  653.3 15.8 %shard_map.430 = (bf16[8,1,88,1408]{3,2,1,0:T(8,128)(2,1)}, bf16[8,1,88,1408]{3,2,1,0:T(8,128)(2,1)}, bf16[8,1,64,1408]{3,2,1,0:T(8,128)(2,1)}, bf16[8,1,64,1408]{3,2,1,0:T(8,128)(2,1)}) custom-call(s32[3]{0:T(128)} %pad_add_fusion.me_ref, bf16[1024,1408]{1,0:T(8,128)(2,1)} %copy-done.22, bf16[1024,1408]{1,0:T(8,128)(2,1)} %pad_maximum_fusion.2.refs_1_, ...), custom_call_target="tpu_custom_call" | custom-call | flops 1 | bytes 1 | tf_op jit(solution)/shard_map/pallas_call | solution.py:445
  679.5 37.0 %shard_map.432 = (bf16[3,8,88,1024]{3,2,1,0:T(8,128)(2,1)}, f32[4,88,128]{2,1,0:T(8,128)}, f32[1,3,8,88,128]{4,3,2,1,0:T(8,128)}) custom-call(f32[2,8,88,1024]{3,2,1,0:T(8,128)} %bitcast.144, f32[2,8,88,1024]{3,2,1,0:T(8,128)} %bitcast.145, f32[1,8,88,1024]{3,2,1,0:T(8,128)} %bitcast.178, bf16[8,88,1024]{2,1,0:T(8,128)(2,1)} %bitcast.200, ...), custom_call_target="tpu_custom_call" | custom-call | flops 1 | bytes 1 | tf_op jit(solution)/shard_map/pallas_call | solution.py:1009
  731.9 11.1 %collective-permute-done.55.got_low.got_high = bf16[8,1,88,1408]{3,2,1,0:T(8,128)(2,1)} collective-permute-done((bf16[8,1,88,1408]{3,2,1,0:T(8,128)(2,1)}, bf16[8,1,88,1408]{3,2,1,0:T(8,128)(2,1)}, u32[]{:S(2)}, u32[]{:S(2)}) %collective-permute-start.55) | collective-permute-done | bytes 1982496 | tf_op jit(solution)/shard_map/ppermute | solution.py:25
  765.5 19.2 %shard_map.437 = (bf16[8,1,88,1408]{3,2,1,0:T(8,128)(2,1)}, bf16[8,1,88,1408]{3,2,1,0:T(8,128)(2,1)}, bf16[8,1,88,1408]{3,2,1,0:T(8,128)(2,1)}, bf16[8,1,88,1408]{3,2,1,0:T(8,128)(2,1)}) custom-call(s32[3]{0:T(128)} %pad_add_fusion.me_ref, bf16[1024,1408]{1,0:T(8,128)(2,1)} %pad_maximum_fusion.1.refs_0_, bf16[1024,1408]{1,0:T(8,128)(2,1)} %copy-done.21, ...), custom_call_target="tpu_custom_call" | custom-call | flops 1 | bytes 1 | tf_op jit(solution)/shard_map/pallas_call | solution.py:445
  801.9 14.8 %shard_map.441 = (bf16[2,16,1,88,704]{4,3,2,1,0:T(8,128)(2,1)}, bf16[2,16,1,88,704]{4,3,2,1,0:T(8,128)(2,1)}) custom-call(s32[3]{0:T(128)} %pad_add_fusion.me_ref, bf16[512,2816]{1,0:T(8,128)(2,1)} %fusion.5.refs_0_, bf16[512,1408]{1,0:T(8,128)(2,1)} %get-tuple-element.167.refs_1_.low_ref, f32[512,1408]{1,0:T(8,128)} %get-tuple-element.169.refs_2_), custom_call_target="tpu_custom_call" | custom-call | flops 1 | bytes 1 | tf_op jit(solution)/shard_map/pallas_call | solution.py:445
  816.8 10.6 %fusion.26 = bf16[512,1408]{1,0:T(8,128)(2,1)} fusion(f32[512,1408]{1,0:T(8,128)S(1)} %copy-done.4, bf16[1408,3072]{1,0:T(8,128)(2,1)} %bitcast.148, bf16[1024,3072]{1,0:T(8,128)(2,1)} %get-tuple-element.131.refs_2_.refs_1_, bf16[512,1408]{1,0:T(8,128)(2,1)} %collective-permute-done.43, f32[1408]{0:T(1024)S(1)} %add.376), kind=kOutput, calls=%fused_computation.38 | convolution fusion | flops 4432789504 | bytes 17569280 | tf_op jit(solution)/shard_map/dot_general | solution.py:635
  849.8 24.0 %collective-permute-done.60.got_ref = bf16[2,2,1,88,1408]{4,3,2,1,0:T(8,128)(2,1)S(1)} collective-permute-done((bf16[2,2,1,88,1408]{4,3,2,1,0:T(8,128)(2,1)}, bf16[2,2,1,88,1408]{4,3,2,1,0:T(8,128)(2,1)S(1)}, u32[]{:S(2)}, u32[]{:S(2)}) %collective-permute-start.60) | collective-permute-done | bytes 991264 | tf_op jit(solution)/shard_map/ppermute | solution.py:25
  878.5 13.6 %shard_map.445 = (f32[512,1408]{1,0:T(8,128)}, f32[512,1408]{1,0:T(8,128)}, f32[2,8,2816]{2,1,0:T(8,128)}) custom-call(bf16[512,1408]{1,0:T(8,128)(2,1)} %get-tuple-element.167.refs_1_.low_ref, bf16[2816,1408]{1,0:T(8,128)(2,1)} %bitcast.154, bf16[512,1408]{1,0:T(8,128)(2,1)} %first_ref.1, bf16[512,1408]{1,0:T(8,128)(2,1)} %second_ref.1, ...), custom_call_target="tpu_custom_call" | custom-call | flops 1 | bytes 1 | tf_op jit(solution)/shard_map/pallas_call | solution.py:735
  953.6 13.5 %collective-permute-done.74.got_ref = bf16[2,2,1,88,1408]{4,3,2,1,0:T(8,128)(2,1)S(1)} collective-permute-done((bf16[2,2,1,88,1408]{4,3,2,1,0:T(8,128)(2,1)}, bf16[2,2,1,88,1408]{4,3,2,1,0:T(8,128)(2,1)S(1)}, u32[]{:S(2)}, u32[]{:S(2)}) %collective-permute-start.74) | collective-permute-done | bytes 991264 | tf_op jit(solution)/shard_map/ppermute | solution.py:25
  1004.0 11.9 %collective-permute-done.78 = bf16[2,1,1,88,704]{4,3,2,1,0:T(8,128)(2,1)S(1)} collective-permute-done((bf16[2,1,1,88,704]{4,3,2,1,0:T(8,128)(2,1)S(1)}, bf16[2,1,1,88,704]{4,3,2,1,0:T(8,128)(2,1)S(1)}, u32[]{:S(2)}, u32[]{:S(2)}) %collective-permute-start.78) | collective-permute-done | bytes 247840 | tf_op jit(solution)/shard_map/ppermute | solution.py:25
  (663 shorter events, 573.1 us)
Async XLA Ops:
  20.6 46.7 %collective-permute-start.9 = (bf16[1,88,2816]{2,1,0:T(8,128)(2,1)S(1)}, bf16[1,88,2816]{2,1,0:T(8,128)(2,1)}, u32[]{:S(2)}, u32[]{:S(2)}) collective-permute-start(bf16[1,88,2816]{2,1,0:T(8,128)(2,1)S(1)} %maximum_bitcast_fusion.first_ref), channel_id=1, source_target_pairs={{0,16},{2,18},{4,20},{6,22},{8,24},{10,26},{12,28},{14,30},{16,0},... | collective-permute-start | bytes 1486856 | tf_op jit(solution)/shard_map/ppermute | solution.py:25
  147.2 53.3 %collective-permute-start.17 = (bf16[8,88,1408]{2,1,0:T(8,128)(2,1)}, bf16[8,88,1408]{2,1,0:T(8,128)(2,1)}, u32[]{:S(2)}, u32[]{:S(2)}) collective-permute-start(bf16[8,88,1408]{2,1,0:T(8,128)(2,1)} %shard_map.402.refs_0_), channel_id=1, source_target_pairs={{0,4},{2,6},{4,0},{6,2},{8,12},{10,14},{12,8},{14,10},{16,20},{18,... | collective-permute-start | bytes 5947400 | tf_op jit(solution)/shard_map/ppermute | solution.py:25
  151.3 54.1 %collective-permute-start.28 = (bf16[8,88,1408]{2,1,0:T(8,128)(2,1)}, bf16[8,88,1408]{2,1,0:T(8,128)(2,1)}, u32[]{:S(2)}, u32[]{:S(2)}) collective-permute-start(bf16[8,88,1408]{2,1,0:T(8,128)(2,1)} %shard_map.403.refs_0_), channel_id=1, source_target_pairs={{0,2},{2,0},{4,6},{6,4},{8,10},{10,8},{12,14},{14,12},{16,18},{18,... | collective-permute-start | bytes 5947400 | tf_op jit(solution)/shard_map/ppermute | solution.py:25
  159.2 50.5 %collective-permute-start.31 = (bf16[1,88,6144]{2,1,0:T(8,128)(2,1)}, bf16[1,88,6144]{2,1,0:T(8,128)(2,1)}, u32[]{:S(2)}, u32[]{:S(2)}) collective-permute-start(bf16[1,88,6144]{2,1,0:T(8,128)(2,1)} %bitcast.181), channel_id=1, source_target_pairs={{0,16},{2,18},{4,20},{6,22},{8,24},{10,26},{12,28},{14,30},{16,0},... | collective-permute-start | bytes 3244040 | tf_op jit(solution)/shard_map/ppermute | solution.py:25
  172.0 53.5 %collective-permute-start.27 = (bf16[512,1408]{1,0:T(8,128)(2,1)}, bf16[512,1408]{1,0:T(8,128)(2,1)}, u32[]{:S(2)}, u32[]{:S(2)}) collective-permute-start(bf16[512,1408]{1,0:T(8,128)(2,1)} %add_convert_fusion.2), channel_id=1, source_target_pairs={{0,1},{1,0},{2,3},{3,2},{4,5},{5,4},{6,7},{7,6},{8,9},{9,8},{10,11... | collective-permute-start | bytes 4325384 | tf_op jit(solution)/shard_map/ppermute | solution.py:29
  212.4 54.3 %collective-permute-start.33 = (bf16[2,88,6144]{2,1,0:T(8,128)(2,1)}, bf16[2,88,6144]{2,1,0:T(8,128)(2,1)}, u32[]{:S(2)}, u32[]{:S(2)}) collective-permute-start(bf16[2,88,6144]{2,1,0:T(8,128)(2,1)} %shard_map.409.refs_0_), channel_id=1, source_target_pairs={{0,8},{2,10},{4,12},{6,14},{8,0},{10,2},{12,4},{14,6},{16,24},{18,... | collective-permute-start | bytes 6488072 | tf_op jit(solution)/shard_map/ppermute | solution.py:25
  219.5 50.7 %collective-permute-start.32 = (bf16[8,88,1408]{2,1,0:T(8,128)(2,1)}, bf16[8,88,1408]{2,1,0:T(8,128)(2,1)}, u32[]{:S(2)}, u32[]{:S(2)}) collective-permute-start(bf16[8,88,1408]{2,1,0:T(8,128)(2,1)} %shard_map.410.refs_0_), channel_id=1, source_target_pairs={{0,4},{2,6},{4,0},{6,2},{8,12},{10,14},{12,8},{14,10},{16,20},{18,... | collective-permute-start | bytes 5947400 | tf_op jit(solution)/shard_map/ppermute | solution.py:25
  288.7 49.6 %collective-permute-start.39 = (bf16[4,88,3072]{2,1,0:T(8,128)(2,1)}, bf16[4,88,3072]{2,1,0:T(8,128)(2,1)}, u32[]{:S(2)}, u32[]{:S(2)}) collective-permute-start(bf16[4,88,3072]{2,1,0:T(8,128)(2,1)} %get-tuple-element.128.refs_2_.first_ref), channel_id=1, source_target_pairs={{0,2},{2,0},{4,6},{6,4},{8,10},{10,8},{12,14},{14,12},{16,18},{18,... | collective-permute-start | bytes 6488072 | tf_op jit(solution)/shard_map/ppermute | solution.py:25
  289.2 54.4 %collective-permute-start.41 = (bf16[4,88,3072]{2,1,0:T(8,128)(2,1)}, bf16[4,88,3072]{2,1,0:T(8,128)(2,1)}, u32[]{:S(2)}, u32[]{:S(2)}) collective-permute-start(bf16[4,88,3072]{2,1,0:T(8,128)(2,1)} %get-tuple-element.130.first_ref), channel_id=1, source_target_pairs={{0,4},{2,6},{4,0},{6,2},{8,12},{10,14},{12,8},{14,10},{16,20},{18,... | collective-permute-start | bytes 6488072 | tf_op jit(solution)/shard_map/ppermute | solution.py:25
  342.1 95.2 %collective-permute-start.40 = (bf16[8,88,3072]{2,1,0:T(8,128)(2,1)}, bf16[8,88,3072]{2,1,0:T(8,128)(2,1)}, u32[]{:S(2)}, u32[]{:S(2)}) collective-permute-start(bf16[8,88,3072]{2,1,0:T(8,128)(2,1)} %shard_map.417.refs_0_), channel_id=1, source_target_pairs={{0,4},{2,6},{4,0},{6,2},{8,12},{10,14},{12,8},{14,10},{16,20},{18,... | collective-permute-start | bytes 12976136 | tf_op jit(solution)/shard_map/ppermute | solution.py:25
  347.4 117.6 %collective-permute-start.42 = (bf16[8,88,3072]{2,1,0:T(8,128)(2,1)}, bf16[8,88,3072]{2,1,0:T(8,128)(2,1)}, u32[]{:S(2)}, u32[]{:S(2)}) collective-permute-start(bf16[8,88,3072]{2,1,0:T(8,128)(2,1)} %shard_map.418.refs_2_.refs_0_), channel_id=1, source_target_pairs={{0,2},{2,0},{4,6},{6,4},{8,10},{10,8},{12,14},{14,12},{16,18},{18,... | collective-permute-start | bytes 12976136 | tf_op jit(solution)/shard_map/ppermute | solution.py:25
  514.9 96.1 %collective-permute-start.48 = (bf16[8,1,88,3072]{3,2,1,0:T(8,128)(2,1)}, bf16[8,1,88,3072]{3,2,1,0:T(8,128)(2,1)}, u32[]{:S(2)}, u32[]{:S(2)}) collective-permute-start(bf16[8,1,88,3072]{3,2,1,0:T(8,128)(2,1)} %get-tuple-element.140), channel_id=1, source_target_pairs={{0,2},{2,0},{4,6},{6,4},{8,10},{10,8},{12,14},{14,12},{16,18},{18,... | collective-permute-start | bytes 12976136 | tf_op jit(solution)/shard_map/ppermute | solution.py:25
  549.9 95.9 %collective-permute-start.51 = (bf16[8,1,88,3072]{3,2,1,0:T(8,128)(2,1)}, bf16[8,1,88,3072]{3,2,1,0:T(8,128)(2,1)}, u32[]{:S(2)}, u32[]{:S(2)}) collective-permute-start(bf16[8,1,88,3072]{3,2,1,0:T(8,128)(2,1)} %get-tuple-element.146), channel_id=1, source_target_pairs={{0,8},{2,10},{4,12},{6,14},{8,0},{10,2},{12,4},{14,6},{16,24},{18,... | collective-permute-start | bytes 12976136 | tf_op jit(solution)/shard_map/ppermute | solution.py:25
  617.0 58.1 %collective-permute-start.50 = (bf16[4,1,88,3072]{3,2,1,0:T(8,128)(2,1)}, bf16[4,1,88,3072]{3,2,1,0:T(8,128)(2,1)}, u32[]{:S(2)}, u32[]{:S(2)}) collective-permute-start(bf16[4,1,88,3072]{3,2,1,0:T(8,128)(2,1)} %get-tuple-element.144), channel_id=1, source_target_pairs={{0,4},{2,6},{4,0},{6,2},{8,12},{10,14},{12,8},{14,10},{16,20},{18,... | collective-permute-start | bytes 6488072 | tf_op jit(solution)/shard_map/ppermute | solution.py:25
  634.6 182.1 %collective-permute-start.43 = (bf16[512,1408]{1,0:T(8,128)(2,1)}, bf16[512,1408]{1,0:T(8,128)(2,1)}, u32[]{:S(2)}, u32[]{:S(2)}) collective-permute-start(bf16[512,1408]{1,0:T(8,128)(2,1)} %fusion.20), channel_id=1, source_target_pairs={{0,1},{1,0},{2,3},{3,2},{4,5},{5,4},{6,7},{7,6},{8,9},{9,8},{10,11... | collective-permute-start | bytes 4325384 | tf_op jit(solution)/shard_map/ppermute | solution.py:29
  651.8 75.8 %collective-permute-start.53 = (bf16[4,1,88,3072]{3,2,1,0:T(8,128)(2,1)}, bf16[4,1,88,3072]{3,2,1,0:T(8,128)(2,1)}, u32[]{:S(2)}, u32[]{:S(2)}) collective-permute-start(bf16[4,1,88,3072]{3,2,1,0:T(8,128)(2,1)} %get-tuple-element.152), channel_id=1, source_target_pairs={{0,2},{2,0},{4,6},{6,4},{8,10},{10,8},{12,14},{14,12},{16,18},{18,... | collective-permute-start | bytes 6488072 | tf_op jit(solution)/shard_map/ppermute | solution.py:25
  669.1 73.9 %collective-permute-start.55 = (bf16[8,1,88,1408]{3,2,1,0:T(8,128)(2,1)}, bf16[8,1,88,1408]{3,2,1,0:T(8,128)(2,1)}, u32[]{:S(2)}, u32[]{:S(2)}) collective-permute-start(bf16[8,1,88,1408]{3,2,1,0:T(8,128)(2,1)} %get-tuple-element.155), channel_id=1, source_target_pairs={{0,2},{2,0},{4,6},{6,4},{8,10},{10,8},{12,14},{14,12},{16,18},{18,... | collective-permute-start | bytes 5947400 | tf_op jit(solution)/shard_map/ppermute | solution.py:25
  669.7 81.2 %collective-permute-start.57 = (bf16[8,1,64,1408]{3,2,1,0:T(8,128)(2,1)}, bf16[8,1,64,1408]{3,2,1,0:T(8,128)(2,1)}, u32[]{:S(2)}, u32[]{:S(2)}) collective-permute-start(bf16[8,1,64,1408]{3,2,1,0:T(8,128)(2,1)} %get-tuple-element.159), channel_id=1, source_target_pairs={{0,4},{2,6},{4,0},{6,2},{8,12},{10,14},{12,8},{14,10},{16,20},{18,... | collective-permute-start | bytes 4325384 | tf_op jit(solution)/shard_map/ppermute | solution.py:25
  727.5 67.2 %collective-permute-start.52 = (bf16[512,1408]{1,0:T(8,128)(2,1)}, bf16[512,1408]{1,0:T(8,128)(2,1)}, u32[]{:S(2)}, u32[]{:S(2)}) collective-permute-start(bf16[512,1408]{1,0:T(8,128)(2,1)} %fusion.19), channel_id=1, source_target_pairs={{0,1},{1,0},{2,3},{3,2},{4,5},{5,4},{6,7},{7,6},{8,9},{9,8},{10,11... | collective-permute-start | bytes 4325384 | tf_op jit(solution)/shard_map/ppermute | solution.py:29
  743.0 49.3 %collective-permute-start.54 = (bf16[2,1,88,3072]{3,2,1,0:T(8,128)(2,1)}, bf16[2,1,88,3072]{3,2,1,0:T(8,128)(2,1)}, u32[]{:S(2)}, u32[]{:S(2)}) collective-permute-start(bf16[2,1,88,3072]{3,2,1,0:T(8,128)(2,1)} %get-tuple-element.154), channel_id=1, source_target_pairs={{0,4},{2,6},{4,0},{6,2},{8,12},{10,14},{12,8},{14,10},{16,20},{18,... | collective-permute-start | bytes 3244040 | tf_op jit(solution)/shard_map/ppermute | solution.py:25
  835.2 60.2 %collective-permute-start.64 = (bf16[8,1,88,1408]{3,2,1,0:T(8,128)(2,1)}, bf16[8,1,88,1408]{3,2,1,0:T(8,128)(2,1)S(1)}, u32[]{:S(2)}, u32[]{:S(2)}) collective-permute-start(bf16[8,1,88,1408]{3,2,1,0:T(8,128)(2,1)} %get-tuple-element.179), channel_id=1, source_target_pairs={{0,4},{2,6},{4,0},{6,2},{8,12},{10,14},{12,8},{14,10},{16,20},{18,... | collective-permute-start | bytes 5947400 | tf_op jit(solution)/shard_map/ppermute | solution.py:25
  836.7 55.4 %collective-permute-start.65 = (bf16[8,1,88,1408]{3,2,1,0:T(8,128)(2,1)}, bf16[8,1,88,1408]{3,2,1,0:T(8,128)(2,1)}, u32[]{:S(2)}, u32[]{:S(2)}) collective-permute-start(bf16[8,1,88,1408]{3,2,1,0:T(8,128)(2,1)} %get-tuple-element.180), channel_id=1, source_target_pairs={{0,2},{2,0},{4,6},{6,4},{8,10},{10,8},{12,14},{14,12},{16,18},{18,... | collective-permute-start | bytes 5947400 | tf_op jit(solution)/shard_map/ppermute | solution.py:25
  839.3 60.8 %collective-permute-start.84 = (bf16[1,1,88,3072]{3,2,1,0:T(8,128)(2,1)}, bf16[1,1,88,3072]{3,2,1,0:T(8,128)(2,1)}, u32[]{:S(2)}, u32[]{:S(2)}) collective-permute-start(bf16[1,1,88,3072]{3,2,1,0:T(8,128)(2,1)} %get-tuple-element.215), channel_id=1, source_target_pairs={{0,16},{2,18},{4,20},{6,22},{8,24},{10,26},{12,28},{14,30},{16,0},... | collective-permute-start | bytes 1622024 | tf_op jit(solution)/shard_map/ppermute | solution.py:25
  848.4 57.9 %collective-permute-start.63 = (bf16[8,1,88,704]{3,2,1,0:T(8,128)(2,1)}, bf16[8,1,88,704]{3,2,1,0:T(8,128)(2,1)}, u32[]{:S(2)}, u32[]{:S(2)}) collective-permute-start(bf16[8,1,88,704]{3,2,1,0:T(8,128)(2,1)} %get-tuple-element.177), channel_id=1, source_target_pairs={{0,2},{2,0},{4,6},{6,4},{8,10},{10,8},{12,14},{14,12},{16,18},{18,... | collective-permute-start | bytes 2973704 | tf_op jit(solution)/shard_map/ppermute | solution.py:25
  (154 other events, 2294.1 us)
